TPU v7x, 32 devices: a whole 2x2x4 slice. The times are simulated.
32 devices in a mesh: dp: 4 (over y, x), ctx: 8 (over z, core).
Axes of the slice: x: 2, y: 2, z: 4, core: 2. Of those that a mesh axis runs over, the one named last changes fastest.
Arguments:
- tokens_in: bfloat16 [4, 1024, 2048], P('dp', 'ctx'), may hold values from -6 to 6
- exit_layer: int32 [4, 1024], P('dp', 'ctx'), may hold values from 8 to 23
- layer_index: int32 [1], replicated, may hold values from 8 to 15
- segment_ids: int32 [4, 1024], P('dp', 'ctx'), may hold values from 0 to 4, as said below
- grad_out: bfloat16 [4, 1024, 2048], P('dp', 'ctx'), may hold values from -6 to 6
- first_gain: bfloat16 [2048], P(('dp', 'ctx')), may hold values from 0.099609375 to 1.8984375
- first_bias: bfloat16 [2048], P(('dp', 'ctx')), may hold values from -1.75 to 1.75
- query_weight: bfloat16 [2048, 2048], P(('dp', 'ctx')), may hold values from -0.125 to 0.125
- query_bias: bfloat16 [2048], P(('dp', 'ctx')), may hold values from -1.75 to 1.75
- key_weight: bfloat16 [2048, 2048], P(('dp', 'ctx')), may hold values from -0.125 to 0.125
- value_weight: bfloat16 [2048, 2048], P(('dp', 'ctx')), may hold values from -0.125 to 0.125
- value_bias: bfloat16 [2048], P(('dp', 'ctx')), may hold values from -0.625 to 0.625
- out_weight: bfloat16 [2048, 2048], P(('dp', 'ctx')), may hold values from -1 to 1
- out_bias: bfloat16 [2048], P(('dp', 'ctx')), may hold values from -1.75 to 1.75
- second_gain: bfloat16 [2048], P(('dp', 'ctx')), may hold values from 0.099609375 to 1.8984375
- second_bias: bfloat16 [2048], P(('dp', 'ctx')), may hold values from -1.75 to 1.75
- up_weight: bfloat16 [2048, 8192], P(('dp', 'ctx')), may hold values from -0.125 to 0.125
- up_bias: bfloat16 [8192], P(('dp', 'ctx')), may hold values from -3 to 3
- down_weight: bfloat16 [8192, 2048], P(('dp', 'ctx')), may hold values from -0.0625 to 0.0625
- down_bias: bfloat16 [2048], P(('dp', 'ctx')), may hold values from -1.75 to 1.75
Outputs:
- layer_out: bfloat16 [4, 1024, 2048], P('dp', 'ctx')
- grad_in: bfloat16 [4, 1024, 2048], P('dp', 'ctx')
- grad_first_gain: float32 [2048], P(('dp', 'ctx'))
- grad_first_bias: float32 [2048], P(('dp', 'ctx'))
- grad_query_weight: float32 [2048, 2048], P(('dp', 'ctx'))
- grad_query_bias: float32 [2048], P(('dp', 'ctx'))
- grad_key_weight: float32 [2048, 2048], P(('dp', 'ctx'))
- grad_value_weight: float32 [2048, 2048], P(('dp', 'ctx'))
- grad_value_bias: float32 [2048], P(('dp', 'ctx'))
- grad_out_weight: float32 [2048, 2048], P(('dp', 'ctx'))
- grad_out_bias: float32 [2048], P(('dp', 'ctx'))
- grad_second_gain: float32 [2048], P(('dp', 'ctx'))
- grad_second_bias: float32 [2048], P(('dp', 'ctx'))
- grad_up_weight: float32 [2048, 8192], P(('dp', 'ctx'))
- grad_up_bias: float32 [8192], P(('dp', 'ctx'))
- grad_down_weight: float32 [8192, 2048], P(('dp', 'ctx'))
- grad_down_bias: float32 [2048], P(('dp', 'ctx'))
Inputs may be any that keep to these rules, and one draw needn't show every extreme that they name: `segment_ids`: in each row the ids start at 0, never fall and rise by one at four places, so a row holds five segments; segment 2 begins within the row's first 128 positions and ends within its last 128; the other four are each shorter than 128.
All inputs are finite; a program needn't handle non-finite values.
Results may differ from a plain program's by a relative error of at most 0.015.
Values may be sent and summed in bfloat16 or wider, within the bound.
No kernel may reach another device: no remote copies, remote signals or barrier semaphores. Data moves between devices by JAX's collectives and lax.ppermute only.
A program may use at most 512 MiB of HBM per device.

v0:
```python
import jax
import jax.numpy as jnp
from jax import lax
from jax.sharding import PartitionSpec as P

HEADS = 32
HEAD_DIM = 64


EPSILON = 1e-05
NEG_FILL = -1e30


def normalize(values_in, gain_vec, bias_vec):
    average = jnp.mean(values_in, axis=-1, keepdims=True)
    centered = values_in - average
    variance = jnp.mean(centered * centered, axis=-1, keepdims=True)
    return centered * lax.rsqrt(variance + EPSILON) * gain_vec + bias_vec


def smooth(pre_act):
    return jax.nn.gelu(pre_act, approximate=True)


def over_blocks(state, piece, block_rows, block_step):
    rows_here = piece.shape[1]
    size_block = min(block_rows, rows_here)

    def inner(index, current):
        offset = index * size_block
        sub_piece = lax.dynamic_slice_in_dim(piece, offset, size_block, 1)
        return block_step(current, sub_piece, offset)

    return lax.fori_loop(0, rows_here // size_block, inner, state)


def local(
    tokens_in,
    exit_layer,
    layer_index,
    segment_ids,
    grad_out,
    first_gain,
    first_bias,
    query_weight,
    query_bias,
    key_weight,
    value_weight,
    value_bias,
    out_weight,
    out_bias,
    second_gain,
    second_bias,
    up_weight,
    up_bias,
    down_weight,
    down_bias,
):
    scale = HEAD_DIM ** (-0.5)
    width = HEADS * HEAD_DIM
    row_count = tokens_in.shape[0]
    local_rows = tokens_in.shape[1]
    model_width = tokens_in.shape[2]
    flat_rows = row_count * local_rows
    inputs = tokens_in.astype(jnp.float32).reshape(flat_rows, model_width)
    parts = lax.axis_size("ctx")
    my_index = lax.axis_index("ctx")
    query_pos = my_index * local_rows + jnp.arange(local_rows, dtype=jnp.int32)
    active = (exit_layer > layer_index[0]).astype(jnp.float32).reshape(flat_rows, 1)
    row_segs = lax.all_gather(segment_ids, "ctx", axis=1, tiled=True)

    def allowed_block(start, count):
        key_seg = lax.dynamic_slice_in_dim(row_segs, start, count, 1)
        key_pos = start + jnp.arange(count, dtype=jnp.int32)
        return (segment_ids[:, :, None] == key_seg[:, None, :]) & (
            key_pos[None, None, :] <= query_pos[None, :, None]
        )

    (
        gain_one,
        bias_one,
        weight_query,
        bias_query,
        weight_key,
        weight_value,
        bias_value,
        weight_out,
        bias_out,
    ) = (
        lax.all_gather(first_gain, ("dp", "ctx"), axis=0, tiled=True),
        lax.all_gather(first_bias, ("dp", "ctx"), axis=0, tiled=True),
        lax.all_gather(query_weight, ("dp", "ctx"), axis=0, tiled=True),
        lax.all_gather(query_bias, ("dp", "ctx"), axis=0, tiled=True),
        lax.all_gather(key_weight, ("dp", "ctx"), axis=0, tiled=True),
        lax.all_gather(value_weight, ("dp", "ctx"), axis=0, tiled=True),
        lax.all_gather(value_bias, ("dp", "ctx"), axis=0, tiled=True),
        lax.all_gather(out_weight, ("dp", "ctx"), axis=0, tiled=True),
        lax.all_gather(out_bias, ("dp", "ctx"), axis=0, tiled=True),
    )
    normed_one = normalize(
        inputs, gain_one.astype(jnp.float32), bias_one.astype(jnp.float32)
    ).astype(jnp.bfloat16)
    queries = (
        jnp.dot(normed_one, weight_query, preferred_element_type=jnp.float32)
        + bias_query.astype(jnp.float32)
    ).astype(jnp.bfloat16)
    keys_local = jnp.dot(normed_one, weight_key, preferred_element_type=jnp.float32).astype(
        jnp.bfloat16
    )
    values_local = (
        jnp.dot(normed_one, weight_value, preferred_element_type=jnp.float32)
        + bias_value.astype(jnp.float32)
    ).astype(jnp.bfloat16)
    query_heads = queries.reshape(row_count, local_rows, HEADS, HEAD_DIM)
    kv_stack = jnp.concatenate([keys_local, values_local], axis=1).reshape(
        row_count, local_rows, 2 * width
    )

    def forward_step(state, piece, start):
        count = piece.shape[1]
        allowed = allowed_block(start, count)

        def forward_compute(current):
            accum, run_max, run_sum = current
            key_heads = piece[..., :width].reshape(row_count, count, HEADS, HEAD_DIM)
            value_heads = piece[..., width:].reshape(row_count, count, HEADS, HEAD_DIM)
            scores = (
                jnp.einsum(
                    "rqhd,rkhd->rhqk", query_heads, key_heads, preferred_element_type=jnp.float32
                )
                * scale
            )
            scores = jnp.where(allowed[:, None], scores, NEG_FILL)
            new_max = jnp.maximum(run_max, jnp.max(scores, axis=-1))
            weights = jnp.where(allowed[:, None], jnp.exp(scores - new_max[..., None]), 0.0)
            factor = jnp.exp(run_max - new_max)
            accum = accum * factor[..., None] + jnp.einsum(
                "rhqk,rkhd->rhqd",
                weights.astype(jnp.bfloat16),
                value_heads,
                preferred_element_type=jnp.float32,
            )
            return (accum, new_max, run_sum * factor + jnp.sum(weights, axis=-1))

        return lax.cond(jnp.any(allowed), forward_compute, lambda current: current, state)

    start_state = (
        jnp.zeros((row_count, HEADS, local_rows, HEAD_DIM), jnp.float32),
        jnp.full((row_count, HEADS, local_rows), NEG_FILL, jnp.float32),
        jnp.zeros((row_count, HEADS, local_rows), jnp.float32),
    )
    accum, run_max, run_sum = over_blocks(
        start_state, lax.all_gather(kv_stack, "ctx", axis=1, tiled=True), local_rows, forward_step
    )
    heads_out = accum / run_sum[..., None]
    log_total = run_max + jnp.log(run_sum)
    mixed = jnp.transpose(heads_out, (0, 2, 1, 3)).reshape(flat_rows, width).astype(jnp.bfloat16)
    branch = jnp.dot(mixed, weight_out, preferred_element_type=jnp.float32) + bias_out.astype(
        jnp.float32
    )
    middle = inputs + active * branch
    gain_two, bias_two, weight_up, bias_up, weight_down, bias_down = (
        lax.all_gather(second_gain, ("dp", "ctx"), axis=0, tiled=True),
        lax.all_gather(second_bias, ("dp", "ctx"), axis=0, tiled=True),
        lax.all_gather(up_weight, ("dp", "ctx"), axis=0, tiled=True),
        lax.all_gather(up_bias, ("dp", "ctx"), axis=0, tiled=True),
        lax.all_gather(down_weight, ("dp", "ctx"), axis=0, tiled=True),
        lax.all_gather(down_bias, ("dp", "ctx"), axis=0, tiled=True),
    )
    normed_two = normalize(
        middle, gain_two.astype(jnp.float32), bias_two.astype(jnp.float32)
    ).astype(jnp.bfloat16)
    pre_act = jnp.dot(normed_two, weight_up, preferred_element_type=jnp.float32) + bias_up.astype(
        jnp.float32
    )
    hidden = smooth(pre_act).astype(jnp.bfloat16)
    result = middle + active * (
        jnp.dot(hidden, weight_down, preferred_element_type=jnp.float32)
        + bias_down.astype(jnp.float32)
    )
    layer_out = result.astype(jnp.bfloat16).reshape(row_count, local_rows, model_width)
    grad_res = grad_out.astype(jnp.float32).reshape(flat_rows, model_width)
    gain_two_back, weight_up_back, weight_down_back = (
        lax.all_gather(second_gain, ("dp", "ctx"), axis=0, tiled=True),
        lax.all_gather(up_weight, ("dp", "ctx"), axis=0, tiled=True),
        lax.all_gather(down_weight, ("dp", "ctx"), axis=0, tiled=True),
    )
    grad_ffn = (active * grad_res).astype(jnp.bfloat16)
    grad_down = jnp.einsum("tf,td->fd", hidden, grad_ffn, preferred_element_type=jnp.float32)
    grad_down_sum = jnp.sum(grad_ffn.astype(jnp.float32), axis=0)
    grad_down_shard, grad_down_bias_shard = (
        lax.psum_scatter(grad_down, ("dp", "ctx"), scatter_dimension=0, tiled=True),
        lax.psum_scatter(grad_down_sum, ("dp", "ctx"), scatter_dimension=0, tiled=True),
    )
    grad_hidden = jnp.einsum(
        "td,fd->tf", grad_ffn, weight_down_back, preferred_element_type=jnp.float32
    )
    unused_value, smooth_back = jax.vjp(smooth, pre_act)
    grad_pre = smooth_back(grad_hidden)[0].astype(jnp.bfloat16)
    grad_up = jnp.einsum("td,tf->df", normed_two, grad_pre, preferred_element_type=jnp.float32)
    grad_up_sum = jnp.sum(grad_pre.astype(jnp.float32), axis=0)
    grad_normed_two = jnp.einsum(
        "tf,df->td", grad_pre, weight_up_back, preferred_element_type=jnp.float32
    )
    zero_bias = jnp.zeros((model_width,), jnp.float32)
    unused_two, norm_back_two = jax.vjp(
        normalize, middle, gain_two_back.astype(jnp.float32), zero_bias
    )
    grad_mid_norm, grad_gain_two, grad_bias_two = norm_back_two(grad_normed_two)
    grad_up_shard, grad_up_bias_shard, grad_gain_two_shard, grad_bias_two_shard = (
        lax.psum_scatter(grad_up, ("dp", "ctx"), scatter_dimension=0, tiled=True),
        lax.psum_scatter(grad_up_sum, ("dp", "ctx"), scatter_dimension=0, tiled=True),
        lax.psum_scatter(grad_gain_two, ("dp", "ctx"), scatter_dimension=0, tiled=True),
        lax.psum_scatter(grad_bias_two, ("dp", "ctx"), scatter_dimension=0, tiled=True),
    )
    grad_middle = grad_res + grad_mid_norm
    gain_one_back, weight_query_back, weight_key_back, weight_value_back, weight_out_back = (
        lax.all_gather(first_gain, ("dp", "ctx"), axis=0, tiled=True),
        lax.all_gather(query_weight, ("dp", "ctx"), axis=0, tiled=True),
        lax.all_gather(key_weight, ("dp", "ctx"), axis=0, tiled=True),
        lax.all_gather(value_weight, ("dp", "ctx"), axis=0, tiled=True),
        lax.all_gather(out_weight, ("dp", "ctx"), axis=0, tiled=True),
    )
    grad_branch = (active * grad_middle).astype(jnp.bfloat16)
    grad_out_w = jnp.einsum("td,te->de", mixed, grad_branch, preferred_element_type=jnp.float32)
    grad_out_sum = jnp.sum(grad_branch.astype(jnp.float32), axis=0)
    grad_out_w_shard, grad_out_b_shard = (
        lax.psum_scatter(grad_out_w, ("dp", "ctx"), scatter_dimension=0, tiled=True),
        lax.psum_scatter(grad_out_sum, ("dp", "ctx"), scatter_dimension=0, tiled=True),
    )
    grad_mixed = jnp.einsum(
        "te,de->td", grad_branch, weight_out_back, preferred_element_type=jnp.float32
    ).astype(jnp.bfloat16)
    grad_heads = grad_mixed.reshape(row_count, local_rows, HEADS, HEAD_DIM)
    delta = jnp.einsum("rqhd,rhqd->rhq", grad_heads.astype(jnp.float32), heads_out)

    def backward_terms(piece, start):
        count = piece.shape[1]
        allowed = allowed_block(start, count)

        def backward_compute(unused):
            key_heads = piece[..., :width].reshape(row_count, count, HEADS, HEAD_DIM)
            value_heads = piece[..., width:].reshape(row_count, count, HEADS, HEAD_DIM)
            scores = (
                jnp.einsum(
                    "rqhd,rkhd->rhqk", query_heads, key_heads, preferred_element_type=jnp.float32
                )
                * scale
            )
            probs = jnp.where(allowed[:, None], jnp.exp(scores - log_total[..., None]), 0.0)
            grad_probs = jnp.einsum(
                "rqhd,rkhd->rhqk", grad_heads, value_heads, preferred_element_type=jnp.float32
            )
            grad_scores = (probs * (grad_probs - delta[..., None])).astype(jnp.bfloat16)
            grad_query_part = (
                jnp.einsum(
                    "rhqk,rkhd->rqhd", grad_scores, key_heads, preferred_element_type=jnp.float32
                )
                * scale
            )
            grad_key_part = (
                jnp.einsum(
                    "rhqk,rqhd->rkhd", grad_scores, query_heads, preferred_element_type=jnp.float32
                )
                * scale
            )
            grad_value_part = jnp.einsum(
                "rhqk,rqhd->rkhd",
                probs.astype(jnp.bfloat16),
                grad_heads,
                preferred_element_type=jnp.float32,
            )
            return (
                grad_query_part,
                jnp.concatenate(
                    [
                        grad_key_part.reshape(row_count, count, width),
                        grad_value_part.reshape(row_count, count, width),
                    ],
                    axis=2,
                ),
            )

        def nothing(unused):
            return (
                jnp.zeros((row_count, local_rows, HEADS, HEAD_DIM), jnp.float32),
                jnp.zeros((row_count, count, 2 * width), jnp.float32),
            )

        return lax.cond(jnp.any(allowed), backward_compute, nothing, 0)

    query_zeros = jnp.zeros((row_count, local_rows, HEADS, HEAD_DIM), jnp.float32)

    def backward_step(state, piece, start):
        grad_query_total, grad_buffer = state
        grad_query_part, grad_kv_part = backward_terms(piece, start)
        count = piece.shape[1]
        previous = lax.dynamic_slice_in_dim(grad_buffer, start, count, 1)
        return (
            grad_query_total + grad_query_part,
            lax.dynamic_update_slice_in_dim(grad_buffer, previous + grad_kv_part, start, 1),
        )

    buffer_start = (query_zeros, jnp.zeros((row_count, local_rows * parts, 2 * width), jnp.float32))
    grad_query_total, grad_buffer = over_blocks(
        buffer_start, lax.all_gather(kv_stack, "ctx", axis=1, tiled=True), local_rows, backward_step
    )
    grad_kv = lax.psum_scatter(
        grad_buffer.astype(jnp.bfloat16), "ctx", scatter_dimension=1, tiled=True
    ).astype(jnp.float32)
    grad_queries = grad_query_total.reshape(flat_rows, width).astype(jnp.bfloat16)
    grad_kv_flat = grad_kv.reshape(flat_rows, 2 * width)
    grad_keys = grad_kv_flat[:, :width].astype(jnp.bfloat16)
    grad_values = grad_kv_flat[:, width:].astype(jnp.bfloat16)
    grad_wq = jnp.einsum("td,te->de", normed_one, grad_queries, preferred_element_type=jnp.float32)
    grad_wk = jnp.einsum("td,te->de", normed_one, grad_keys, preferred_element_type=jnp.float32)
    grad_wv = jnp.einsum("td,te->de", normed_one, grad_values, preferred_element_type=jnp.float32)
    grad_bq = jnp.sum(grad_queries.astype(jnp.float32), axis=0)
    grad_bv = jnp.sum(grad_values.astype(jnp.float32), axis=0)
    grad_normed_one = jnp.einsum(
        "te,de->td", grad_queries, weight_query_back, preferred_element_type=jnp.float32
    )
    grad_normed_one = grad_normed_one + jnp.einsum(
        "te,de->td", grad_keys, weight_key_back, preferred_element_type=jnp.float32
    )
    grad_normed_one = grad_normed_one + jnp.einsum(
        "te,de->td", grad_values, weight_value_back, preferred_element_type=jnp.float32
    )
    unused_one, norm_back_one = jax.vjp(
        normalize, inputs, gain_one_back.astype(jnp.float32), zero_bias
    )
    grad_in_norm, grad_gain_one, grad_bias_one = norm_back_one(grad_normed_one)
    grad_in = (
        (grad_middle + grad_in_norm)
        .astype(jnp.bfloat16)
        .reshape(row_count, local_rows, model_width)
    )
    (
        grad_wq_shard,
        grad_bq_shard,
        grad_wk_shard,
        grad_wv_shard,
        grad_bv_shard,
        grad_gain_one_shard,
        grad_bias_one_shard,
    ) = (
        lax.psum_scatter(grad_wq, ("dp", "ctx"), scatter_dimension=0, tiled=True),
        lax.psum_scatter(grad_bq, ("dp", "ctx"), scatter_dimension=0, tiled=True),
        lax.psum_scatter(grad_wk, ("dp", "ctx"), scatter_dimension=0, tiled=True),
        lax.psum_scatter(grad_wv, ("dp", "ctx"), scatter_dimension=0, tiled=True),
        lax.psum_scatter(grad_bv, ("dp", "ctx"), scatter_dimension=0, tiled=True),
        lax.psum_scatter(grad_gain_one, ("dp", "ctx"), scatter_dimension=0, tiled=True),
        lax.psum_scatter(grad_bias_one, ("dp", "ctx"), scatter_dimension=0, tiled=True),
    )
    return (
        layer_out,
        grad_in,
        grad_gain_one_shard,
        grad_bias_one_shard,
        grad_wq_shard,
        grad_bq_shard,
        grad_wk_shard,
        grad_wv_shard,
        grad_bv_shard,
        grad_out_w_shard,
        grad_out_b_shard,
        grad_gain_two_shard,
        grad_bias_two_shard,
        grad_up_shard,
        grad_up_bias_shard,
        grad_down_shard,
        grad_down_bias_shard,
    )


def solution(mesh):
    in_specs = (
        P("dp", "ctx", None),
        P("dp", "ctx"),
        P(),
        P("dp", "ctx"),
        P("dp", "ctx", None),
        P(("dp", "ctx")),
        P(("dp", "ctx")),
        P(("dp", "ctx"), None),
        P(("dp", "ctx")),
        P(("dp", "ctx"), None),
        P(("dp", "ctx"), None),
        P(("dp", "ctx")),
        P(("dp", "ctx"), None),
        P(("dp", "ctx")),
        P(("dp", "ctx")),
        P(("dp", "ctx")),
        P(("dp", "ctx"), None),
        P(("dp", "ctx")),
        P(("dp", "ctx"), None),
        P(("dp", "ctx")),
    )
    out_specs = (
        P("dp", "ctx", None),
        P("dp", "ctx", None),
        P(("dp", "ctx")),
        P(("dp", "ctx")),
        P(("dp", "ctx"), None),
        P(("dp", "ctx")),
        P(("dp", "ctx"), None),
        P(("dp", "ctx"), None),
        P(("dp", "ctx")),
        P(("dp", "ctx"), None),
        P(("dp", "ctx")),
        P(("dp", "ctx")),
        P(("dp", "ctx")),
        P(("dp", "ctx"), None),
        P(("dp", "ctx")),
        P(("dp", "ctx"), None),
        P(("dp", "ctx")),
    )
    return jax.shard_map(local, mesh=mesh, in_specs=in_specs, out_specs=out_specs, check_vma=False)
```

profile of v0, /device:TPU:0, one launch (start us, length us, event | category | flops | bytes accessed | tf_op | source)
XLA Modules:
  0.0 3466.9 jit_solution(203868724645858263)
XLA Ops:
  16.2 43.0 %all-reduce.18 = (bf16[2048]{0:T(1024)(128)(2,1)S(1)}, bf16[2048]{0:T(1024)(128)(2,1)S(1)}, bf16[2048]{0:T(1024)(128)(2,1)S(1)}, bf16[2048]{0:T(1024)(128)(2,1)S...) all-reduce(bf16[2048]{0:T(1024)(128)(2,1)S(1)} %dynamic-update-slic, ...), channel_id=1, replica_groups=mesh['dp'=4,'ctx'=8] {'dp','ctx'}, use_global_device_ids=true, to_apply=%add.2 | all-reduce | flops 16384 | bytes 65536
  61.9 29.5 all-gather.10.cloned.1.call-done
  96.3 74.1 %all-gather.12.cloned.1.call-done = bf16[2048,2048]{1,0:T(8,128)(2,1)} async-done(((bf16[64,2048]{1,0:T(8,128)(2,1)}), bf16[2048,2048]{1,0:T(8,128)(2,1)}) %all-gather.12.cloned.1.call-update) | async-done | bytes 8388624 | tf_op jit(solution)/shard_map/all_gather | solution.py:95
  178.9 39.2 %all-gather.1 = bf16[32,1,256]{2,1,0:T(2,128)(2,1)S(1)} all-gather(bf16[1,1,256]{2,1,0:T(2,128)(2,1)S(1)} %reshape.561), channel_id=1, replica_groups=mesh['dp'=4,'ctx'=8] {'dp','ctx'}, dimensions={0}, use_global_device_ids=true | all-gather | bytes 16896 | tf_op jit(solution)/shard_map/all_gather | solution.py:166
  218.2 9.3 all_gather.60
  227.5 22.1 all-gather.14.cloned.1.call-done
  255.3 77.0 %all-gather.22.cloned.1.call-done = bf16[1024,4096]{1,0:T(8,128)(2,1)} async-done(((bf16[128,4096]{1,0:T(8,128)(2,1)}), bf16[1024,4096]{1,0:T(8,128)(2,1)}) %all-gather.22.cloned.1.call-update) | async-done | bytes 8388624 | tf_op jit(solution)/shard_map/all_gather | solution.py:153
  332.3 12.0 copy.60
  344.4 16.0 while.34
  360.6 50.6 %all-gather.16.cloned.1.call-done = bf16[2048,2048]{1,0:T(8,128)(2,1)} async-done(((bf16[64,2048]{1,0:T(8,128)(2,1)}), bf16[2048,2048]{1,0:T(8,128)(2,1)}) %all-gather.16.cloned.1.call-update) | async-done | bytes 8388624 | tf_op jit(solution)/shard_map/all_gather | solution.py:97
  416.3 191.2 %all-gather.18.cloned.1.call-done = bf16[2048,8192]{1,0:T(8,128)(2,1)} async-done(((bf16[64,8192]{1,0:T(8,128)(2,1)}), bf16[2048,8192]{1,0:T(8,128)(2,1)}) %all-gather.18.cloned.1.call-update) | async-done | bytes 33554448 | tf_op jit(solution)/shard_map/all_gather | solution.py:165
  607.5 17.9 convolution_add_fusion
  625.4 178.0 %all-gather.20.cloned.1.call-done = bf16[8192,2048]{1,0:T(8,128)(2,1)} async-done(((bf16[256,2048]{1,0:T(8,128)(2,1)}), bf16[8192,2048]{1,0:T(8,128)(2,1)}) %all-gather.20.cloned.1.call-update) | async-done | bytes 33554448 | tf_op jit(solution)/shard_map/all_gather | solution.py:167
  803.5 19.8 convert_reduce_fusion
  823.2 19.6 multiply_reduce_fusion
  863.9 65.4 %while.35 = (s32[]{:T(128)}, f32[1,128,32,64]{1,3,2,0:T(8,128)}, f32[1,1024,4096]{1,2,0:T(8,128)}, s32[1,128]{1,0:T(1,128)S(1)}, s32[1,1024]{1,0:T(1,128)S(1)}, ...) while((s32[]{:T(128)}, f32[1,128,32,64]{1,3,2,0:T(8,128)}, ...), condition=%wide.region_17.18_spmd.clone, body=%wide.region_13.17_spmd.clone.sunk | while | flops 341377280 | bytes 32052024 | solution.py:34
  865.5 8.9 conditional.7
  929.2 9.1 convert_element_type.170
  938.3 36.6 %copy.75 = bf16[1,1024,4096]{2,0,1:T(2,128)(2,1)} copy(bf16[1,1024,4096]{1,2,0:T(8,128)(2,1)} %convert_element_type.170) | data formatting | bytes 16777216
  974.9 16.8 copy.80
  1000.2 139.4 %reduce-scatter.22.cloned.1.call-done = bf16[128,4096]{1,0:T(8,128)(2,1)} async-done(((bf16[1024,4096]{1,0:T(8,128)(2,1)}), bf16[128,4096]{1,0:T(8,128)(2,1)}) %reduce-scatter.22.cloned.1.call-update) | async-done | bytes 1048592
  1174.4 9.2 fusion.99
  1201.6 24.9 fusion.87
  1227.5 25.5 fusion.80
  1253.6 17.8 fusion.43
  1272.8 16.1 all-reduce.21.cloned.1.call-done
  1300.3 179.1 %reduce-scatter.10.cloned.1.call-done = f32[64,2048]{1,0:T(8,128)} async-done(((f32[2048,2048]{1,0:T(8,128)}), f32[64,2048]{1,0:T(8,128)}) %reduce-scatter.10.cloned.1.call-update) | async-done | bytes 524304 | tf_op jit(solution)/shard_map/reduce_scatter | solution.py:347
  1479.4 187.4 %reduce-scatter.16.cloned.1.call-done = f32[64,2048]{1,0:T(8,128)} async-done(((f32[2048,2048]{1,0:T(8,128)}), f32[64,2048]{1,0:T(8,128)}) %reduce-scatter.16.cloned.1.call-update) | async-done | bytes 524304 | tf_op jit(solution)/shard_map/reduce_scatter | solution.py:228
  1666.8 187.2 %reduce-scatter.12.cloned.1.call-done = f32[64,2048]{1,0:T(8,128)} async-done(((f32[2048,2048]{1,0:T(8,128)}), f32[64,2048]{1,0:T(8,128)}) %reduce-scatter.12.cloned.1.call-update) | async-done | bytes 524304 | tf_op jit(solution)/shard_map/reduce_scatter | solution.py:349
  1854.0 187.3 %reduce-scatter.14.cloned.1.call-done = f32[64,2048]{1,0:T(8,128)} async-done(((f32[2048,2048]{1,0:T(8,128)}), f32[64,2048]{1,0:T(8,128)}) %reduce-scatter.14.cloned.1.call-update) | async-done | bytes 524304 | tf_op jit(solution)/shard_map/reduce_scatter | solution.py:350
  2041.3 710.0 %reduce-scatter.18.cloned.1.call-done = f32[64,8192]{1,0:T(8,128)} async-done(((f32[2048,8192]{1,0:T(8,128)}), f32[64,8192]{1,0:T(8,128)}) %reduce-scatter.18.cloned.1.call-update) | async-done | bytes 2097168 | tf_op jit(solution)/shard_map/reduce_scatter | solution.py:211
  2751.3 708.8 %reduce-scatter.20.cloned.1.call-done = f32[256,2048]{1,0:T(8,128)} async-done(((f32[8192,2048]{1,0:T(8,128)}), f32[256,2048]{1,0:T(8,128)}) %reduce-scatter.20.cloned.1.call-update) | async-done | bytes 2097168 | tf_op jit(solution)/shard_map/reduce_scatter | solution.py:192
  (279 shorter events, 207.8 us)
Async XLA Ops:
  7.2 84.2 %all-gather.10.cloned.1.call-start = ((), (), s32[]{:S(2)}) async-start(), calls=%async_computation.7 | async-start | bytes 8650752 | tf_op jit(solution)/shard_map/all_gather | solution.py:94
  7.9 162.5 %all-gather.12.cloned.1.call-start = ((), (), s32[]{:S(2)}) async-start(), calls=%async_computation.8 | async-start | bytes 8650752 | tf_op jit(solution)/shard_map/all_gather | solution.py:95
  8.7 240.9 %all-gather.14.cloned.1.call-start = ((), (), s32[]{:S(2)}) async-start(), calls=%async_computation.9 | async-start | bytes 8650752 | tf_op jit(solution)/shard_map/all_gather | solution.py:92
  9.4 322.9 %all-gather.22.cloned.1.call-start = ((), (), s32[]{:S(2)}) async-start(), calls=%async_computation.19 | async-start | bytes 9437184 | tf_op jit(solution)/shard_map/all_gather | solution.py:153
  59.3 190.3 %copy-start.14 = (f32[2048]{0:T(1024)}, f32[2048]{0:T(1024)S(1)}, u32[]{:S(2)}) copy-start(f32[2048]{0:T(1024)S(1)} %convert_element_type.146) | copy-start | bytes 24580
  59.3 190.3 %copy-start.12 = (f32[2048]{0:T(1024)}, f32[2048]{0:T(1024)S(1)}, u32[]{:S(2)}) copy-start(f32[2048]{0:T(1024)S(1)} %convert_element_type.145) | copy-start | bytes 24580
  60.5 189.1 %copy-start.19 = (f32[128]{0:T(128)}, f32[128]{0:T(128)S(1)}, u32[]{:S(2)}) copy-start(f32[128]{0:T(128)S(1)} %broadcast_multiply_fusion.1) | copy-start | bytes 1540
  61.8 34.4 copy-start.28
  61.8 187.7 %copy-start.21 = (f32[128]{0:T(128)}, f32[128]{0:T(128)S(1)}, u32[]{:S(2)}) copy-start(f32[128]{0:T(128)S(1)} %fusion.78) | copy-start | bytes 1540
  61.9 108.5 %copy-start = (bf16[1,128,2048]{2,1,0:T(8,128)(2,1)S(1)}, bf16[1,128,2048]{2,1,0:T(8,128)(2,1)}, u32[]{:S(2)}) copy-start(bf16[1,128,2048]{2,1,0:T(8,128)(2,1)} %param.28) | copy-start | bytes 1572868
  175.1 43.1 %copy-start.18 = (s32[1,128]{1,0:T(1,128)S(1)}, s32[1,128]{1,0:T(1,128)}, u32[]{:S(2)}) copy-start(s32[1,128]{1,0:T(1,128)} %param.31) | copy-start | bytes 1540
  175.1 52.4 %copy-start.31 = (s32[1,128]{1,0:T(1,128)S(1)}, s32[1,128]{1,0:T(1,128)}, u32[]{:S(2)}) copy-start(s32[1,128]{1,0:T(1,128)} %param.29) | copy-start | bytes 1540
  176.2 235.0 %all-gather.16.cloned.1.call-start = ((), (), s32[]{:S(2)}) async-start(), calls=%async_computation.10 | async-start | bytes 8650752 | tf_op jit(solution)/shard_map/all_gather | solution.py:97
  176.8 430.7 %all-gather.18.cloned.1.call-start = ((), (), s32[]{:S(2)}) async-start(), calls=%async_computation.11 | async-start | bytes 34603008 | tf_op jit(solution)/shard_map/all_gather | solution.py:165
  177.4 626.1 %all-gather.20.cloned.1.call-start = ((), (), s32[]{:S(2)}) async-start(), calls=%async_computation.12 | async-start | bytes 34603008 | tf_op jit(solution)/shard_map/all_gather | solution.py:167
  178.1 961.5 %reduce-scatter.22.cloned.1.call-start = ((), (), s32[]{:S(2)}) async-start(), calls=%async_computation.20 | async-start | bytes 9437184
  218.2 389.3 %copy-start.16 = (f32[2048]{0:T(1024)}, f32[2048]{0:T(1024)S(1)}, u32[]{:S(2)}) copy-start(f32[2048]{0:T(1024)S(1)} %convert_element_type.158) | copy-start | bytes 24580
  227.5 617.0 %copy-start.23 = (f32[128]{0:T(128)}, f32[128]{0:T(128)S(1)}, u32[]{:S(2)}) copy-start(f32[128]{0:T(128)S(1)} %fusion.77) | copy-start | bytes 1540
  360.6 55.4 %copy-start.7 = (bf16[1,32,128,64]{2,3,1,0:T(8,128)(2,1)}, bf16[1,32,128,64]{2,3,1,0:T(8,128)(2,1)S(1)}, u32[]{:S(2)}) copy-start(bf16[1,32,128,64]{2,3,1,0:T(8,128)(2,1)S(1)} %fusion.73) | copy-start | bytes 1572868
  416.0 426.9 %copy-start.2 = (f32[128,2048]{1,0:T(8,128)}, f32[128,2048]{1,0:T(8,128)S(1)}, u32[]{:S(2)}) copy-start(f32[128,2048]{1,0:T(8,128)S(1)} %get-tuple-element.667) | copy-start | bytes 3145732
  607.5 196.0 %copy-start.9 = (bf16[1,128,2048]{2,1,0:T(8,128)(2,1)S(1)}, bf16[1,128,2048]{2,1,0:T(8,128)(2,1)}, u32[]{:S(2)}) copy-start(bf16[1,128,2048]{2,1,0:T(8,128)(2,1)} %param.32) | copy-start | bytes 1572868
  844.5 9.2 copy-start.26
  991.7 297.2 %all-reduce.21.cloned.1.call-start = ((), (), s32[]{:S(2)}) async-start(), calls=%async_computation.21 | async-start | bytes 196608
  1156.9 8.2 copy-start.15
  1165.1 314.4 %reduce-scatter.10.cloned.1.call-start = ((), (), s32[]{:S(2)}) async-start(), calls=%async_computation.13 | async-start | bytes 17301504 | tf_op jit(solution)/shard_map/reduce_scatter | solution.py:347
  1173.3 493.4 %reduce-scatter.16.cloned.1.call-start = ((), (), s32[]{:S(2)}) async-start(), calls=%async_computation.16 | async-start | bytes 17301504 | tf_op jit(solution)/shard_map/reduce_scatter | solution.py:228
  1183.6 670.4 %reduce-scatter.12.cloned.1.call-start = ((), (), s32[]{:S(2)}) async-start(), calls=%async_computation.14 | async-start | bytes 17301504 | tf_op jit(solution)/shard_map/reduce_scatter | solution.py:349
  1192.0 849.3 %reduce-scatter.14.cloned.1.call-start = ((), (), s32[]{:S(2)}) async-start(), calls=%async_computation.15 | async-start | bytes 17301504 | tf_op jit(solution)/shard_map/reduce_scatter | solution.py:350
  1200.4 1550.9 %reduce-scatter.18.cloned.1.call-start = ((), (), s32[]{:S(2)}) async-start(), calls=%async_computation.17 | async-start | bytes 69206016 | tf_op jit(solution)/shard_map/reduce_scatter | solution.py:211
  1226.5 2233.7 %reduce-scatter.20.cloned.1.call-start = ((), (), s32[]{:S(2)}) async-start(), calls=%async_computation.18 | async-start | bytes 69206016 | tf_op jit(solution)/shard_map/reduce_scatter | solution.py:192
  1253.6 17.9 copy-start.6
  1253.6 17.9 copy-start.27
  (15 other events, 46.3 us)
Sparse Core Ops, SparseCore 0:
  11.0 80.3 all-gather.9
  94.4 75.9 all-gather.11
  173.4 76.1 all-gather.13
  251.6 80.6 all-gather.21
  335.1 76.0 all-gather.15
  414.0 193.3 all-gather.17
  610.4 192.9 all-gather.19
  991.8 147.7 reduce-scatter.21
  1165.2 123.6 all-reduce.20
  1291.7 187.6 reduce-scatter.9
  1482.4 184.3 reduce-scatter.15
  1669.6 184.3 reduce-scatter.11
  1857.0 184.3 reduce-scatter.13
  2044.2 707.0 reduce-scatter.17
  2754.2 705.9 reduce-scatter.19
where the time goes:
time: 3480 us; the launch traced here: 3470 us
  waiting for transfers between devices  2940 us (84%)
  matrix products  214 us (6%)
  local copies, waits for them, and re-layouts  115 us (3%)
  blocking collectives  91.5 us (3%)
  other arithmetic  76.3 us (2%)
    reduce_scatter x1, waiting for transfers between devices, local(): lax.psum_scatter(grad_up, ('dp', 'ctx'), scatter_dimension=0, tiled=True)  710 us
    reduce_scatter x1, waiting for transfers between devices, local(): lax.psum_scatter(grad_down, ('dp', 'ctx'), scatter_dimension=0, tiled=True)  709 us
    all_gather x1, waiting for transfers between devices, local(): lax.all_gather(up_weight, ('dp', 'ctx'), axis=0, tiled=True)  191 us
    reduce_scatter x1, waiting for transfers between devices, local(): lax.psum_scatter(grad_out_w, ('dp', 'ctx'), scatter_dimension=0, tiled=True)  187 us
    reduce_scatter x1, waiting for transfers between devices, local(): lax.psum_scatter(grad_wv, ('dp', 'ctx'), scatter_dimension=0, tiled=True)  187 us
    reduce_scatter x1, waiting for transfers between devices, local(): lax.psum_scatter(grad_wk, ('dp', 'ctx'), scatter_dimension=0, tiled=True)  187 us
    reduce_scatter x1, waiting for transfers between devices, local(): lax.psum_scatter(grad_wq, ('dp', 'ctx'), scatter_dimension=0, tiled=True)  179 us
    all_gather x1, waiting for transfers between devices, local(): lax.all_gather(down_weight, ('dp', 'ctx'), axis=0, tiled=True)  178 us
  transfers between devices with their start and end apart: 15, of which 15 were waited for; matrix products, arithmetic and copies ran while one was open for 6% of the time, Pallas kernels for 0%

commit v1 on v0

v1 whole, which is shorter than its diff:
```python
import jax
import jax.numpy as jnp
from jax import lax
from jax.experimental import pallas as pl
from jax.experimental.pallas import tpu as pltpu
from jax.sharding import PartitionSpec as P

HEADS = 32
HEAD_DIM = 64
EPSILON = 1e-05
NEG_FILL = -1e30
SCALE = HEAD_DIM ** (-0.5)
QUERY_BLOCK = 256
BF16 = jnp.bfloat16
F32 = jnp.float32

NN = (((1,), (0,)), ((), ()))
NT = (((1,), (1,)), ((), ()))
TN = (((0,), (0,)), ((), ()))


def dot(left, right, dims=NN):
    return lax.dot_general(left, right, dims, preferred_element_type=F32)


def forward_kernel(qkv_ref, seg_col_ref, seg_row_ref, mixed_ref, log_ref, *, heads, lanes, block):
    rows = qkv_ref.shape[0]
    head_of_lane = lax.broadcasted_iota(jnp.int32, (1, lanes), 1) // HEAD_DIM
    diagonal = lax.broadcasted_iota(jnp.int32, (block, block), 1) <= lax.broadcasted_iota(
        jnp.int32, (block, block), 0
    )
    for b in range(rows // block):
        low, high = b * block, (b + 1) * block
        queries = qkv_ref[low:high, :lanes] * jnp.asarray(SCALE, BF16)
        keys = qkv_ref[:high, lanes : 2 * lanes]
        values = qkv_ref[:high, 2 * lanes :]
        allowed = seg_col_ref[low:high, :] == seg_row_ref[:, :high]
        last = allowed[:, low:] & diagonal
        allowed = jnp.concatenate([allowed[:, :low], last], axis=1) if b else last
        mixed = jnp.zeros((block, lanes), F32)
        for h in range(heads):
            mine = head_of_lane == h
            scores = dot(jnp.where(mine, queries, jnp.zeros_like(queries)), keys, NT)
            scores = jnp.where(allowed, scores, NEG_FILL)
            top = jnp.max(scores, axis=1, keepdims=True)
            weights = jnp.exp(scores - top)
            total = jnp.sum(weights, axis=1, keepdims=True)
            product = dot(weights.astype(BF16), values)
            mixed = mixed + jnp.where(mine, product / total, 0.0)
            log_total = jnp.broadcast_to(top + jnp.log(total), (block, 128))
            log_ref[h : h + 1, low:high] = jnp.transpose(log_total)[:1, :]
        mixed_ref[low:high, :] = mixed.astype(BF16)


def backward_kernel(
    qkv_ref, grad_ref, log_ref, delta_ref, seg_col_ref, seg_row_ref, out_ref, dk_ref, dv_ref, *, heads, lanes, block
):
    rows = qkv_ref.shape[0]
    head_of_lane = lax.broadcasted_iota(jnp.int32, (1, lanes), 1) // HEAD_DIM
    diagonal = lax.broadcasted_iota(jnp.int32, (block, block), 0) <= lax.broadcasted_iota(
        jnp.int32, (block, block), 1
    )
    scale = jnp.asarray(SCALE, BF16)
    for b in range(rows // block):
        low, high = b * block, (b + 1) * block
        queries = qkv_ref[low:high, :lanes] * scale
        grads = grad_ref[low:high, :]
        keys = qkv_ref[:high, lanes : 2 * lanes]
        values = qkv_ref[:high, 2 * lanes :]
        allowed = seg_col_ref[:high, :] == seg_row_ref[:, low:high]
        last = allowed[low:, :] & diagonal
        allowed = jnp.concatenate([allowed[:low, :], last], axis=0) if b else last
        grad_queries = jnp.zeros((block, lanes), F32)
        grad_keys = jnp.zeros((high, lanes), F32)
        grad_values = jnp.zeros((high, lanes), F32)
        for h in range(heads):
            mine = head_of_lane == h
            query_h = jnp.where(mine, queries, jnp.zeros_like(queries))
            grad_h = jnp.where(mine, grads, jnp.zeros_like(grads))
            scores = dot(keys, query_h, NT)
            probs = jnp.where(allowed, jnp.exp(scores - log_ref[h : h + 1, low:high]), 0.0)
            grad_probs = dot(values, grad_h, NT)
            grad_scores = (probs * (grad_probs - delta_ref[h : h + 1, low:high])).astype(BF16)
            grad_values = grad_values + dot(probs.astype(BF16), grad_h)
            grad_keys = grad_keys + dot(grad_scores, query_h)
            grad_queries = grad_queries + jnp.where(mine, dot(grad_scores, keys, TN), 0.0)
        out_ref[low:high, :lanes] = (grad_queries * SCALE).astype(BF16)
        if b:
            dk_ref[:low, :] = dk_ref[:low, :] + grad_keys[:low, :]
            dv_ref[:low, :] = dv_ref[:low, :] + grad_values[:low, :]
        dk_ref[low:high, :] = grad_keys[low:, :]
        dv_ref[low:high, :] = grad_values[low:, :]
    out_ref[:, lanes : 2 * lanes] = dk_ref[...].astype(BF16)
    out_ref[:, 2 * lanes :] = dv_ref[...].astype(BF16)


def attention_forward(qkv, seg_col, seg_row):
    rows, lanes = qkv.shape[0], qkv.shape[1] // 3
    heads = lanes // HEAD_DIM
    pairs = rows * rows * heads // 2
    return pl.pallas_call(
        lambda *refs: forward_kernel(*refs, heads=heads, lanes=lanes, block=QUERY_BLOCK),
        out_shape=(jax.ShapeDtypeStruct((rows, lanes), BF16), jax.ShapeDtypeStruct((heads, rows), F32)),
        compiler_params=pltpu.CompilerParams(vmem_limit_bytes=48 * 2**20),
        cost_estimate=pl.CostEstimate(flops=pairs * 1024, bytes_accessed=8 * rows * lanes, transcendentals=pairs),
        name="attention_forward",
    )(qkv, seg_col, seg_row)


def attention_backward(qkv, grads, log_total, delta, seg_col, seg_row):
    rows, lanes = qkv.shape[0], qkv.shape[1] // 3
    heads = lanes // HEAD_DIM
    pairs = rows * rows * heads // 2
    return pl.pallas_call(
        lambda *refs: backward_kernel(*refs, heads=heads, lanes=lanes, block=QUERY_BLOCK),
        out_shape=jax.ShapeDtypeStruct((rows, 3 * lanes), BF16),
        scratch_shapes=[pltpu.VMEM((rows, lanes), F32), pltpu.VMEM((rows, lanes), F32)],
        compiler_params=pltpu.CompilerParams(vmem_limit_bytes=48 * 2**20),
        cost_estimate=pl.CostEstimate(flops=pairs * 2560, bytes_accessed=14 * rows * lanes, transcendentals=pairs),
        name="attention_backward",
    )(qkv, grads, log_total, delta, seg_col, seg_row)


def chips():
    return lax.axis_size("ctx") // 2


def turn(value, k):
    count = chips()
    return lax.ppermute(
        value, "ctx", [(2 * s + core, 2 * ((s + k) % count) + core) for s in range(count) for core in range(2)]
    )


def swap(value):
    return lax.ppermute(value, "ctx", [(i, i ^ 1) for i in range(2 * chips())])


def place():
    me = lax.axis_index("ctx")
    return me // 2, me % 2


def gather_ctx(block):
    count = chips()
    chip, core = place()
    same = [block] + [turn(block, k) for k in range(1, count)]
    other = [swap(item) for item in same]
    out = jnp.zeros((2 * count,) + block.shape, block.dtype)
    for k in range(count):
        base = 2 * ((chip + count - k) % count)
        out = lax.dynamic_update_index_in_dim(out, same[k], base + core, 0)
        out = lax.dynamic_update_index_in_dim(out, other[k], base + 1 - core, 0)
    return out


def exchange_ctx(blocks):
    count = chips()
    chip, core = place()
    pairs = blocks.reshape((count, 2) + blocks.shape[1:])
    same = []
    for k in range(count):
        piece = lax.dynamic_index_in_dim(pairs, (chip + k) % count, 0, keepdims=False)
        same.append(turn(piece, k) if k else piece)
    mine = [lax.dynamic_index_in_dim(item, core, 0, keepdims=False) for item in same]
    other = swap(jnp.stack([lax.dynamic_index_in_dim(item, 1 - core, 0, keepdims=False) for item in same]))
    out = jnp.zeros(blocks.shape, blocks.dtype)
    for k in range(count):
        base = 2 * ((chip + count - k) % count)
        out = lax.dynamic_update_index_in_dim(out, mine[k], base + core, 0)
        out = lax.dynamic_update_index_in_dim(out, other[k], base + 1 - core, 0)
    return out


def split_rows(rows):
    count = chips()
    chip, core = place()
    pairs = rows.reshape((count, 2, rows.shape[0] // (2 * count), rows.shape[1]))
    turned = [lax.dynamic_index_in_dim(pairs, (chip + k) % count, 0, keepdims=False) for k in range(1, count + 1)]
    pick = lambda which: jnp.concatenate(
        [lax.dynamic_index_in_dim(item, which, 0, keepdims=False) for item in turned], axis=0
    )
    return pick(core), pick(1 - core)


def reduce_ctx(left, right, dims):
    count = chips()
    mine, other = split_rows(left)
    arrived = swap(dot(other, right, dims).astype(BF16))
    own = dot(mine, right, dims)
    n = own.shape[0] // count
    sums = [own[k * n : (k + 1) * n] + arrived[k * n : (k + 1) * n].astype(F32) for k in range(count)]
    total = sums[-1]
    for k in range(1, count):
        total = total + turn(sums[k - 1].astype(BF16), k).astype(F32)
    return total


def reduce_ctx_small(blocks):
    count = chips()
    chip, core = place()
    pairs = blocks.reshape(count, 2, blocks.shape[1])
    arrived = swap(lax.dynamic_index_in_dim(pairs, 1 - core, 1, keepdims=False))
    sums = arrived + lax.dynamic_index_in_dim(pairs, core, 1, keepdims=False)
    total = lax.dynamic_index_in_dim(sums, chip, 0, keepdims=False)
    for k in range(1, count):
        total = total + turn(lax.dynamic_index_in_dim(sums, (chip + k) % count, 0, keepdims=False), k)
    return total


def gather_dp_small(value):
    parts = lax.axis_size("dp")
    me = lax.axis_index("dp")
    out = jnp.zeros((parts,) + value.shape, value.dtype)
    out = lax.dynamic_update_index_in_dim(out, value, me, 0)
    for k in range(1, parts):
        arrived = lax.ppermute(value, "dp", [(i, (i + k) % parts) for i in range(parts)])
        out = lax.dynamic_update_index_in_dim(out, arrived, (me + parts - k) % parts, 0)
    return out


def reduce_dp_small(blocks):
    parts = lax.axis_size("dp")
    me = lax.axis_index("dp")
    total = lax.dynamic_index_in_dim(blocks, me, 0, keepdims=False)
    for k in range(1, parts):
        piece = lax.dynamic_index_in_dim(blocks, (me + k) % parts, 0, keepdims=False)
        total = total + lax.ppermute(piece, "dp", [(i, (i + k) % parts) for i in range(parts)])
    return total


def gather_dp(value):
    return lax.all_gather(value, "dp", axis=0, tiled=True)


def scatter_dp(value):
    return lax.psum_scatter(value, "dp", scatter_dimension=0, tiled=True)


def standardize(values):
    average = jnp.mean(values, axis=-1, keepdims=True)
    centered = values - average
    variance = jnp.mean(centered * centered, axis=-1, keepdims=True)
    factor = lax.rsqrt(variance + EPSILON)
    return centered * factor, factor


def norm_back(grad, gain, standard, factor):
    scaled = grad * gain
    return (
        scaled
        - jnp.mean(scaled, axis=-1, keepdims=True)
        - standard * jnp.mean(scaled * standard, axis=-1, keepdims=True)
    ) * factor


def smooth(pre_act):
    return jax.nn.gelu(pre_act, approximate=True)


def smooth_slope(u):
    inner = 0.7978845608028654 * (u + 0.044715 * u * u * u)
    bend = jnp.tanh(inner)
    return 0.5 * (1.0 + bend) + 0.5 * u * (1.0 - bend * bend) * 0.7978845608028654 * (1.0 + 3.0 * 0.044715 * u * u)


def local(
    tokens_in,
    exit_layer,
    layer_index,
    segment_ids,
    grad_out,
    first_gain,
    first_bias,
    query_weight,
    query_bias,
    key_weight,
    value_weight,
    value_bias,
    out_weight,
    out_bias,
    second_gain,
    second_bias,
    up_weight,
    up_bias,
    down_weight,
    down_bias,
):
    T, N = lax.axis_size("ctx"), lax.axis_size("dp")
    me = lax.axis_index("ctx")
    n, D = tokens_in.shape[1], tokens_in.shape[2]
    r = first_gain.shape[0]
    f = up_bias.shape[0]
    S = T * n
    B = max(HEAD_DIM, r)
    A = D // (T * B)
    L = A * B
    x = tokens_in[0]
    g_out = grad_out[0]
    active = (exit_layer[0] > layer_index[0]).astype(F32)

    def columns(weight, lead, width):
        return weight.reshape(r, lead, T, width).transpose(2, 0, 1, 3).reshape(T, r, lead * width)

    qkv_send = jnp.concatenate([columns(w, A, B) for w in (query_weight, key_weight, value_weight)], axis=2)
    w_qkv = gather_dp(exchange_ctx(qkv_send).reshape(T * r, 3 * L))
    natural = r % HEAD_DIM == 0
    if natural:
        w_out = gather_dp(out_weight)
    else:
        w_all = lax.all_gather(out_weight, ("dp", "ctx"), axis=0, tiled=True).reshape(A, T, B, D)
        w_out = lax.dynamic_index_in_dim(w_all, me, 1, keepdims=False).reshape(L, D)
    w_up = gather_dp(exchange_ctx(columns(up_weight, N, f)).reshape(T * r, N * f))
    w_down = gather_dp(down_weight)

    small = jnp.concatenate(
        [first_gain, first_bias, query_bias, value_bias, out_bias, second_gain, second_bias, down_bias, up_bias]
    )
    small_dp = gather_dp_small(small).reshape(-1)
    flags = jnp.concatenate([active.astype(BF16), segment_ids[0].astype(BF16)])
    small_all = gather_ctx(jnp.concatenate([small_dp, flags]))
    params = small_all[:, : N * (8 * r + f)].reshape(T, N, 8 * r + f).transpose(1, 0, 2)
    feature = lambda i: params[:, :, i * r : (i + 1) * r].reshape(D).astype(F32)
    gain_one, bias_one, bias_query, bias_value, bias_out, gain_two, bias_two, bias_down = (
        feature(i) for i in range(8)
    )
    bias_up = lax.dynamic_index_in_dim(params, me, 1, keepdims=False)[:, 8 * r :].reshape(N * f).astype(F32)
    active_row = small_all[:, -2 * n : -n].reshape(S)
    segs = small_all[:, -n:].reshape(S).astype(jnp.int32)
    seg_col, seg_row = segs.reshape(S, 1), segs.reshape(1, S)
    own_heads = lambda v: lax.dynamic_index_in_dim(v.reshape(A, T, B), me, 1, keepdims=False).reshape(L)
    bias_qkv = jnp.concatenate([own_heads(bias_query), jnp.zeros((L,), F32), own_heads(bias_value)])

    x_all = gather_ctx(x).reshape(S, D)
    standard_one, _ = standardize(x_all.astype(F32))
    normed_one = (standard_one * gain_one + bias_one).astype(BF16)
    qkv = (dot(normed_one, w_qkv) + bias_qkv).astype(BF16)
    mixed, log_total = attention_forward(qkv, seg_col, seg_row)
    branch = reduce_ctx(mixed, w_out, NN) + bias_out
    inputs = x.astype(F32)
    active_own = active[:, None]
    middle = inputs + active_own * branch

    standard_two, factor_two = standardize(middle)
    normed_two = (standard_two * gain_two + bias_two).astype(BF16)
    g_all = gather_ctx(g_out).reshape(S, D)
    normed_two_all = gather_ctx(normed_two).reshape(S, D)
    pre_act = dot(normed_two_all, w_up) + bias_up
    hidden = smooth(pre_act).astype(BF16)
    feed = reduce_ctx(hidden, w_down, NN)
    layer_out = (middle + active_own * (feed + bias_down)).astype(BF16)[None]

    grad_ffn = (active_row[:, None] * g_all).astype(BF16)
    grad_hidden = dot(grad_ffn, w_down, NT)
    grad_pre = (grad_hidden * smooth_slope(pre_act)).astype(BF16)
    grad_normed_two = reduce_ctx(grad_pre, w_up, NT)
    grad_down = scatter_dp(dot(hidden, grad_ffn, TN).astype(BF16)).astype(F32)
    grad_up_mine = scatter_dp(dot(normed_two_all, grad_pre, TN).astype(BF16))

    def rows_back(mine, lead, width):
        got = exchange_ctx(mine.reshape(T, r, lead * width))
        return got.reshape(T, r, lead, width).transpose(1, 2, 0, 3).reshape(r, lead * T * width).astype(F32)

    grad_up = rows_back(grad_up_mine, N, f)
    grad_res = g_out.astype(F32)
    grad_middle = grad_res + norm_back(grad_normed_two, gain_two, standard_two, factor_two)
    grad_branch = (active_own * grad_middle).astype(BF16)

    grad_branch_all = gather_ctx(grad_branch).reshape(S, D)
    grad_heads = dot(grad_branch_all, w_out, NT).astype(BF16)
    delta = jnp.sum(
        (grad_heads.astype(F32) * mixed.astype(F32)).reshape(S, L // HEAD_DIM, HEAD_DIM), axis=2
    ).transpose()
    grad_qkv = attention_backward(qkv, grad_heads, log_total, delta, seg_col, seg_row)
    grad_normed_one = reduce_ctx(grad_qkv, w_qkv, NT)
    grad_out_w = dot(mixed, grad_branch_all, TN)
    if natural:
        grad_out_w = scatter_dp(grad_out_w.astype(BF16)).astype(F32)
    else:
        spread = jnp.zeros((A, T, B, D), F32)
        spread = lax.dynamic_update_index_in_dim(spread, grad_out_w.reshape(A, B, D), me, 1)
        grad_out_w = lax.psum_scatter(spread.reshape(D, D), ("dp", "ctx"), scatter_dimension=0, tiled=True)
    grad_qkv_mine = scatter_dp(dot(normed_one, grad_qkv, TN).astype(BF16))
    got = exchange_ctx(grad_qkv_mine.reshape(T, r, 3 * L)).reshape(T, r, 3, A, B)
    grad_q, grad_k, grad_v = (
        got[:, :, i].transpose(1, 2, 0, 3).reshape(r, D).astype(F32) for i in range(3)
    )
    standard_in, factor_in = standardize(inputs)
    grad_in = (grad_middle + norm_back(grad_normed_one, gain_one, standard_in, factor_in)).astype(BF16)[None]

    partial_one = dot(grad_qkv, w_qkv, NT)
    grad_gain_one = jnp.sum(partial_one * standard_one, axis=0)
    grad_bias_one = jnp.sum(partial_one, axis=0)
    grad_gain_two = jnp.sum(grad_normed_two * standard_two, axis=0)
    grad_bias_two = jnp.sum(grad_normed_two, axis=0)
    ctx_index = lax.broadcasted_iota(jnp.int32, (1, T, 1), 1)
    spread_heads = lambda v: jnp.where(ctx_index == me, v.reshape(A, 1, B), 0.0).reshape(D)
    grad_bias_qkv = jnp.sum(grad_qkv.astype(F32), axis=0)
    grad_out_sum = jnp.sum(grad_branch.astype(F32), axis=0)
    grad_down_sum = jnp.sum((active_own * grad_res), axis=0)
    grad_up_sum = jnp.sum(grad_pre.astype(F32), axis=0)
    features = jnp.stack(
        [
            grad_gain_one,
            grad_bias_one,
            spread_heads(grad_bias_qkv[:L]),
            spread_heads(grad_bias_qkv[2 * L :]),
            grad_out_sum,
            grad_gain_two,
            grad_bias_two,
            grad_down_sum,
        ]
    )
    features = features.reshape(8, N, T, r).transpose(2, 1, 0, 3).reshape(T, N, 8 * r)
    units = jnp.where(
        lax.broadcasted_iota(jnp.int32, (T, 1, 1), 0) == me, grad_up_sum.reshape(1, N, f), 0.0
    )
    sums = jnp.concatenate([features, units], axis=2).reshape(T, N * (8 * r + f))
    sums = reduce_dp_small(reduce_ctx_small(sums).reshape(N, 8 * r + f))
    shard = lambda i: sums[i * r : (i + 1) * r]
    return (
        layer_out,
        grad_in,
        shard(0),
        shard(1),
        grad_q,
        shard(2),
        grad_k,
        grad_v,
        shard(3),
        grad_out_w,
        shard(4),
        shard(5),
        shard(6),
        grad_up,
        sums[8 * r :],
        grad_down,
        shard(7),
    )


def solution(mesh):
    rows = P("dp", "ctx", None)
    flags = P("dp", "ctx")
    vector = P(("dp", "ctx"))
    matrix = P(("dp", "ctx"), None)
    in_specs = (
        rows, flags, P(), flags, rows, vector, vector, matrix, vector, matrix,
        matrix, vector, matrix, vector, vector, vector, matrix, vector, matrix, vector,
    )
    out_specs = (
        rows, rows, vector, vector, matrix, vector, matrix, matrix, vector, matrix,
        vector, vector, vector, matrix, vector, matrix, vector,
    )
    return jax.shard_map(local, mesh=mesh, in_specs=in_specs, out_specs=out_specs, check_vma=False)
```

time: 3480 us -> 768 us (0.22)
  waiting for transfers between devices: 2940 us -> 343 us
  starting transfers between devices: 0.98 us -> 156 us
  matrix products: 214 us -> 96 us
  blocking collectives: 91.5 us -> 0 us
    reduce_scatter x6 -> x4, waiting for transfers between devices: 2160 us -> 30.6 us  [scatter_dp(): return lax.psum_scatter(value, 'dp', scatter_dimension=0, tiled=True)]
    all_gather x7 -> x4, waiting for transfers between devices: 622 us -> 0.03 us  [gather_dp(): return lax.all_gather(value, 'dp', axis=0, tiled=True)]
    ppermute x0 -> x77, waiting for transfers between devices: none -> 312 us  [the longest x42 303 us: turn(): lax.ppermute(value, 'ctx', [(2 * s + core, 2 * ((s + k) % count) + core)...]
    unnamed x17 -> x8, waiting for transfers between devices: 159 us -> 0.13 us
    ppermute x0 -> x77, starting transfers between devices: none -> 155 us  [the longest x42 143 us: turn(): lax.ppermute(value, 'ctx', [(2 * s + core, 2 * ((s + k) % count) + core)...]
    dot_general x25 -> x17, matrix products: 214 us -> 96 us  [dot(): return lax.dot_general(left, right, dims, preferred_element_type=F32)]
    unnamed x95 -> x111, local copies, waits for them, and re-layouts: 100 us -> 16.9 us
    all_gather x2 -> x0, blocking collectives: 48.5 us -> none  [the longest x1 39.2 us: local(): lax.all_gather(up_bias, ('dp', 'ctx'), axis=0, tiled=True)]
  transfers between devices with their start and end apart: 15 -> 85, of which waited for: 15 -> 28; matrix products, arithmetic and copies ran while one was open for 6% -> 23% of each run, Pallas kernels for 0% -> 2%
where the time goes in v1:
time: 768 us; the launch traced here: 758 us
  waiting for transfers between devices  343 us (45%)
  starting transfers between devices  156 us (20%)
  matrix products  96 us (12%)
  local copies, waits for them, and re-layouts  88.9 us (12%)
  other arithmetic  43.9 us (6%)
  between operations  17.2 us (2%)
  Pallas kernels  13.2 us (2%)
    ppermute x42, waiting for transfers between devices, turn(): lax.ppermute(value, 'ctx', [(2 * s + core, 2 * ((s + k) % count) + core)...  303 us
    ppermute x42, starting transfers between devices, turn(): lax.ppermute(value, 'ctx', [(2 * s + core, 2 * ((s + k) % count) + core)...  143 us
    dot_general x17, matrix products, dot(): return lax.dot_general(left, right, dims, preferred_element_type=F32)  96 us
    reduce_scatter x4, waiting for transfers between devices, scatter_dp(): return lax.psum_scatter(value, 'dp', scatter_dimension=0, tiled=True)  30.6 us
    unnamed x111, local copies, waits for them, and re-layouts  16.9 us
  transfers between devices with their start and end apart: 85, of which 28 were waited for; matrix products, arithmetic and copies ran while one was open for 23% of the time, Pallas kernels for 2%

profile of v1, /device:TPU:0, one launch (start us, length us, event | category | flops | bytes accessed | tf_op | source)
XLA Modules:
  0.0 757.5 jit_solution(2611024069944305190)
XLA Ops:
  23.1 11.3 %collective-permute-done.18 = bf16[2,64,768]{2,1,0:T(8,128)(2,1)S(1)} collective-permute-done((bf16[2,64,768]{2,1,0:T(8,128)(2,1)S(1)}, bf16[2,64,768]{2,1,0:T(8,128)(2,1)S(1)}, u32[]{:S(2)}, u32[]{:S(2)}) %collective-permute-start.18) | collective-permute-done | bytes 196640 | tf_op jit(solution)/shard_map/ppermute | solution.py:130
  50.2 17.9 %collective-permute-done.33 = bf16[2,64,1024]{2,1,0:T(8,128)(2,1)S(1)} collective-permute-done((bf16[2,64,1024]{2,1,0:T(8,128)(2,1)S(1)}, bf16[2,64,1024]{2,1,0:T(8,128)(2,1)S(1)}, u32[]{:S(2)}, u32[]{:S(2)}) %collective-permute-start.33) | collective-permute-done | bytes 262176 | tf_op jit(solution)/shard_map/ppermute | solution.py:130
  103.1 7.3 collective-permute-done.1
  110.9 21.9 %collective-permute-done.3 = bf16[128,2048]{1,0:T(8,128)(2,1)S(1)} collective-permute-done((bf16[128,2048]{1,0:T(8,128)(2,1)S(1)}, bf16[128,2048]{1,0:T(8,128)(2,1)S(1)}, u32[]{:S(2)}, u32[]{:S(2)}) %collective-permute-start.3) | collective-permute-done | bytes 524320 | tf_op jit(solution)/shard_map/ppermute | solution.py:130
  132.8 12.0 %collective-permute-start.45 = (bf16[128,2048]{1,0:T(8,128)(2,1)S(1)}, bf16[128,2048]{1,0:T(8,128)(2,1)}, u32[]{:S(2)}, u32[]{:S(2)}) collective-permute-start(bf16[128,2048]{1,0:T(8,128)(2,1)S(1)} %bitcast.333), channel_id=1, source_target_pairs={{0,6},{1,7},{2,0},{3,1},{4,2},{5,3},{6,4},{7,5},{8,14},{9,15},{10,... | collective-permute-start | bytes 1572872 | tf_op jit(solution)/shard_map/ppermute | solution.py:130
  148.1 29.3 %collective-permute-done.43 = bf16[128,2048]{1,0:T(8,128)(2,1)} collective-permute-done((bf16[128,2048]{1,0:T(8,128)(2,1)S(1)}, bf16[128,2048]{1,0:T(8,128)(2,1)}, u32[]{:S(2)}, u32[]{:S(2)}) %collective-permute-start.43) | collective-permute-done | bytes 524320 | tf_op jit(solution)/shard_map/ppermute | solution.py:130
  194.3 7.0 add_convert_fusion.1.refs_0_
  219.4 11.4 %collective-permute-start.22 = (bf16[128,2048]{1,0:T(8,128)(2,1)S(1)}, bf16[128,2048]{1,0:T(8,128)(2,1)S(1)}, u32[]{:S(2)}, u32[]{:S(2)}) collective-permute-start(bf16[128,2048]{1,0:T(8,128)(2,1)S(1)} %get-tuple-element.53), channel_id=1, source_target_pairs={{0,2},{1,3},{2,4},{3,5},{4,6},{5,7},{6,0},{7,1},{8,10},{9,11},{10,... | collective-permute-start | bytes 1572872 | tf_op jit(solution)/shard_map/ppermute | solution.py:130
  243.6 21.9 %collective-permute-done.23 = bf16[128,2048]{1,0:T(8,128)(2,1)S(1)} collective-permute-done((bf16[128,2048]{1,0:T(8,128)(2,1)S(1)}, bf16[128,2048]{1,0:T(8,128)(2,1)S(1)}, u32[]{:S(2)}, u32[]{:S(2)}) %collective-permute-start.23) | collective-permute-done | bytes 524320 | tf_op jit(solution)/shard_map/ppermute | solution.py:130
  270.1 11.8 %collective-permute-start.26 = (bf16[128,2048]{1,0:T(8,128)(2,1)S(1)}, bf16[128,2048]{1,0:T(8,128)(2,1)S(1)}, u32[]{:S(2)}, u32[]{:S(2)}) collective-permute-start(bf16[128,2048]{1,0:T(8,128)(2,1)S(1)} %get-tuple-element.39), channel_id=1, source_target_pairs={{0,2},{1,3},{2,4},{3,5},{4,6},{5,7},{6,0},{7,1},{8,10},{9,11},{10,... | collective-permute-start | bytes 1572872 | tf_op jit(solution)/shard_map/ppermute | solution.py:130
  284.7 8.5 %collective-permute-start.30 = (bf16[128,2048]{1,0:T(8,128)(2,1)S(1)}, bf16[128,2048]{1,0:T(8,128)(2,1)S(1)}, u32[]{:S(2)}, u32[]{:S(2)}) collective-permute-start(bf16[128,2048]{1,0:T(8,128)(2,1)S(1)} %get-tuple-element.39), channel_id=1, source_target_pairs={{0,6},{1,7},{2,0},{3,1},{4,2},{5,3},{6,4},{7,5},{8,14},{9,15},{10,... | collective-permute-start | bytes 1572872 | tf_op jit(solution)/shard_map/ppermute | solution.py:130
  297.6 21.6 %collective-permute-done.28 = bf16[128,2048]{1,0:T(8,128)(2,1)S(1)} collective-permute-done((bf16[128,2048]{1,0:T(8,128)(2,1)S(1)}, bf16[128,2048]{1,0:T(8,128)(2,1)S(1)}, u32[]{:S(2)}, u32[]{:S(2)}) %collective-permute-start.28) | collective-permute-done | bytes 524320 | tf_op jit(solution)/shard_map/ppermute | solution.py:130
  325.6 10.7 %fusion.8 = (bf16[1024,1024]{1,0:T(8,128)(2,1)S(1)}, f32[1024,1024]{1,0:T(8,128)}) fusion(f32[1024]{0:T(1024)S(1)} %bitcast.356, bf16[1024,2048]{1,0:T(8,128)(2,1)} %bitcast.45, bf16[2048,1024]{1,0:T(8,128)(2,1)} %all-gather.9.cloned.1.call-done), kind=kOutput, calls=%fused_computation.16 | convolution fusion | flops 4305453056 | bytes 14684160 | tf_op jit(solution)/shard_map/dot_general | solution.py:23
  338.9 11.4 %convert_reduce_fusion.1 = (f32[1024]{0:T(1024)S(1)}, bf16[1024,1024]{1,0:T(8,128)(2,1)S(1)}) fusion(f32[1024,1024]{1,0:T(8,128)} %get-tuple-element.137, f32[1024]{0:T(1024)S(1)} %bitcast.357, bf16[1024,2048]{1,0:T(8,128)(2,1)} %bitcast_multiply_fusion, bf16[1024,2048]{1,0:T(8,128)(2,1)} %all-gather.11.cloned.1.call-done), kind=kOutput, calls=%fused_computation.25 | convolution fusion | flops 4318034944 | bytes 14688256 | tf_op jit(solution)/shard_map/dot_general | solution.py:23
  371.1 11.3 %collective-permute-start.48 = (bf16[128,2048]{1,0:T(8,128)(2,1)S(1)}, bf16[128,2048]{1,0:T(8,128)(2,1)S(1)}, u32[]{:S(2)}, u32[]{:S(2)}) collective-permute-start(bf16[128,2048]{1,0:T(8,128)(2,1)S(1)} %get-tuple-element.47), channel_id=1, source_target_pairs={{0,2},{1,3},{2,4},{3,5},{4,6},{5,7},{6,0},{7,1},{8,10},{9,11},{10,... | collective-permute-start | bytes 1572872 | tf_op jit(solution)/shard_map/ppermute | solution.py:130
  397.4 20.5 %collective-permute-done.49 = bf16[128,2048]{1,0:T(8,128)(2,1)S(1)} collective-permute-done((bf16[128,2048]{1,0:T(8,128)(2,1)S(1)}, bf16[128,2048]{1,0:T(8,128)(2,1)S(1)}, u32[]{:S(2)}, u32[]{:S(2)}) %collective-permute-start.49) | collective-permute-done | bytes 524320 | tf_op jit(solution)/shard_map/ppermute | solution.py:130
  419.7 9.4 %collective-permute-done.37 = bf16[128,2048]{1,0:T(8,128)(2,1)S(1)} collective-permute-done((bf16[128,2048]{1,0:T(8,128)(2,1)S(1)}, bf16[128,2048]{1,0:T(8,128)(2,1)S(1)}, u32[]{:S(2)}, u32[]{:S(2)}) %collective-permute-start.37) | collective-permute-done | bytes 524320 | tf_op jit(solution)/shard_map/ppermute | solution.py:130
  429.1 33.1 %collective-permute-done.38 = bf16[128,2048]{1,0:T(8,128)(2,1)S(1)} collective-permute-done((bf16[128,2048]{1,0:T(8,128)(2,1)S(1)}, bf16[128,2048]{1,0:T(8,128)(2,1)S(1)}, u32[]{:S(2)}, u32[]{:S(2)}) %collective-permute-start.38) | collective-permute-done | bytes 524320 | tf_op jit(solution)/shard_map/ppermute | solution.py:130
  465.5 11.7 %collective-permute-start.52 = (bf16[128,2048]{1,0:T(8,128)(2,1)S(1)}, bf16[128,2048]{1,0:T(8,128)(2,1)S(1)}, u32[]{:S(2)}, u32[]{:S(2)}) collective-permute-start(bf16[128,2048]{1,0:T(8,128)(2,1)S(1)} %get-tuple-element.34), channel_id=1, source_target_pairs={{0,2},{1,3},{2,4},{3,5},{4,6},{5,7},{6,0},{7,1},{8,10},{9,11},{10,... | collective-permute-start | bytes 1572872 | tf_op jit(solution)/shard_map/ppermute | solution.py:130
  480.9 11.2 %collective-permute-done.52 = bf16[128,2048]{1,0:T(8,128)(2,1)S(1)} collective-permute-done((bf16[128,2048]{1,0:T(8,128)(2,1)S(1)}, bf16[128,2048]{1,0:T(8,128)(2,1)S(1)}, u32[]{:S(2)}, u32[]{:S(2)}) %collective-permute-start.52) | collective-permute-done | bytes 524320 | tf_op jit(solution)/shard_map/ppermute | solution.py:130
  492.2 21.7 %collective-permute-done.54 = bf16[128,2048]{1,0:T(8,128)(2,1)S(1)} collective-permute-done((bf16[128,2048]{1,0:T(8,128)(2,1)S(1)}, bf16[128,2048]{1,0:T(8,128)(2,1)S(1)}, u32[]{:S(2)}, u32[]{:S(2)}) %collective-permute-start.54) | collective-permute-done | bytes 524320 | tf_op jit(solution)/shard_map/ppermute | solution.py:130
  521.0 9.5 %convolution_convert_fusion.1 = bf16[2048,1024]{1,0:T(8,128)(2,1)} fusion(bf16[1024,2048]{1,0:T(8,128)(2,1)} %bitcast.45, bf16[1024,1024]{1,0:T(8,128)(2,1)} %copy-done.11), kind=kOutput, calls=%fused_computation.27 | convolution fusion | flops 4297064448 | bytes 10485760 | tf_op jit(solution)/shard_map/dot_general | solution.py:23
  530.5 9.4 %convolution_convert_fusion = bf16[1024,2048]{1,0:T(8,128)(2,1)} fusion(bf16[1024,1024]{1,0:T(8,128)(2,1)} %copy-done.10, bf16[1024,2048]{1,0:T(8,128)(2,1)} %bitcast_multiply_fusion), kind=kOutput, calls=%fused_computation.26 | convolution fusion | flops 4297064448 | bytes 10485760 | tf_op jit(solution)/shard_map/dot_general | solution.py:23
  548.7 8.0 %attention_backward.1 = bf16[1024,768]{1,0:T(8,128)(2,1)S(1)} custom-call(bf16[1024,768]{1,0:T(8,128)(2,1)S(1)} %copy-done.1, bf16[1024,256]{1,0:T(8,128)(2,1)S(1)} %get-tuple-element.139.refs_1_, f32[4,1024]{1,0:T(4,128)S(1)} %get-tuple-element.20.refs_2_, f32[4,1024]{1,0:T(4,128)S(1)} %bitcast.314, s32[1024,1]{1,0:T(8,128)S(1)} %copy.50.refs_1_.refs_4_, ...), custom_call_target="tpu_custom_call" | custom-call | flops 5368709120 | bytes 3670016 | tf_op jit(solution)/shard_map/attention_backward/pallas_call | solution.py:114
  558.0 7.7 %convolution_convert_fusion.2 = bf16[2048,768]{1,0:T(8,128)(2,1)} fusion(bf16[1024,2048]{1,0:T(8,128)(2,1)} %add_convert_fusion, bf16[1024,768]{1,0:T(8,128)(2,1)S(1)} %attention_backward.1), kind=kOutput, calls=%fused_computation.28 | convolution fusion | flops 3222798336 | bytes 8912896 | tf_op jit(solution)/shard_map/dot_general | solution.py:23
  580.8 10.8 %collective-permute-start.63 = (f32[3072]{0:T(1024)S(1)}, f32[3072]{0:T(1024)S(1)}, u32[]{:S(2)}, u32[]{:S(2)}) collective-permute-start(f32[3072]{0:T(1024)S(1)} %bitcast.354), channel_id=1, source_target_pairs={{0,2},{1,3},{2,4},{3,5},{4,6},{5,7},{6,0},{7,1},{8,10},{9,11},{10,... | collective-permute-start | bytes 36872 | tf_op jit(solution)/shard_map/ppermute | solution.py:130
  614.8 9.9 %collective-permute-done.59 = bf16[128,2048]{1,0:T(8,128)(2,1)S(1)} collective-permute-done((bf16[128,2048]{1,0:T(8,128)(2,1)}, bf16[128,2048]{1,0:T(8,128)(2,1)S(1)}, u32[]{:S(2)}, u32[]{:S(2)}) %collective-permute-start.59) | collective-permute-done | bytes 524320 | tf_op jit(solution)/shard_map/ppermute | solution.py:130
  624.7 20.3 %collective-permute-done.60 = bf16[128,2048]{1,0:T(8,128)(2,1)} collective-permute-done((bf16[128,2048]{1,0:T(8,128)(2,1)}, bf16[128,2048]{1,0:T(8,128)(2,1)}, u32[]{:S(2)}, u32[]{:S(2)}) %collective-permute-start.60) | collective-permute-done | bytes 524320 | tf_op jit(solution)/shard_map/ppermute | solution.py:130
  648.6 11.2 %collective-permute-start.74 = (bf16[2,64,1024]{2,1,0:T(8,128)(2,1)S(1)}, bf16[2,64,1024]{2,1,0:T(8,128)(2,1)S(1)}, u32[]{:S(2)}, u32[]{:S(2)}) collective-permute-start(bf16[2,64,1024]{2,1,0:T(8,128)(2,1)S(1)} %get-tuple-element.86), channel_id=1, source_target_pairs={{0,4},{1,5},{2,6},{3,7},{4,0},{5,1},{6,2},{7,3},{8,12},{9,13},{10,... | collective-permute-start | bytes 786440 | tf_op jit(solution)/shard_map/ppermute | solution.py:130
  664.6 13.6 %collective-permute-done.74 = bf16[2,64,1024]{2,1,0:T(8,128)(2,1)S(1)} collective-permute-done((bf16[2,64,1024]{2,1,0:T(8,128)(2,1)S(1)}, bf16[2,64,1024]{2,1,0:T(8,128)(2,1)S(1)}, u32[]{:S(2)}, u32[]{:S(2)}) %collective-permute-start.74) | collective-permute-done | bytes 262176 | tf_op jit(solution)/shard_map/ppermute | solution.py:130
  685.0 30.6 %reduce-scatter.5.cloned.1.call-done = bf16[512,768]{1,0:T(8,128)(2,1)} async-done(((bf16[2048,768]{1,0:T(8,128)(2,1)}), bf16[512,768]{1,0:T(8,128)(2,1)}) %reduce-scatter.5.cloned.1.call-update) | async-done | bytes 786448 | tf_op jit(solution)/shard_map/reduce_scatter | solution.py:237
  724.3 9.6 %collective-permute-done.70 = bf16[2,64,768]{2,1,0:T(8,128)(2,1)S(1)} collective-permute-done((bf16[2,64,768]{2,1,0:T(8,128)(2,1)S(1)}, bf16[2,64,768]{2,1,0:T(8,128)(2,1)S(1)}, u32[]{:S(2)}, u32[]{:S(2)}) %collective-permute-start.70) | collective-permute-done | bytes 196640 | tf_op jit(solution)/shard_map/ppermute | solution.py:130
  (503 shorter events, 276.7 us)
Async XLA Ops:
  7.2 187.1 %all-gather.5.cloned.1.call-start = ((), (), s32[]{:S(2)}) async-start(), calls=%async_computation.4 | async-start | bytes 3932160 | tf_op jit(solution)/shard_map/all_gather | solution.py:233
  38.9 168.9 %all-gather.7.cloned.1.call-start = ((), (), s32[]{:S(2)}) async-start(), calls=%async_computation.5 | async-start | bytes 1310720 | tf_op jit(solution)/shard_map/all_gather | solution.py:233
  69.7 255.9 %all-gather.9.cloned.1.call-start = ((), (), s32[]{:S(2)}) async-start(), calls=%async_computation.6 | async-start | bytes 5242880 | tf_op jit(solution)/shard_map/all_gather | solution.py:233
  74.8 264.1 %all-gather.11.cloned.1.call-start = ((), (), s32[]{:S(2)}) async-start(), calls=%async_computation.7 | async-start | bytes 5242880 | tf_op jit(solution)/shard_map/all_gather | solution.py:233
  79.5 533.5 %reduce-scatter.7.cloned.1.call-start = ((), (), s32[]{:S(2)}) async-start(), calls=%async_computation.9 | async-start | bytes 1310720 | tf_op jit(solution)/shard_map/reduce_scatter | solution.py:237
  96.2 36.6 %collective-permute-start.3 = (bf16[128,2048]{1,0:T(8,128)(2,1)S(1)}, bf16[128,2048]{1,0:T(8,128)(2,1)S(1)}, u32[]{:S(2)}, u32[]{:S(2)}) collective-permute-start(bf16[128,2048]{1,0:T(8,128)(2,1)S(1)} %bitcast.320), channel_id=1, source_target_pairs={{0,4},{1,5},{2,6},{3,7},{4,0},{5,1},{6,2},{7,3},{8,12},{9,13},{10,... | collective-permute-start | bytes 1572872 | tf_op jit(solution)/shard_map/ppermute | solution.py:130
  98.5 49.1 %collective-permute-start.5 = (bf16[128,2048]{1,0:T(8,128)(2,1)S(1)}, bf16[128,2048]{1,0:T(8,128)(2,1)}, u32[]{:S(2)}, u32[]{:S(2)}) collective-permute-start(bf16[128,2048]{1,0:T(8,128)(2,1)S(1)} %bitcast.321), channel_id=1, source_target_pairs={{0,6},{1,7},{2,0},{3,1},{4,2},{5,3},{6,4},{7,5},{8,14},{9,15},{10,... | collective-permute-start | bytes 1572872 | tf_op jit(solution)/shard_map/ppermute | solution.py:130
  99.5 45.3 %collective-permute-start.40 = (bf16[128,2048]{1,0:T(8,128)(2,1)S(1)}, bf16[128,2048]{1,0:T(8,128)(2,1)}, u32[]{:S(2)}, u32[]{:S(2)}) collective-permute-start(bf16[128,2048]{1,0:T(8,128)(2,1)S(1)} %bitcast.330), channel_id=1, source_target_pairs={{0,1},{1,0},{2,3},{3,2},{4,5},{5,4},{6,7},{7,6},{8,9},{9,8},{10,11... | collective-permute-start | bytes 1572872 | tf_op jit(solution)/shard_map/ppermute | solution.py:136
  100.8 47.3 %collective-permute-start.41 = (bf16[128,2048]{1,0:T(8,128)(2,1)S(1)}, bf16[128,2048]{1,0:T(8,128)(2,1)}, u32[]{:S(2)}, u32[]{:S(2)}) collective-permute-start(bf16[128,2048]{1,0:T(8,128)(2,1)S(1)} %bitcast.331), channel_id=1, source_target_pairs={{0,2},{1,3},{2,4},{3,5},{4,6},{5,7},{6,0},{7,1},{8,10},{9,11},{10,... | collective-permute-start | bytes 1572872 | tf_op jit(solution)/shard_map/ppermute | solution.py:130
  110.4 67.1 %collective-permute-start.43 = (bf16[128,2048]{1,0:T(8,128)(2,1)S(1)}, bf16[128,2048]{1,0:T(8,128)(2,1)}, u32[]{:S(2)}, u32[]{:S(2)}) collective-permute-start(bf16[128,2048]{1,0:T(8,128)(2,1)S(1)} %bitcast.332), channel_id=1, source_target_pairs={{0,4},{1,5},{2,6},{3,7},{4,0},{5,1},{6,2},{7,3},{8,12},{9,13},{10,... | collective-permute-start | bytes 1572872 | tf_op jit(solution)/shard_map/ppermute | solution.py:130
  132.8 44.6 %collective-permute-start.45 = (bf16[128,2048]{1,0:T(8,128)(2,1)S(1)}, bf16[128,2048]{1,0:T(8,128)(2,1)}, u32[]{:S(2)}, u32[]{:S(2)}) collective-permute-start(bf16[128,2048]{1,0:T(8,128)(2,1)S(1)} %bitcast.333), channel_id=1, source_target_pairs={{0,6},{1,7},{2,0},{3,1},{4,2},{5,3},{6,4},{7,5},{8,14},{9,15},{10,... | collective-permute-start | bytes 1572872 | tf_op jit(solution)/shard_map/ppermute | solution.py:130
  148.1 34.5 %collective-permute-start.6 = (bf16[128,2048]{1,0:T(8,128)(2,1)}, bf16[128,2048]{1,0:T(8,128)(2,1)S(1)}, u32[]{:S(2)}, u32[]{:S(2)}) collective-permute-start(bf16[128,2048]{1,0:T(8,128)(2,1)} %collective-permute-done.5), channel_id=1, source_target_pairs={{0,1},{1,0},{2,3},{3,2},{4,5},{5,4},{6,7},{7,6},{8,9},{9,8},{10,11... | collective-permute-start | bytes 1572872 | tf_op jit(solution)/shard_map/ppermute | solution.py:136
  177.5 35.0 %collective-permute-start.42 = (bf16[128,2048]{1,0:T(8,128)(2,1)}, bf16[128,2048]{1,0:T(8,128)(2,1)}, u32[]{:S(2)}, u32[]{:S(2)}) collective-permute-start(bf16[128,2048]{1,0:T(8,128)(2,1)} %collective-permute-done.41), channel_id=1, source_target_pairs={{0,1},{1,0},{2,3},{3,2},{4,5},{5,4},{6,7},{7,6},{8,9},{9,8},{10,11... | collective-permute-start | bytes 1572872 | tf_op jit(solution)/shard_map/ppermute | solution.py:136
  177.5 38.8 %collective-permute-start.44 = (bf16[128,2048]{1,0:T(8,128)(2,1)}, bf16[128,2048]{1,0:T(8,128)(2,1)}, u32[]{:S(2)}, u32[]{:S(2)}) collective-permute-start(bf16[128,2048]{1,0:T(8,128)(2,1)} %collective-permute-done.43), channel_id=1, source_target_pairs={{0,1},{1,0},{2,3},{3,2},{4,5},{5,4},{6,7},{7,6},{8,9},{9,8},{10,11... | collective-permute-start | bytes 1572872 | tf_op jit(solution)/shard_map/ppermute | solution.py:136
  178.0 57.2 %collective-permute-start.46 = (bf16[128,2048]{1,0:T(8,128)(2,1)}, bf16[128,2048]{1,0:T(8,128)(2,1)}, u32[]{:S(2)}, u32[]{:S(2)}) collective-permute-start(bf16[128,2048]{1,0:T(8,128)(2,1)} %collective-permute-done.45), channel_id=1, source_target_pairs={{0,1},{1,0},{2,3},{3,2},{4,5},{5,4},{6,7},{7,6},{8,9},{9,8},{10,11... | collective-permute-start | bytes 1572872 | tf_op jit(solution)/shard_map/ppermute | solution.py:136
  230.8 34.7 %collective-permute-start.23 = (bf16[128,2048]{1,0:T(8,128)(2,1)S(1)}, bf16[128,2048]{1,0:T(8,128)(2,1)S(1)}, u32[]{:S(2)}, u32[]{:S(2)}) collective-permute-start(bf16[128,2048]{1,0:T(8,128)(2,1)S(1)} %get-tuple-element.55), channel_id=1, source_target_pairs={{0,4},{1,5},{2,6},{3,7},{4,0},{5,1},{6,2},{7,3},{8,12},{9,13},{10,... | collective-permute-start | bytes 1572872 | tf_op jit(solution)/shard_map/ppermute | solution.py:130
  231.3 34.2 %collective-permute-start.24 = (bf16[128,2048]{1,0:T(8,128)(2,1)S(1)}, bf16[128,2048]{1,0:T(8,128)(2,1)S(1)}, u32[]{:S(2)}, u32[]{:S(2)}) collective-permute-start(bf16[128,2048]{1,0:T(8,128)(2,1)S(1)} %get-tuple-element.54), channel_id=1, source_target_pairs={{0,6},{1,7},{2,0},{3,1},{4,2},{5,3},{6,4},{7,5},{8,14},{9,15},{10,... | collective-permute-start | bytes 1572872 | tf_op jit(solution)/shard_map/ppermute | solution.py:130
  270.1 49.6 %collective-permute-start.25 = (bf16[128,2048]{1,0:T(8,128)(2,1)S(1)}, bf16[128,2048]{1,0:T(8,128)(2,1)S(1)}, u32[]{:S(2)}, u32[]{:S(2)}) collective-permute-start(bf16[128,2048]{1,0:T(8,128)(2,1)S(1)} %get-tuple-element.39), channel_id=1, source_target_pairs={{0,1},{1,0},{2,3},{3,2},{4,5},{5,4},{6,7},{7,6},{8,9},{9,8},{10,11... | collective-permute-start | bytes 1572872 | tf_op jit(solution)/shard_map/ppermute | solution.py:136
  281.9 37.3 %collective-permute-start.28 = (bf16[128,2048]{1,0:T(8,128)(2,1)S(1)}, bf16[128,2048]{1,0:T(8,128)(2,1)S(1)}, u32[]{:S(2)}, u32[]{:S(2)}) collective-permute-start(bf16[128,2048]{1,0:T(8,128)(2,1)S(1)} %get-tuple-element.39), channel_id=1, source_target_pairs={{0,4},{1,5},{2,6},{3,7},{4,0},{5,1},{6,2},{7,3},{8,12},{9,13},{10,... | collective-permute-start | bytes 1572872 | tf_op jit(solution)/shard_map/ppermute | solution.py:130
  284.7 34.6 %collective-permute-start.30 = (bf16[128,2048]{1,0:T(8,128)(2,1)S(1)}, bf16[128,2048]{1,0:T(8,128)(2,1)S(1)}, u32[]{:S(2)}, u32[]{:S(2)}) collective-permute-start(bf16[128,2048]{1,0:T(8,128)(2,1)S(1)} %get-tuple-element.39), channel_id=1, source_target_pairs={{0,6},{1,7},{2,0},{3,1},{4,2},{5,3},{6,4},{7,5},{8,14},{9,15},{10,... | collective-permute-start | bytes 1572872 | tf_op jit(solution)/shard_map/ppermute | solution.py:130
  382.5 35.4 %collective-permute-start.49 = (bf16[128,2048]{1,0:T(8,128)(2,1)S(1)}, bf16[128,2048]{1,0:T(8,128)(2,1)S(1)}, u32[]{:S(2)}, u32[]{:S(2)}) collective-permute-start(bf16[128,2048]{1,0:T(8,128)(2,1)S(1)} %get-tuple-element.49), channel_id=1, source_target_pairs={{0,4},{1,5},{2,6},{3,7},{4,0},{5,1},{6,2},{7,3},{8,12},{9,13},{10,... | collective-permute-start | bytes 1572872 | tf_op jit(solution)/shard_map/ppermute | solution.py:130
  383.0 34.8 %collective-permute-start.50 = (bf16[128,2048]{1,0:T(8,128)(2,1)S(1)}, bf16[128,2048]{1,0:T(8,128)(2,1)S(1)}, u32[]{:S(2)}, u32[]{:S(2)}) collective-permute-start(bf16[128,2048]{1,0:T(8,128)(2,1)S(1)} %get-tuple-element.48), channel_id=1, source_target_pairs={{0,6},{1,7},{2,0},{3,1},{4,2},{5,3},{6,4},{7,5},{8,14},{9,15},{10,... | collective-permute-start | bytes 1572872 | tf_op jit(solution)/shard_map/ppermute | solution.py:130
  386.8 42.3 %collective-permute-start.37 = (bf16[128,2048]{1,0:T(8,128)(2,1)S(1)}, bf16[128,2048]{1,0:T(8,128)(2,1)S(1)}, u32[]{:S(2)}, u32[]{:S(2)}) collective-permute-start(bf16[128,2048]{1,0:T(8,128)(2,1)S(1)} %get-tuple-element.50), channel_id=1, source_target_pairs={{0,2},{1,3},{2,4},{3,5},{4,6},{5,7},{6,0},{7,1},{8,10},{9,11},{10,... | collective-permute-start | bytes 1572872 | tf_op jit(solution)/shard_map/ppermute | solution.py:130
  387.0 75.2 %collective-permute-start.38 = (bf16[128,2048]{1,0:T(8,128)(2,1)S(1)}, bf16[128,2048]{1,0:T(8,128)(2,1)S(1)}, u32[]{:S(2)}, u32[]{:S(2)}) collective-permute-start(bf16[128,2048]{1,0:T(8,128)(2,1)S(1)} %get-tuple-element.52), channel_id=1, source_target_pairs={{0,4},{1,5},{2,6},{3,7},{4,0},{5,1},{6,2},{7,3},{8,12},{9,13},{10,... | collective-permute-start | bytes 1572872 | tf_op jit(solution)/shard_map/ppermute | solution.py:130
  395.3 66.8 %collective-permute-start.39 = (bf16[128,2048]{1,0:T(8,128)(2,1)S(1)}, bf16[128,2048]{1,0:T(8,128)(2,1)S(1)}, u32[]{:S(2)}, u32[]{:S(2)}) collective-permute-start(bf16[128,2048]{1,0:T(8,128)(2,1)S(1)} %get-tuple-element.51), channel_id=1, source_target_pairs={{0,6},{1,7},{2,0},{3,1},{4,2},{5,3},{6,4},{7,5},{8,14},{9,15},{10,... | collective-permute-start | bytes 1572872 | tf_op jit(solution)/shard_map/ppermute | solution.py:130
  477.2 36.7 %collective-permute-start.54 = (bf16[128,2048]{1,0:T(8,128)(2,1)S(1)}, bf16[128,2048]{1,0:T(8,128)(2,1)S(1)}, u32[]{:S(2)}, u32[]{:S(2)}) collective-permute-start(bf16[128,2048]{1,0:T(8,128)(2,1)S(1)} %get-tuple-element.34), channel_id=1, source_target_pairs={{0,4},{1,5},{2,6},{3,7},{4,0},{5,1},{6,2},{7,3},{8,12},{9,13},{10,... | collective-permute-start | bytes 1572872 | tf_op jit(solution)/shard_map/ppermute | solution.py:130
  480.3 34.1 %collective-permute-start.51 = (bf16[128,2048]{1,0:T(8,128)(2,1)S(1)}, bf16[128,2048]{1,0:T(8,128)(2,1)S(1)}, u32[]{:S(2)}, u32[]{:S(2)}) collective-permute-start(bf16[128,2048]{1,0:T(8,128)(2,1)S(1)} %get-tuple-element.34), channel_id=1, source_target_pairs={{0,1},{1,0},{2,3},{3,2},{4,5},{5,4},{6,7},{7,6},{8,9},{9,8},{10,11... | collective-permute-start | bytes 1572872 | tf_op jit(solution)/shard_map/ppermute | solution.py:136
  520.9 126.5 %reduce-scatter.9.cloned.1.call-start = ((), (), s32[]{:S(2)}) async-start(), calls=%async_computation.10 | async-start | bytes 5242880 | tf_op jit(solution)/shard_map/reduce_scatter | solution.py:237
  530.5 150.5 %reduce-scatter.11.cloned.1.call-start = ((), (), s32[]{:S(2)}) async-start(), calls=%async_computation.11 | async-start | bytes 5242880 | tf_op jit(solution)/shard_map/reduce_scatter | solution.py:237
  540.0 175.7 %reduce-scatter.5.cloned.1.call-start = ((), (), s32[]{:S(2)}) async-start(), calls=%async_computation.8 | async-start | bytes 3932160 | tf_op jit(solution)/shard_map/reduce_scatter | solution.py:237
  609.3 35.7 %collective-permute-start.60 = (bf16[128,2048]{1,0:T(8,128)(2,1)}, bf16[128,2048]{1,0:T(8,128)(2,1)}, u32[]{:S(2)}, u32[]{:S(2)}) collective-permute-start(bf16[128,2048]{1,0:T(8,128)(2,1)} %get-tuple-element.46), channel_id=1, source_target_pairs={{0,4},{1,5},{2,6},{3,7},{4,0},{5,1},{6,2},{7,3},{8,12},{9,13},{10,... | collective-permute-start | bytes 1572872 | tf_op jit(solution)/shard_map/ppermute | solution.py:130
  610.3 34.7 %collective-permute-start.61 = (bf16[128,2048]{1,0:T(8,128)(2,1)}, bf16[128,2048]{1,0:T(8,128)(2,1)}, u32[]{:S(2)}, u32[]{:S(2)}) collective-permute-start(bf16[128,2048]{1,0:T(8,128)(2,1)} %get-tuple-element.45), channel_id=1, source_target_pairs={{0,6},{1,7},{2,0},{3,1},{4,2},{5,3},{6,4},{7,5},{8,14},{9,15},{10,... | collective-permute-start | bytes 1572872 | tf_op jit(solution)/shard_map/ppermute | solution.py:130
  (105 other events, 1372.1 us)
Sparse Core Ops, SparseCore 0:
  39.0 44.4 all-gather.4
  85.4 26.6 all-gather.6
  114.5 52.6 all-gather.8
  168.9 52.6 all-gather.10
  521.0 35.5 reduce-scatter.6
  559.8 52.8 reduce-scatter.8
  615.7 52.6 reduce-scatter.10
  671.6 43.9 reduce-scatter.4

commit v2 on v1

v2 whole, which is shorter than its diff:
```python
import jax
import jax.numpy as jnp
from jax import lax
from jax.experimental import pallas as pl
from jax.experimental.pallas import tpu as pltpu
from jax.sharding import PartitionSpec as P

HEADS = 32
HEAD_DIM = 64
EPSILON = 1e-05
NEG_FILL = -1e30
SCALE = HEAD_DIM ** (-0.5)
QUERY_BLOCK = 256
BF16 = jnp.bfloat16
F32 = jnp.float32

NN = (((1,), (0,)), ((), ()))
NT = (((1,), (1,)), ((), ()))
TN = (((0,), (0,)), ((), ()))
ANYWHERE = pl.BlockSpec(memory_space=pl.ANY)


def dot(left, right, dims=NN):
    return lax.dot_general(left, right, dims, preferred_element_type=F32)


def forward_kernel(*refs, heads, lanes, block):
    qkv_ref, seg_col_ref, seg_row_ref = refs[:3]
    mixed_ref, log_ref = refs[-2:]
    rows = qkv_ref.shape[0]
    head_of_lane = lax.broadcasted_iota(jnp.int32, (1, lanes), 1) // HEAD_DIM
    diagonal = lax.broadcasted_iota(jnp.int32, (block, block), 1) <= lax.broadcasted_iota(
        jnp.int32, (block, block), 0
    )
    for b in range(rows // block):
        low, high = b * block, (b + 1) * block
        queries = qkv_ref[low:high, :lanes] * jnp.asarray(SCALE, BF16)
        keys = qkv_ref[:high, lanes : 2 * lanes]
        values = qkv_ref[:high, 2 * lanes :]
        allowed = seg_col_ref[low:high, :] == seg_row_ref[:, :high]
        last = allowed[:, low:] & diagonal
        allowed = jnp.concatenate([allowed[:, :low], last], axis=1) if b else last
        mixed = jnp.zeros((block, lanes), F32)
        for h in range(heads):
            mine = head_of_lane == h
            scores = dot(jnp.where(mine, queries, jnp.zeros_like(queries)), keys, NT)
            scores = jnp.where(allowed, scores, NEG_FILL)
            top = jnp.max(scores, axis=1, keepdims=True)
            weights = jnp.exp(scores - top)
            total = jnp.sum(weights, axis=1, keepdims=True)
            product = dot(weights.astype(BF16), values)
            mixed = mixed + jnp.where(mine, product / total, 0.0)
            log_total = jnp.broadcast_to(top + jnp.log(total), (block, 128))
            log_ref[h : h + 1, low:high] = jnp.transpose(log_total)[:1, :]
        mixed_ref[low:high, :] = mixed.astype(BF16)


def backward_kernel(*refs, heads, lanes, block):
    qkv_ref, grad_ref, log_ref, mixed_ref, seg_col_ref, seg_row_ref = refs[:6]
    out_ref, dk_ref, dv_ref = refs[-3:]
    rows = qkv_ref.shape[0]
    head_of_lane = lax.broadcasted_iota(jnp.int32, (1, lanes), 1) // HEAD_DIM
    diagonal = lax.broadcasted_iota(jnp.int32, (block, block), 0) <= lax.broadcasted_iota(
        jnp.int32, (block, block), 1
    )
    scale = jnp.asarray(SCALE, BF16)
    head_rows = jnp.where(lax.broadcasted_iota(jnp.int32, (16, lanes), 0) == head_of_lane, 1.0, 0.0).astype(BF16)
    for b in range(rows // block):
        low, high = b * block, (b + 1) * block
        queries = qkv_ref[low:high, :lanes] * scale
        grads = grad_ref[low:high, :]
        keys = qkv_ref[:high, lanes : 2 * lanes]
        values = qkv_ref[:high, 2 * lanes :]
        allowed = seg_col_ref[:high, :] == seg_row_ref[:, low:high]
        last = allowed[low:, :] & diagonal
        allowed = jnp.concatenate([allowed[:low, :], last], axis=0) if b else last
        products = grads.astype(F32) * mixed_ref[low:high, :].astype(F32)
        coarse = products.astype(BF16)
        fine = (products - coarse.astype(F32)).astype(BF16)
        delta = dot(head_rows, coarse, NT) + dot(head_rows, fine, NT)
        grad_queries = jnp.zeros((block, lanes), F32)
        grad_keys = jnp.zeros((high, lanes), F32)
        grad_values = jnp.zeros((high, lanes), F32)
        for h in range(heads):
            mine = head_of_lane == h
            query_h = jnp.where(mine, queries, jnp.zeros_like(queries))
            grad_h = jnp.where(mine, grads, jnp.zeros_like(grads))
            scores = dot(keys, query_h, NT)
            probs = jnp.where(allowed, jnp.exp(scores - log_ref[h : h + 1, low:high]), 0.0)
            grad_probs = dot(values, grad_h, NT)
            grad_scores = (probs * (grad_probs - delta[h : h + 1, :])).astype(BF16)
            grad_values = grad_values + dot(probs.astype(BF16), grad_h)
            grad_keys = grad_keys + dot(grad_scores, query_h)
            grad_queries = grad_queries + jnp.where(mine, dot(grad_scores, keys, TN), 0.0)
        out_ref[low:high, :lanes] = (grad_queries * SCALE).astype(BF16)
        if b:
            dk_ref[:low, :] = dk_ref[:low, :] + grad_keys[:low, :]
            dv_ref[:low, :] = dv_ref[:low, :] + grad_values[:low, :]
        dk_ref[low:high, :] = grad_keys[low:, :]
        dv_ref[low:high, :] = grad_values[low:, :]
    out_ref[:, lanes : 2 * lanes] = dk_ref[...].astype(BF16)
    out_ref[:, 2 * lanes :] = dv_ref[...].astype(BF16)


def attention_forward(qkv, seg_col, seg_row, earlier):
    rows, lanes = qkv.shape[0], qkv.shape[1] // 3
    heads = lanes // HEAD_DIM
    pairs = rows * rows * heads // 2
    return pl.pallas_call(
        lambda *refs: forward_kernel(*refs, heads=heads, lanes=lanes, block=QUERY_BLOCK),
        out_shape=(jax.ShapeDtypeStruct((rows, lanes), BF16), jax.ShapeDtypeStruct((heads, rows), F32)),
        compiler_params=pltpu.CompilerParams(vmem_limit_bytes=48 * 2**20),
        cost_estimate=pl.CostEstimate(flops=pairs * 5000, bytes_accessed=8 * rows * lanes, transcendentals=pairs),
        in_specs=[pl.BlockSpec(memory_space=pltpu.VMEM)] * 3 + [ANYWHERE] * len(earlier),
        name="attention_forward",
    )(qkv, seg_col, seg_row, *earlier)


def attention_backward(qkv, grads, log_total, mixed, seg_col, seg_row, earlier):
    rows, lanes = qkv.shape[0], qkv.shape[1] // 3
    heads = lanes // HEAD_DIM
    pairs = rows * rows * heads // 2
    return pl.pallas_call(
        lambda *refs: backward_kernel(*refs, heads=heads, lanes=lanes, block=QUERY_BLOCK),
        out_shape=jax.ShapeDtypeStruct((rows, 3 * lanes), BF16),
        scratch_shapes=[pltpu.VMEM((rows, lanes), F32), pltpu.VMEM((rows, lanes), F32)],
        compiler_params=pltpu.CompilerParams(vmem_limit_bytes=48 * 2**20),
        cost_estimate=pl.CostEstimate(flops=pairs * 5000, bytes_accessed=14 * rows * lanes, transcendentals=pairs),
        in_specs=[pl.BlockSpec(memory_space=pltpu.VMEM)] * 6 + [ANYWHERE] * len(earlier),
        name="attention_backward",
    )(qkv, grads, log_total, mixed, seg_col, seg_row, *earlier)


def chips():
    return lax.axis_size("ctx") // 2


def turn(value, k):
    count = chips()
    return lax.ppermute(
        value, "ctx", [(2 * s + core, 2 * ((s + k) % count) + core) for s in range(count) for core in range(2)]
    )


def swap(value):
    return lax.ppermute(value, "ctx", [(i, i ^ 1) for i in range(2 * chips())])


def place():
    me = lax.axis_index("ctx")
    return me // 2, me % 2


def after(value, *earlier, cost=0):
    def nothing(*refs):
        pass

    return pl.pallas_call(
        nothing,
        out_shape=jax.ShapeDtypeStruct(value.shape, value.dtype),
        in_specs=[ANYWHERE] * (1 + len(earlier)),
        out_specs=ANYWHERE,
        input_output_aliases={0: 0},
        cost_estimate=pl.CostEstimate(flops=cost * 10**9, bytes_accessed=cost * 3 * 10**6, transcendentals=0),
        name="after",
    )(value, *earlier)


def gather_ctx(block):
    count = chips()
    chip, core = place()
    same = [block] + [turn(block, k) for k in range(1, count)]
    chip_of = [(chip + count - k) % count for k in range(count)]
    other = [swap(item) for item in same]
    out = jnp.zeros((2 * count,) + block.shape, block.dtype)
    for k in range(count):
        base = 2 * chip_of[k]
        out = lax.dynamic_update_index_in_dim(out, same[k], base + core, 0)
        out = lax.dynamic_update_index_in_dim(out, other[k], base + 1 - core, 0)
    return out, same[1]


def where_am_i():
    return jnp.stack(place()).astype(jnp.int32)


def pack_columns(weights, cuts, vectors):
    count = chips()
    r = weights[0].shape[0]
    total = sum(lead * width for lead, width in cuts)
    below = -(-len(vectors) // 16) * 16

    def kernel(at_ref, *refs):
        ins, outs = refs[: len(weights)], refs[-(count + 1) :]
        chip, core = at_ref[0], at_ref[1]
        for j in range(2 * count):
            pieces = [
                ref[:, (a * 2 * count + j) * width : (a * 2 * count + j + 1) * width]
                for ref, (lead, width) in zip(ins, cuts)
                for a in range(lead)
            ]
            block = jnp.concatenate(pieces, axis=1)
            slot = lax.rem(j // 2 + count - chip, count)
            for k in range(count):

                @pl.when((slot == k) & (core == j % 2))
                def _(k=k, block=block):
                    outs[k][:r, :] = block

                @pl.when((slot == k) & (core != j % 2))
                def _(k=k, block=block):
                    outs[count][k, :r, :] = block

        if vectors:
            lines = [ref[...].astype(F32) for ref in refs[len(weights) : len(weights) + len(vectors)]]
            lines = [
                jnp.concatenate([line, jnp.zeros((1, total - line.shape[1]), F32)], axis=1) for line in lines
            ]
            more = jnp.concatenate(lines + [jnp.zeros((below - len(lines), total), F32)], axis=0).astype(BF16)
            for k in range(count):
                outs[k][r:, :] = more
                outs[count][k, r:, :] = more

    block_shape = jax.ShapeDtypeStruct((r + below, total), BF16)
    return pl.pallas_call(
        kernel,
        out_shape=[block_shape] * count + [jax.ShapeDtypeStruct((count,) + block_shape.shape, BF16)],
        in_specs=[pl.BlockSpec(memory_space=pltpu.SMEM)]
        + [pl.BlockSpec(memory_space=pltpu.VMEM)] * (len(weights) + len(vectors)),
        name="pack_columns",
    )(where_am_i(), *weights, *vectors)


def pack_rows(arrays, more, height):
    count = chips()
    width = sum(item.shape[1] for item in arrays)
    below = more.shape[1]

    def kernel(at_ref, *refs):
        ins, outs = refs[: len(arrays)], refs[-(count + 1) :]
        chip, core = at_ref[0], at_ref[1]
        for k in range(count):
            base = 2 * lax.rem(chip + k, count)
            start = 0
            for ref in ins:
                end = start + ref.shape[1]
                mine = pl.ds(pl.multiple_of((base + core) * height, height), height)
                other = pl.ds(pl.multiple_of((base + 1 - core) * height, height), height)
                outs[k][:height, start:end] = ref[mine, :]
                outs[count][k, :height, start:end] = ref[other, :]
                start = end
            outs[k][height:, :] = refs[len(arrays)][base + core]
            outs[count][k, height:, :] = refs[len(arrays)][base + 1 - core]

    block_shape = jax.ShapeDtypeStruct((height + below, width), BF16)
    return pl.pallas_call(
        kernel,
        out_shape=[block_shape] * count + [jax.ShapeDtypeStruct((count,) + block_shape.shape, BF16)],
        in_specs=[pl.BlockSpec(memory_space=pltpu.SMEM)] + [pl.BlockSpec(memory_space=pltpu.VMEM)] * (1 + len(arrays)),
        name="pack_rows",
    )(where_am_i(), *arrays, more)


def exchange_ctx(packed):
    count = chips()
    arrived = swap(packed[count])
    both = [jnp.stack([packed[k], arrived[k]]) for k in range(count)]
    return [both[0]] + [turn(both[k], k) for k in range(1, count)]


def source_index(at_ref, k, side, count):
    core = at_ref[1] if side == 0 else 1 - at_ref[1]
    return 2 * lax.rem(at_ref[0] + count - k, count) + core


def unpack_to_rows(got, r, widths, earlier):
    count = chips()
    height, total = got[0].shape[1:]
    below = height - r

    def kernel(at_ref, *refs):
        ins, outs = refs[:count], refs[count + len(earlier) :]
        for k in range(count):
            for side in range(2):
                index = source_index(at_ref, k, side, count)
                start = 0
                for out, width in zip(outs, widths):
                    out[pl.ds(pl.multiple_of(index * r, r), r), :] = ins[k][side, :r, start : start + width]
                    start += width
                if below:
                    outs[-1][index] = ins[k][side, r:, :]

    return pl.pallas_call(
        kernel,
        out_shape=[jax.ShapeDtypeStruct((2 * count * r, width), BF16) for width in widths]
        + [jax.ShapeDtypeStruct((2 * count, below, total), BF16)] * (below > 0),
        in_specs=[pl.BlockSpec(memory_space=pltpu.SMEM)]
        + [pl.BlockSpec(memory_space=pltpu.VMEM)] * count
        + [ANYWHERE] * len(earlier),
        name="unpack_to_rows",
    )(where_am_i(), *got, *earlier)


def unpack_to_columns(got, r, cuts):
    count = chips()
    height, total = got[0].shape[1:]

    def kernel(at_ref, *refs):
        ins, outs, held = refs[:count], refs[count:-1], refs[-1]
        for k in range(count):
            for side in range(2):
                held[source_index(at_ref, k, side, count)] = ins[k][side]
        for j in range(2 * count):
            block = held[j, :r, :].astype(F32)
            start = 0
            for out, (lead, width) in zip(outs, cuts):
                for a in range(lead):
                    column = (a * 2 * count + j) * width
                    out[:, column : column + width] = block[:, start : start + width]
                    start += width
        below = held[0, r:, :].astype(F32)
        for j in range(1, 2 * count):
            below = below + held[j, r:, :].astype(F32)
        outs[-1][...] = jnp.sum(below, axis=0, keepdims=True)

    return pl.pallas_call(
        kernel,
        out_shape=[jax.ShapeDtypeStruct((r, 2 * count * lead * width), F32) for lead, width in cuts]
        + [jax.ShapeDtypeStruct((1, total), F32)],
        in_specs=[pl.BlockSpec(memory_space=pltpu.SMEM)] + [pl.BlockSpec(memory_space=pltpu.VMEM)] * count,
        scratch_shapes=[pltpu.VMEM((2 * count, height, total), BF16)],
        name="unpack_to_columns",
    )(where_am_i(), *got)


def split_rows(rows):
    count = chips()
    chip, core = place()
    pairs = rows.reshape((count, 2, rows.shape[0] // (2 * count), rows.shape[1]))
    order = [(chip + k) % count for k in range(1, count + 1)]
    turned = [lax.dynamic_index_in_dim(pairs, index, 0, keepdims=False) for index in order]
    pick = lambda which: jnp.concatenate(
        [lax.dynamic_index_in_dim(item, which, 0, keepdims=False) for item in turned], axis=0
    )
    return pick(core), pick(1 - core)


def chip_sums(left, right, dims, earlier=()):
    count = chips()
    mine, other = split_rows(left)
    leaving = dot(other, right, dims).astype(BF16)
    arrived = swap(after(leaving, *earlier) if earlier else leaving)
    own = dot(mine, right, dims)
    n = own.shape[0] // count
    sums = [own[k * n : (k + 1) * n] + arrived[k * n : (k + 1) * n].astype(F32) for k in range(count)]
    return [item.astype(BF16) for item in sums[:-1]] + sums[-1:]


def add_over_chips(sums, earlier=()):
    count = chips()
    total = sums[-1]
    for k in range(1, count):
        arrived = turn(sums[k - 1], k)
        arrived = after(arrived, *earlier) if earlier else arrived
        total = total + arrived.astype(F32)
        first = arrived if k == 1 else first
    return total, first


def reduce_dp_small(blocks):
    parts = lax.axis_size("dp")
    me = lax.axis_index("dp")
    total = lax.dynamic_index_in_dim(blocks, me, 0, keepdims=False)
    for k in range(1, parts):
        piece = lax.dynamic_index_in_dim(blocks, (me + k) % parts, 0, keepdims=False)
        total = total + lax.ppermute(piece, "dp", [(i, (i + k) % parts) for i in range(parts)])
    return total


def gather_dp(value):
    return lax.all_gather(value, "dp", axis=0, tiled=True)


def scatter_dp(value):
    return lax.psum_scatter(value, "dp", scatter_dimension=0, tiled=True)


def across(value, k):
    return lax.ppermute(value, "dp", [(i, i ^ k) for i in range(lax.axis_size("dp"))])


def turn_gather_dp(value):
    parts = lax.axis_size("dp")
    me = lax.axis_index("dp")
    out = jnp.zeros((parts,) + value.shape, value.dtype)
    out = lax.dynamic_update_index_in_dim(out, value, me, 0)
    for k in range(1, parts):
        out = lax.dynamic_update_index_in_dim(out, across(value, k), me ^ k, 0)
    return out.reshape((parts * value.shape[0],) + value.shape[1:])


def turn_scatter_dp(blocks):
    parts = lax.axis_size("dp")
    me = lax.axis_index("dp")
    blocks = blocks.reshape((parts, blocks.shape[0] // parts) + blocks.shape[1:])
    total = lax.dynamic_index_in_dim(blocks, me, 0, keepdims=False).astype(F32)
    for k in range(1, parts):
        total = total + across(lax.dynamic_index_in_dim(blocks, me ^ k, 0, keepdims=False), k).astype(F32)
    return total


def standardize(values):
    average = jnp.mean(values, axis=-1, keepdims=True)
    centered = values - average
    variance = jnp.mean(centered * centered, axis=-1, keepdims=True)
    factor = lax.rsqrt(variance + EPSILON)
    return centered * factor, factor


def norm_back(grad, gain, standard, factor):
    scaled = grad * gain
    return (
        scaled
        - jnp.mean(scaled, axis=-1, keepdims=True)
        - standard * jnp.mean(scaled * standard, axis=-1, keepdims=True)
    ) * factor


def smooth(pre_act):
    return jax.nn.gelu(pre_act, approximate=True)


def smooth_slope(u):
    inner = 0.7978845608028654 * (u + 0.044715 * u * u * u)
    bend = jnp.tanh(inner)
    return 0.5 * (1.0 + bend) + 0.5 * u * (1.0 - bend * bend) * 0.7978845608028654 * (1.0 + 3.0 * 0.044715 * u * u)


def local(
    tokens_in,
    exit_layer,
    layer_index,
    segment_ids,
    grad_out,
    first_gain,
    first_bias,
    query_weight,
    query_bias,
    key_weight,
    value_weight,
    value_bias,
    out_weight,
    out_bias,
    second_gain,
    second_bias,
    up_weight,
    up_bias,
    down_weight,
    down_bias,
):
    T, N = lax.axis_size("ctx"), lax.axis_size("dp")
    me = lax.axis_index("ctx")
    n, D = tokens_in.shape[1], tokens_in.shape[2]
    r = first_gain.shape[0]
    f = up_bias.shape[0]
    S = T * n
    B = max(HEAD_DIM, r)
    A = D // (T * B)
    L = A * B
    x = tokens_in[0]
    g_out = grad_out[0]
    active = (exit_layer[0] > layer_index[0]).astype(F32)

    x_all = lax.all_gather(x, "ctx", axis=0, tiled=True)
    natural = r % HEAD_DIM == 0
    if natural:
        w_out = turn_gather_dp(out_weight)
    else:
        w_all = lax.all_gather(out_weight, ("dp", "ctx"), axis=0, tiled=True).reshape(A, T, B, D)
        w_out = lax.dynamic_index_in_dim(w_all, me, 1, keepdims=False).reshape(L, D)
    vectors = [first_gain, first_bias, query_bias, value_bias, out_bias, second_gain, second_bias, down_bias, up_bias]
    vectors = [v.reshape(1, -1) for v in vectors + [active.astype(BF16), segment_ids[0].astype(BF16)]]
    got = exchange_ctx(pack_columns([query_weight, key_weight, value_weight], [(A, B)] * 3, vectors))
    qkv_rows, small_got = unpack_to_rows(got, r, (3 * L,), (x_all, w_out))
    up_packed = pack_columns([up_weight], [(N, f)], [])
    w_qkv = gather_dp(qkv_rows)
    small_width = max(r, f)
    params = turn_gather_dp(small_got[:, :9, :small_width].reshape(T * 9, small_width)).reshape(N, T, 9, small_width)
    g_all, g_begun = gather_ctx(after(g_out, qkv_rows))
    g_all = g_all.reshape(S, D)

    feature = lambda i: params[:, :, i, :r].reshape(D).astype(F32)
    gain_one, bias_one, bias_query, bias_value, bias_out, gain_two, bias_two, bias_down = (
        feature(i) for i in range(8)
    )
    bias_up = lax.dynamic_index_in_dim(params[:, :, 8, :f], me, 1, keepdims=False).reshape(N * f).astype(F32)
    active_row = small_got[:, 9, :n].reshape(S)
    segs = small_got[:, 10, :n].reshape(S).astype(jnp.int32)
    seg_col, seg_row = segs.reshape(S, 1), segs.reshape(1, S)
    own_heads = lambda v: lax.dynamic_index_in_dim(v.reshape(A, T, B), me, 1, keepdims=False).reshape(L)
    bias_qkv = jnp.concatenate([own_heads(bias_query), jnp.zeros((L,), F32), own_heads(bias_value)])

    standard_one, _ = standardize(x_all.astype(F32))
    normed_one = after((standard_one * gain_one + bias_one).astype(BF16), g_all)
    qkv = (dot(normed_one, w_qkv) + bias_qkv).astype(BF16)
    w_down = gather_dp(after(down_weight, qkv))
    up_got = exchange_ctx([*up_packed[:-1], after(up_packed[-1], g_begun)])
    mixed, log_total = attention_forward(qkv, seg_col, seg_row, ())
    (up_rows,) = unpack_to_rows(up_got, r, (N * f,), (mixed,))
    w_up = gather_dp(up_rows)
    branch = add_over_chips(chip_sums(mixed, w_out, NN, (up_rows,)))[0] + bias_out
    inputs = x.astype(F32)
    active_own = active[:, None]
    middle = inputs + active_own * branch

    standard_two, factor_two = standardize(middle)
    normed_two = (standard_two * gain_two + bias_two).astype(BF16)
    normed_two_all = gather_ctx(after(normed_two, cost=0))[0].reshape(S, D)
    pre_act = dot(normed_two_all, w_up) + bias_up
    hidden = smooth(pre_act).astype(BF16)

    grad_ffn = (active_row[:, None] * g_all).astype(BF16)
    grad_hidden = dot(grad_ffn, w_down, NT)
    grad_pre = (grad_hidden * smooth_slope(pre_act)).astype(BF16)
    sums_two = chip_sums(grad_pre, w_up, NT)
    grad_normed_two, begun_two = add_over_chips(sums_two)
    hidden = after(hidden, sums_two[0])
    grad_down_part = dot(hidden, grad_ffn, TN).astype(BF16)
    grad_down = scatter_dp(grad_down_part)
    grad_up_part = dot(after(normed_two_all, sums_two[0]), grad_pre, TN).astype(BF16)
    grad_up_mine = scatter_dp(grad_up_part)
    feed_sums = chip_sums(after(hidden, begun_two), w_down, NN)
    grad_res = g_out.astype(F32)
    grad_middle = grad_res + norm_back(grad_normed_two, gain_two, standard_two, factor_two)
    grad_branch = after((active_own * grad_middle).astype(BF16), cost=250)

    grad_branch_all = gather_ctx(grad_branch)[0].reshape(S, D)
    grad_heads = dot(grad_branch_all, w_out, NT).astype(BF16)
    grad_out_w = dot(mixed, grad_branch_all, TN)
    if natural:
        grad_out_w = scatter_dp(grad_out_w.astype(BF16))
    else:
        spread = jnp.zeros((A, T, B, D), F32)
        spread = lax.dynamic_update_index_in_dim(spread, grad_out_w.reshape(A, B, D), me, 1)
        grad_out_w = lax.psum_scatter(spread.reshape(D, D), ("dp", "ctx"), scatter_dimension=0, tiled=True)
    grad_qkv = attention_backward(
        qkv, grad_heads, log_total, mixed, seg_col, seg_row, (grad_down, grad_up_mine)
    )

    grad_qkv_part = dot(normed_one, grad_qkv, TN).astype(BF16)
    feed, _ = add_over_chips([after(item, grad_branch_all) for item in feed_sums[:-1]] + feed_sums[-1:], (grad_qkv,))
    sums_one = chip_sums(grad_qkv, w_qkv, NT, (grad_qkv_part, feed, grad_out_w))
    grad_normed_one, _ = add_over_chips(sums_one)
    grad_normed_one = after(grad_normed_one, cost=0)
    layer_out = (middle + active_own * (feed + bias_down)).astype(BF16)[None]
    standard_in, factor_in = standardize(inputs)
    grad_in = (grad_middle + norm_back(grad_normed_one, gain_one, standard_in, factor_in)).astype(BF16)[None]

    grad_gain_one = jnp.sum(grad_normed_one * standard_in, axis=0)
    grad_bias_one = jnp.sum(grad_normed_one, axis=0)
    grad_gain_two = jnp.sum(grad_normed_two * standard_two, axis=0)
    grad_bias_two = jnp.sum(grad_normed_two, axis=0)
    ctx_index = lax.broadcasted_iota(jnp.int32, (1, T, 1), 1)
    spread_heads = lambda v: jnp.where(ctx_index == me, v.reshape(A, 1, B), 0.0).reshape(D)
    grad_bias_qkv = jnp.sum(grad_qkv.astype(F32), axis=0)
    grad_out_sum = jnp.sum(grad_branch.astype(F32), axis=0)
    grad_down_sum = jnp.sum((active_own * grad_res), axis=0)
    grad_up_sum = jnp.sum(grad_pre.astype(F32), axis=0)
    features = jnp.stack(
        [
            grad_gain_one,
            grad_bias_one,
            spread_heads(grad_bias_qkv[:L]),
            spread_heads(grad_bias_qkv[2 * L :]),
            grad_out_sum,
            grad_gain_two,
            grad_bias_two,
            grad_down_sum,
        ]
    )
    features = features.reshape(8, N, T, r).transpose(1, 2, 0, 3).reshape(N, T, 8 * r)
    units = jnp.where(
        lax.broadcasted_iota(jnp.int32, (1, T, 1), 1) == me, grad_up_sum.reshape(N, 1, f), 0.0
    )
    sums = jnp.concatenate([features, units], axis=2).reshape(N, T * (8 * r + f))
    sums = reduce_dp_small(sums).reshape(T, 8 * r + f)
    grad_qkv_mine = scatter_dp(grad_qkv_part)
    coarse = sums.astype(BF16)
    fine = (sums - coarse.astype(F32)).astype(BF16)
    more = jnp.stack([coarse, fine], axis=1)
    more = jnp.pad(more, ((0, 0), (0, 14), (0, 3 * L + N * f - more.shape[2])))
    grad_got = exchange_ctx(pack_rows([after(grad_qkv_mine, grad_normed_one), grad_up_mine], more, r))
    grad_q, grad_k, grad_v, grad_up, sums = unpack_to_columns(grad_got, r, [(A, B)] * 3 + [(N, f)])
    sums = sums[0, : 8 * r + f]
    begun_one = grad_got[0]
    shard = lambda i: sums[i * r : (i + 1) * r]
    return (
        layer_out,
        grad_in,
        shard(0),
        shard(1),
        grad_q,
        shard(2),
        grad_k,
        grad_v,
        shard(3),
        grad_out_w.astype(F32),
        shard(4),
        shard(5),
        shard(6),
        grad_up,
        sums[8 * r :],
        after(grad_down, begun_one).astype(F32),
        shard(7),
    )


def solution(mesh):
    rows = P("dp", "ctx", None)
    flags = P("dp", "ctx")
    vector = P(("dp", "ctx"))
    matrix = P(("dp", "ctx"), None)
    in_specs = (
        rows, flags, P(), flags, rows, vector, vector, matrix, vector, matrix,
        matrix, vector, matrix, vector, vector, vector, matrix, vector, matrix, vector,
    )
    out_specs = (
        rows, rows, vector, vector, matrix, vector, matrix, matrix, vector, matrix,
        vector, vector, vector, matrix, vector, matrix, vector,
    )
    return jax.shard_map(local, mesh=mesh, in_specs=in_specs, out_specs=out_specs, check_vma=False)
```

time: 768 us -> 647 us (0.84)
  waiting for transfers between devices: 343 us -> 262 us
  local copies, waits for them, and re-layouts: 88.9 us -> 56.3 us
  Pallas kernels: 13.2 us -> 33.2 us
  starting transfers between devices: 156 us -> 138 us
  matrix products: 96 us -> 83.9 us
  other arithmetic: 43.9 us -> 53.4 us
    ppermute x42 -> x30, waiting for transfers between devices: 303 us -> 246 us  [turn(): lax.ppermute(value, 'ctx', [(2 * s + core, 2 * ((s + k) % count) + core)...]
    reduce_scatter x4, waiting for transfers between devices: 30.6 us -> 0.01 us  [scatter_dp(): return lax.psum_scatter(value, 'dp', scatter_dimension=0, tiled=True)]
    ppermute x42 -> x30, starting transfers between devices: 143 us -> 123 us  [turn(): lax.ppermute(value, 'ctx', [(2 * s + core, 2 * ((s + k) % count) + core)...]
    pallas_call x0 -> x26, Pallas kernels: none -> 18 us  [the longest x2 5.92 us: pack_columns(): pl.pallas_call(kernel, out_shape=[block_shape] * count + [jax.ShapeDtypeS...]
    dot_general x17 -> x16, matrix products: 96 us -> 83.9 us  [dot(): return lax.dot_general(left, right, dims, preferred_element_type=F32)]
    dynamic_update_slice x20 -> x12, local copies, waits for them, and re-layouts: 15.2 us -> 6.99 us  [gather_ctx(): out = lax.dynamic_update_index_in_dim(out, other[k], base + 1 - core, 0)]
    another operation x4 -> x14, other arithmetic: 2.6 us -> 10.8 us  [the longest x12 9.32 us: exchange_ctx(): both = [jnp.stack([packed[k], arrived[k]]) for k in range(count)]]
    convert_element_type x15 -> x7, local copies, waits for them, and re-layouts: 9.35 us -> 1.25 us  [the longest x6 1.03 us: local(): feature = lambda i: params[:, :, i, :r].reshape(D).astype(F32)]
  transfers between devices with their start and end apart: 85 -> 66, of which waited for: 28 -> 24; matrix products, arithmetic and copies ran while one was open for 23% -> 23% of each run, Pallas kernels for 2% -> 3%
where the time goes in v2:
time: 647 us; the launch traced here: 643 us
  waiting for transfers between devices  262 us (40%)
  starting transfers between devices  138 us (21%)
  matrix products  83.9 us (13%)
  local copies, waits for them, and re-layouts  56.3 us (9%)
  other arithmetic  53.4 us (8%)
  Pallas kernels  33.2 us (5%)
  between operations  16.4 us (3%)
    ppermute x30, waiting for transfers between devices, turn(): lax.ppermute(value, 'ctx', [(2 * s + core, 2 * ((s + k) % count) + core)...  246 us
    ppermute x30, starting transfers between devices, turn(): lax.ppermute(value, 'ctx', [(2 * s + core, 2 * ((s + k) % count) + core)...  123 us
    dot_general x16, matrix products, dot(): return lax.dot_general(left, right, dims, preferred_element_type=F32)  83.9 us
    unnamed x146, local copies, waits for them, and re-layouts  20 us
  transfers between devices with their start and end apart: 66, of which 24 were waited for; matrix products, arithmetic and copies ran while one was open for 23% of the time, Pallas kernels for 3%

profile of v2, /device:TPU:0, one launch (start us, length us, event | category | flops | bytes accessed | tf_op | source)
XLA Modules:
  0.0 643.3 jit_solution(5341332480517573244)
XLA Ops:
  33.6 12.8 %collective-permute-done.3.refs_3_ = bf16[2,80,768]{2,1,0:T(8,128)(2,1)S(1)} collective-permute-done((bf16[2,80,768]{2,1,0:T(8,128)(2,1)S(1)}, bf16[2,80,768]{2,1,0:T(8,128)(2,1)S(1)}, u32[]{:S(2)}, u32[]{:S(2)}) %collective-permute-start.3) | collective-permute-done | bytes 245792 | tf_op jit(solution)/shard_map/ppermute | solution.py:140
  46.3 30.2 %collective-permute-done.2.refs_2_ = bf16[2,80,768]{2,1,0:T(8,128)(2,1)S(1)} collective-permute-done((bf16[2,80,768]{2,1,0:T(8,128)(2,1)S(1)}, bf16[2,80,768]{2,1,0:T(8,128)(2,1)S(1)}, u32[]{:S(2)}, u32[]{:S(2)}) %collective-permute-start.2) | collective-permute-done | bytes 245792 | tf_op jit(solution)/shard_map/ppermute | solution.py:140
  107.8 4.7 fusion.5.refs_0_
  113.8 9.5 %collective-permute-done.13 = bf16[128,2048]{1,0:T(8,128)(2,1)S(1)} collective-permute-done((bf16[128,2048]{1,0:T(8,128)(2,1)S(1)}, bf16[128,2048]{1,0:T(8,128)(2,1)S(1)}, u32[]{:S(2)}, u32[]{:S(2)}) %collective-permute-start.13) | collective-permute-done | bytes 524320 | tf_op jit(solution)/shard_map/ppermute | solution.py:140
  128.2 10.2 %collective-permute-start.18 = (bf16[2,64,1024]{2,1,0:T(8,128)(2,1)}, bf16[2,64,1024]{2,1,0:T(8,128)(2,1)}, u32[]{:S(2)}, u32[]{:S(2)}) collective-permute-start(bf16[2,64,1024]{2,1,0:T(8,128)(2,1)} %pad_maximum_fusion.5), channel_id=1, source_target_pairs={{0,2},{1,3},{2,4},{3,5},{4,6},{5,7},{6,0},{7,1},{8,10},{9,11},{10,... | collective-permute-start | bytes 786440 | tf_op jit(solution)/shard_map/ppermute | solution.py:140
  149.1 6.6 %add_convert_fusion.refs_0_.refs_1_ = bf16[1024,768]{1,0:T(8,128)(2,1)S(1)} fusion(bf16[1024,2048]{1,0:T(8,128)(2,1)} %after.21, bf16[2048,768]{1,0:T(8,128)(2,1)} %all-gather.6.cloned.1.call-done, f32[768]{0:T(1024)S(1)} %pad_maximum_fusion.12), kind=kOutput, calls=%fused_computation.34 | convolution fusion | flops 3222798336 | bytes 8915968 | tf_op jit(solution)/shard_map/dot_general | solution.py:24
  155.7 5.2 attention_forward.1
  178.9 11.2 %collective-permute-done.22 = bf16[128,2048]{1,0:T(8,128)(2,1)S(1)} collective-permute-done((bf16[128,2048]{1,0:T(8,128)(2,1)}, bf16[128,2048]{1,0:T(8,128)(2,1)S(1)}, u32[]{:S(2)}, u32[]{:S(2)}) %collective-permute-start.22) | collective-permute-done | bytes 524320 | tf_op jit(solution)/shard_map/ppermute | solution.py:140
  190.2 21.7 %collective-permute-done.23 = bf16[128,2048]{1,0:T(8,128)(2,1)S(1)} collective-permute-done((bf16[128,2048]{1,0:T(8,128)(2,1)S(1)}, bf16[128,2048]{1,0:T(8,128)(2,1)S(1)}, u32[]{:S(2)}, u32[]{:S(2)}) %collective-permute-start.23) | collective-permute-done | bytes 524320 | tf_op jit(solution)/shard_map/ppermute | solution.py:140
  215.7 22.3 %collective-permute-start.26 = (bf16[128,2048]{1,0:T(8,128)(2,1)}, bf16[128,2048]{1,0:T(8,128)(2,1)S(1)}, u32[]{:S(2)}, u32[]{:S(2)}) collective-permute-start(bf16[128,2048]{1,0:T(8,128)(2,1)} %after.24), channel_id=1, source_target_pairs={{0,2},{1,3},{2,4},{3,5},{4,6},{5,7},{6,0},{7,1},{8,10},{9,11},{10,... | collective-permute-start | bytes 1572872 | tf_op jit(solution)/shard_map/ppermute | solution.py:140
  244.0 8.4 %collective-permute-done.26 = bf16[128,2048]{1,0:T(8,128)(2,1)S(1)} collective-permute-done((bf16[128,2048]{1,0:T(8,128)(2,1)}, bf16[128,2048]{1,0:T(8,128)(2,1)S(1)}, u32[]{:S(2)}, u32[]{:S(2)}) %collective-permute-start.26) | collective-permute-done | bytes 524320 | tf_op jit(solution)/shard_map/ppermute | solution.py:140
  252.4 22.3 %collective-permute-done.28 = bf16[128,2048]{1,0:T(8,128)(2,1)S(1)} collective-permute-done((bf16[128,2048]{1,0:T(8,128)(2,1)}, bf16[128,2048]{1,0:T(8,128)(2,1)S(1)}, u32[]{:S(2)}, u32[]{:S(2)}) %collective-permute-start.28) | collective-permute-done | bytes 524320 | tf_op jit(solution)/shard_map/ppermute | solution.py:140
  281.1 11.4 %fusion.13 = (bf16[1024,1024]{1,0:T(8,128)(2,1)}, f32[1024,1024]{1,0:T(8,128)}) fusion(f32[1024]{0:T(1024)S(1)} %bitcast.333, bf16[1024,2048]{1,0:T(8,128)(2,1)} %bitcast.60.refs_0_, bf16[2048,1024]{1,0:T(8,128)(2,1)} %all-gather.8.cloned.1.call-done), kind=kOutput, calls=%fused_computation.18 | convolution fusion | flops 4305453056 | bytes 14684160 | tf_op jit(solution)/shard_map/dot_general | solution.py:24
  292.5 11.8 %convert_reduce_fusion.1 = (f32[1024]{0:T(1024)}, bf16[1024,1024]{1,0:T(8,128)(2,1)S(1)}) fusion(f32[1024,1024]{1,0:T(8,128)} %get-tuple-element.168, f32[1024]{0:T(1024)S(1)} %bitcast.334, bf16[1024,2048]{1,0:T(8,128)(2,1)} %all-gather.10.cloned.1.call-done, bf16[1024,2048]{1,0:T(8,128)(2,1)} %bitcast.300, bf16[1024]{0:T(1024)(128)(2,1)S(1)} %bitcast.335), kind=kOutput, calls=%fused_computation.26 | convolution fusion | flops 4320132096 | bytes 14690304 | tf_op jit(solution)/shard_map/dot_general | solution.py:24
  315.2 8.4 %convolution_convert_fusion = bf16[2048,1024]{1,0:T(8,128)(2,1)} fusion(bf16[1024,2048]{1,0:T(8,128)(2,1)} %after.30, bf16[1024,1024]{1,0:T(8,128)(2,1)S(1)} %get-tuple-element.170), kind=kOutput, calls=%fused_computation.27 | convolution fusion | flops 4297064448 | bytes 10485760 | tf_op jit(solution)/shard_map/dot_general | solution.py:24
  324.6 11.7 %collective-permute-start.33 = (bf16[128,2048]{1,0:T(8,128)(2,1)S(1)}, bf16[128,2048]{1,0:T(8,128)(2,1)S(1)}, u32[]{:S(2)}, u32[]{:S(2)}) collective-permute-start(bf16[128,2048]{1,0:T(8,128)(2,1)S(1)} %copy-done.24), channel_id=1, source_target_pairs={{0,2},{1,3},{2,4},{3,5},{4,6},{5,7},{6,0},{7,1},{8,10},{9,11},{10,... | collective-permute-start | bytes 1572872 | tf_op jit(solution)/shard_map/ppermute | solution.py:140
  339.1 10.1 %convolution_convert_fusion.1 = bf16[1024,2048]{1,0:T(8,128)(2,1)} fusion(bf16[1024,1024]{1,0:T(8,128)(2,1)} %after.26.refs_0_, bf16[1024,2048]{1,0:T(8,128)(2,1)} %bitcast.301, bf16[1024]{0:T(1024)(128)(2,1)S(1)} %bitcast.336), kind=kOutput, calls=%fused_computation.28 | convolution fusion | flops 4299161600 | bytes 10487808 | tf_op jit(solution)/shard_map/dot_general | solution.py:24
  349.8 22.4 %collective-permute-done.35 = bf16[128,2048]{1,0:T(8,128)(2,1)} collective-permute-done((bf16[128,2048]{1,0:T(8,128)(2,1)}, bf16[128,2048]{1,0:T(8,128)(2,1)}, u32[]{:S(2)}, u32[]{:S(2)}) %collective-permute-start.35) | collective-permute-done | bytes 524320 | tf_op jit(solution)/shard_map/ppermute | solution.py:140
  377.8 11.8 %collective-permute-start.38 = (bf16[128,2048]{1,0:T(8,128)(2,1)}, bf16[128,2048]{1,0:T(8,128)(2,1)S(1)}, u32[]{:S(2)}, u32[]{:S(2)}) collective-permute-start(bf16[128,2048]{1,0:T(8,128)(2,1)} %after.28), channel_id=1, source_target_pairs={{0,2},{1,3},{2,4},{3,5},{4,6},{5,7},{6,0},{7,1},{8,10},{9,11},{10,... | collective-permute-start | bytes 1572872 | tf_op jit(solution)/shard_map/ppermute | solution.py:140
  399.5 4.4 fusion.84
  403.9 21.7 %collective-permute-done.40 = bf16[128,2048]{1,0:T(8,128)(2,1)S(1)} collective-permute-done((bf16[128,2048]{1,0:T(8,128)(2,1)}, bf16[128,2048]{1,0:T(8,128)(2,1)S(1)}, u32[]{:S(2)}, u32[]{:S(2)}) %collective-permute-start.40) | collective-permute-done | bytes 524320 | tf_op jit(solution)/shard_map/ppermute | solution.py:140
  439.4 10.9 %collective-permute-start.44 = (bf16[128,2048]{1,0:T(8,128)(2,1)}, bf16[128,2048]{1,0:T(8,128)(2,1)}, u32[]{:S(2)}, u32[]{:S(2)}) collective-permute-start(bf16[128,2048]{1,0:T(8,128)(2,1)} %after.29), channel_id=1, source_target_pairs={{0,2},{1,3},{2,4},{3,5},{4,6},{5,7},{6,0},{7,1},{8,10},{9,11},{10,... | collective-permute-start | bytes 1572872 | tf_op jit(solution)/shard_map/ppermute | solution.py:140
  455.2 10.0 %attention_backward.1.refs_1_ = bf16[1024,768]{1,0:T(8,128)(2,1)S(1)} custom-call(bf16[1024,768]{1,0:T(8,128)(2,1)} %copy-done.5, bf16[1024,256]{1,0:T(8,128)(2,1)S(1)} %convolution_convert_fusion.8.refs_1_, f32[4,1024]{1,0:T(4,128)S(1)} %get-tuple-element.54.refs_2_, bf16[1024,256]{1,0:T(8,128)(2,1)S(1)} %copy-done.4, s32[1024,1]{1,0:T(8,128)S(1)} %copy-done.8, ...), custom_call_target="tpu_custom_call" | custom-call | flops 10485760000 | bytes 3670016 | tf_op jit(solution)/shard_map/attention_backward/pallas_call | solution.py:123
  465.2 5.2 convolution_convert_fusion.2.refs_1_
  470.6 5.1 convolution_convert_fusion.6.refs_0_
  475.7 11.5 %collective-permute-done.45.refs_0_ = bf16[128,2048]{1,0:T(8,128)(2,1)} collective-permute-done((bf16[128,2048]{1,0:T(8,128)(2,1)}, bf16[128,2048]{1,0:T(8,128)(2,1)}, u32[]{:S(2)}, u32[]{:S(2)}) %collective-permute-start.45) | collective-permute-done | bytes 524320 | tf_op jit(solution)/shard_map/ppermute | solution.py:140
  499.0 11.5 %collective-permute-start.48 = (bf16[128,2048]{1,0:T(8,128)(2,1)}, bf16[128,2048]{1,0:T(8,128)(2,1)S(1)}, u32[]{:S(2)}, u32[]{:S(2)}) collective-permute-start(bf16[128,2048]{1,0:T(8,128)(2,1)} %get-tuple-element.80), channel_id=1, source_target_pairs={{0,2},{1,3},{2,4},{3,5},{4,6},{5,7},{6,0},{7,1},{8,10},{9,11},{10,... | collective-permute-start | bytes 1572872 | tf_op jit(solution)/shard_map/ppermute | solution.py:140
  513.4 10.2 %collective-permute-done.48 = bf16[128,2048]{1,0:T(8,128)(2,1)S(1)} collective-permute-done((bf16[128,2048]{1,0:T(8,128)(2,1)}, bf16[128,2048]{1,0:T(8,128)(2,1)S(1)}, u32[]{:S(2)}, u32[]{:S(2)}) %collective-permute-start.48) | collective-permute-done | bytes 524320 | tf_op jit(solution)/shard_map/ppermute | solution.py:140
  523.6 21.5 %collective-permute-done.49 = bf16[128,2048]{1,0:T(8,128)(2,1)S(1)} collective-permute-done((bf16[128,2048]{1,0:T(8,128)(2,1)S(1)}, bf16[128,2048]{1,0:T(8,128)(2,1)S(1)}, u32[]{:S(2)}, u32[]{:S(2)}) %collective-permute-start.49) | collective-permute-done | bytes 524320 | tf_op jit(solution)/shard_map/ppermute | solution.py:140
  566.2 13.7 %collective-permute-start.57 = (bf16[2,80,1792]{2,1,0:T(8,128)(2,1)}, bf16[2,80,1792]{2,1,0:T(8,128)(2,1)S(1)}, u32[]{:S(2)}, u32[]{:S(2)}) collective-permute-start(bf16[2,80,1792]{2,1,0:T(8,128)(2,1)} %pad_maximum_fusion.3), channel_id=1, source_target_pairs={{0,6},{1,7},{2,0},{3,1},{4,2},{5,3},{6,4},{7,5},{8,14},{9,15},{10,... | collective-permute-start | bytes 1720328 | tf_op jit(solution)/shard_map/ppermute | solution.py:140
  587.2 6.5 %collective-permute-done.57.refs_3_ = bf16[2,80,1792]{2,1,0:T(8,128)(2,1)S(1)} collective-permute-done((bf16[2,80,1792]{2,1,0:T(8,128)(2,1)}, bf16[2,80,1792]{2,1,0:T(8,128)(2,1)S(1)}, u32[]{:S(2)}, u32[]{:S(2)}) %collective-permute-start.57) | collective-permute-done | bytes 573472 | tf_op jit(solution)/shard_map/ppermute | solution.py:140
  593.7 35.9 %collective-permute-done.56.refs_2_ = bf16[2,80,1792]{2,1,0:T(8,128)(2,1)} collective-permute-done((bf16[2,80,1792]{2,1,0:T(8,128)(2,1)}, bf16[2,80,1792]{2,1,0:T(8,128)(2,1)}, u32[]{:S(2)}, u32[]{:S(2)}) %collective-permute-start.56) | collective-permute-done | bytes 573472 | tf_op jit(solution)/shard_map/ppermute | solution.py:140
  (440 shorter events, 206.4 us)
Async XLA Ops:
  7.2 73.3 %all-gather.12.cloned.1.call-start = ((), (), s32[]{:S(2)}) async-start(), calls=%async_computation.11 | async-start | bytes 4718592 | tf_op jit(solution)/shard_map/all_gather | solution.py:474
  9.6 139.5 %all-gather.6.cloned.1.call-start = ((), (), s32[]{:S(2)}) async-start(), calls=%async_computation.4 | async-start | bytes 3932160 | tf_op jit(solution)/shard_map/all_gather | solution.py:381
  31.6 44.9 %collective-permute-start.2 = (bf16[2,80,768]{2,1,0:T(8,128)(2,1)S(1)}, bf16[2,80,768]{2,1,0:T(8,128)(2,1)S(1)}, u32[]{:S(2)}, u32[]{:S(2)}) collective-permute-start(bf16[2,80,768]{2,1,0:T(8,128)(2,1)S(1)} %pad_maximum_fusion.10), channel_id=1, source_target_pairs={{0,4},{1,5},{2,6},{3,7},{4,0},{5,1},{6,2},{7,3},{8,12},{9,13},{10,... | collective-permute-start | bytes 737288 | tf_op jit(solution)/shard_map/ppermute | solution.py:140
  31.7 44.8 %collective-permute-start.1 = (bf16[2,80,768]{2,1,0:T(8,128)(2,1)S(1)}, bf16[2,80,768]{2,1,0:T(8,128)(2,1)S(1)}, u32[]{:S(2)}, u32[]{:S(2)}) collective-permute-start(bf16[2,80,768]{2,1,0:T(8,128)(2,1)S(1)} %pad_maximum_fusion.9), channel_id=1, source_target_pairs={{0,2},{1,3},{2,4},{3,5},{4,6},{5,7},{6,0},{7,1},{8,10},{9,11},{10,... | collective-permute-start | bytes 737288 | tf_op jit(solution)/shard_map/ppermute | solution.py:140
  82.9 41.0 %collective-permute-start.10 = (bf16[128,2048]{1,0:T(8,128)(2,1)}, bf16[128,2048]{1,0:T(8,128)(2,1)S(1)}, u32[]{:S(2)}, u32[]{:S(2)}) collective-permute-start(bf16[128,2048]{1,0:T(8,128)(2,1)} %after.20), channel_id=1, source_target_pairs={{0,1},{1,0},{2,3},{3,2},{4,5},{5,4},{6,7},{7,6},{8,9},{9,8},{10,11... | collective-permute-start | bytes 1572872 | tf_op jit(solution)/shard_map/ppermute | solution.py:146
  87.6 193.5 %all-gather.8.cloned.1.call-start = ((), (), s32[]{:S(2)}) async-start(), calls=%async_computation.5 | async-start | bytes 5242880 | tf_op jit(solution)/shard_map/all_gather | solution.py:381
  113.3 29.5 %collective-permute-start.12 = (bf16[128,2048]{1,0:T(8,128)(2,1)}, bf16[128,2048]{1,0:T(8,128)(2,1)S(1)}, u32[]{:S(2)}, u32[]{:S(2)}) collective-permute-start(bf16[128,2048]{1,0:T(8,128)(2,1)} %copy-done.34), channel_id=1, source_target_pairs={{0,1},{1,0},{2,3},{3,2},{4,5},{5,4},{6,7},{7,6},{8,9},{9,8},{10,11... | collective-permute-start | bytes 1572872 | tf_op jit(solution)/shard_map/ppermute | solution.py:146
  128.2 33.5 %collective-permute-start.18 = (bf16[2,64,1024]{2,1,0:T(8,128)(2,1)}, bf16[2,64,1024]{2,1,0:T(8,128)(2,1)}, u32[]{:S(2)}, u32[]{:S(2)}) collective-permute-start(bf16[2,64,1024]{2,1,0:T(8,128)(2,1)} %pad_maximum_fusion.5), channel_id=1, source_target_pairs={{0,2},{1,3},{2,4},{3,5},{4,6},{5,7},{6,0},{7,1},{8,10},{9,11},{10,... | collective-permute-start | bytes 786440 | tf_op jit(solution)/shard_map/ppermute | solution.py:140
  164.1 128.3 %all-gather.10.cloned.1.call-start = ((), (), s32[]{:S(2)}) async-start(), calls=%async_computation.6 | async-start | bytes 5242880 | tf_op jit(solution)/shard_map/all_gather | solution.py:381
  176.3 35.6 %collective-permute-start.23 = (bf16[128,2048]{1,0:T(8,128)(2,1)S(1)}, bf16[128,2048]{1,0:T(8,128)(2,1)S(1)}, u32[]{:S(2)}, u32[]{:S(2)}) collective-permute-start(bf16[128,2048]{1,0:T(8,128)(2,1)S(1)} %get-tuple-element.91), channel_id=1, source_target_pairs={{0,4},{1,5},{2,6},{3,7},{4,0},{5,1},{6,2},{7,3},{8,12},{9,13},{10,... | collective-permute-start | bytes 1572872 | tf_op jit(solution)/shard_map/ppermute | solution.py:140
  176.9 34.9 %collective-permute-start.24 = (bf16[128,2048]{1,0:T(8,128)(2,1)S(1)}, bf16[128,2048]{1,0:T(8,128)(2,1)S(1)}, u32[]{:S(2)}, u32[]{:S(2)}) collective-permute-start(bf16[128,2048]{1,0:T(8,128)(2,1)S(1)} %get-tuple-element.90), channel_id=1, source_target_pairs={{0,6},{1,7},{2,0},{3,1},{4,2},{5,3},{6,4},{7,5},{8,14},{9,15},{10,... | collective-permute-start | bytes 1572872 | tf_op jit(solution)/shard_map/ppermute | solution.py:140
  178.9 273.8 %reduce-scatter.7.cloned.1.call-start = ((), (), s32[]{:S(2)}) async-start(), calls=%async_computation.8 | async-start | bytes 5242880 | tf_op jit(solution)/shard_map/reduce_scatter | solution.py:385
  215.7 59.4 %collective-permute-start.25 = (bf16[128,2048]{1,0:T(8,128)(2,1)}, bf16[128,2048]{1,0:T(8,128)(2,1)S(1)}, u32[]{:S(2)}, u32[]{:S(2)}) collective-permute-start(bf16[128,2048]{1,0:T(8,128)(2,1)} %after.24), channel_id=1, source_target_pairs={{0,1},{1,0},{2,3},{3,2},{4,5},{5,4},{6,7},{7,6},{8,9},{9,8},{10,11... | collective-permute-start | bytes 1572872 | tf_op jit(solution)/shard_map/ppermute | solution.py:146
  215.7 36.7 %collective-permute-start.26 = (bf16[128,2048]{1,0:T(8,128)(2,1)}, bf16[128,2048]{1,0:T(8,128)(2,1)S(1)}, u32[]{:S(2)}, u32[]{:S(2)}) collective-permute-start(bf16[128,2048]{1,0:T(8,128)(2,1)} %after.24), channel_id=1, source_target_pairs={{0,2},{1,3},{2,4},{3,5},{4,6},{5,7},{6,0},{7,1},{8,10},{9,11},{10,... | collective-permute-start | bytes 1572872 | tf_op jit(solution)/shard_map/ppermute | solution.py:140
  238.1 36.6 %collective-permute-start.28 = (bf16[128,2048]{1,0:T(8,128)(2,1)}, bf16[128,2048]{1,0:T(8,128)(2,1)S(1)}, u32[]{:S(2)}, u32[]{:S(2)}) collective-permute-start(bf16[128,2048]{1,0:T(8,128)(2,1)} %after.24), channel_id=1, source_target_pairs={{0,4},{1,5},{2,6},{3,7},{4,0},{5,1},{6,2},{7,3},{8,12},{9,13},{10,... | collective-permute-start | bytes 1572872 | tf_op jit(solution)/shard_map/ppermute | solution.py:140
  239.8 34.8 %collective-permute-start.30 = (bf16[128,2048]{1,0:T(8,128)(2,1)}, bf16[128,2048]{1,0:T(8,128)(2,1)S(1)}, u32[]{:S(2)}, u32[]{:S(2)}) collective-permute-start(bf16[128,2048]{1,0:T(8,128)(2,1)} %after.24), channel_id=1, source_target_pairs={{0,6},{1,7},{2,0},{3,1},{4,2},{5,3},{6,4},{7,5},{8,14},{9,15},{10,... | collective-permute-start | bytes 1572872 | tf_op jit(solution)/shard_map/ppermute | solution.py:140
  323.6 129.1 %reduce-scatter.5.cloned.1.call-start = ((), (), s32[]{:S(2)}) async-start(), calls=%async_computation.7 | async-start | bytes 5242880 | tf_op jit(solution)/shard_map/reduce_scatter | solution.py:385
  336.4 35.8 %collective-permute-start.35 = (bf16[128,2048]{1,0:T(8,128)(2,1)}, bf16[128,2048]{1,0:T(8,128)(2,1)}, u32[]{:S(2)}, u32[]{:S(2)}) collective-permute-start(bf16[128,2048]{1,0:T(8,128)(2,1)} %get-tuple-element.86), channel_id=1, source_target_pairs={{0,4},{1,5},{2,6},{3,7},{4,0},{5,1},{6,2},{7,3},{8,12},{9,13},{10,... | collective-permute-start | bytes 1572872 | tf_op jit(solution)/shard_map/ppermute | solution.py:140
  337.4 34.7 %collective-permute-start.36 = (bf16[128,2048]{1,0:T(8,128)(2,1)S(1)}, bf16[128,2048]{1,0:T(8,128)(2,1)}, u32[]{:S(2)}, u32[]{:S(2)}) collective-permute-start(bf16[128,2048]{1,0:T(8,128)(2,1)S(1)} %copy-done.41), channel_id=1, source_target_pairs={{0,6},{1,7},{2,0},{3,1},{4,2},{5,3},{6,4},{7,5},{8,14},{9,15},{10,... | collective-permute-start | bytes 1572872 | tf_op jit(solution)/shard_map/ppermute | solution.py:140
  349.3 141.6 %reduce-scatter.9.cloned.1.call-start = ((), (), s32[]{:S(2)}) async-start(), calls=%async_computation.9 | async-start | bytes 1310720 | tf_op jit(solution)/shard_map/reduce_scatter | solution.py:385
  377.8 48.4 %collective-permute-start.37 = (bf16[128,2048]{1,0:T(8,128)(2,1)}, bf16[128,2048]{1,0:T(8,128)(2,1)S(1)}, u32[]{:S(2)}, u32[]{:S(2)}) collective-permute-start(bf16[128,2048]{1,0:T(8,128)(2,1)} %after.28), channel_id=1, source_target_pairs={{0,1},{1,0},{2,3},{3,2},{4,5},{5,4},{6,7},{7,6},{8,9},{9,8},{10,11... | collective-permute-start | bytes 1572872 | tf_op jit(solution)/shard_map/ppermute | solution.py:146
  389.6 36.1 %collective-permute-start.40 = (bf16[128,2048]{1,0:T(8,128)(2,1)}, bf16[128,2048]{1,0:T(8,128)(2,1)S(1)}, u32[]{:S(2)}, u32[]{:S(2)}) collective-permute-start(bf16[128,2048]{1,0:T(8,128)(2,1)} %after.28), channel_id=1, source_target_pairs={{0,4},{1,5},{2,6},{3,7},{4,0},{5,1},{6,2},{7,3},{8,12},{9,13},{10,... | collective-permute-start | bytes 1572872 | tf_op jit(solution)/shard_map/ppermute | solution.py:140
  390.8 34.8 %collective-permute-start.42 = (bf16[128,2048]{1,0:T(8,128)(2,1)}, bf16[128,2048]{1,0:T(8,128)(2,1)S(1)}, u32[]{:S(2)}, u32[]{:S(2)}) collective-permute-start(bf16[128,2048]{1,0:T(8,128)(2,1)} %after.28), channel_id=1, source_target_pairs={{0,6},{1,7},{2,0},{3,1},{4,2},{5,3},{6,4},{7,5},{8,14},{9,15},{10,... | collective-permute-start | bytes 1572872 | tf_op jit(solution)/shard_map/ppermute | solution.py:140
  398.4 38.2 %collective-permute-start.34 = (bf16[512,2048]{1,0:T(8,128)(2,1)}, bf16[512,2048]{1,0:T(8,128)(2,1)}, u32[]{:S(2)}, u32[]{:S(2)}) collective-permute-start(bf16[512,2048]{1,0:T(8,128)(2,1)} %convolution_convert_fusion.3), channel_id=1, source_target_pairs={{0,1},{1,0},{2,3},{3,2},{4,5},{5,4},{6,7},{7,6},{8,9},{9,8},{10,11... | collective-permute-start | bytes 6291464 | tf_op jit(solution)/shard_map/ppermute | solution.py:146
  432.6 125.4 %reduce-scatter.11.cloned.1.call-start = ((), (), s32[]{:S(2)}) async-start(), calls=%async_computation.10 | async-start | bytes 3932160 | tf_op jit(solution)/shard_map/reduce_scatter | solution.py:385
  439.4 36.3 %collective-permute-start.44 = (bf16[128,2048]{1,0:T(8,128)(2,1)}, bf16[128,2048]{1,0:T(8,128)(2,1)}, u32[]{:S(2)}, u32[]{:S(2)}) collective-permute-start(bf16[128,2048]{1,0:T(8,128)(2,1)} %after.29), channel_id=1, source_target_pairs={{0,2},{1,3},{2,4},{3,5},{4,6},{5,7},{6,0},{7,1},{8,10},{9,11},{10,... | collective-permute-start | bytes 1572872 | tf_op jit(solution)/shard_map/ppermute | solution.py:140
  450.3 36.9 %collective-permute-start.45 = (bf16[128,2048]{1,0:T(8,128)(2,1)}, bf16[128,2048]{1,0:T(8,128)(2,1)}, u32[]{:S(2)}, u32[]{:S(2)}) collective-permute-start(bf16[128,2048]{1,0:T(8,128)(2,1)} %after.32), channel_id=1, source_target_pairs={{0,4},{1,5},{2,6},{3,7},{4,0},{5,1},{6,2},{7,3},{8,12},{9,13},{10,... | collective-permute-start | bytes 1572872 | tf_op jit(solution)/shard_map/ppermute | solution.py:140
  452.6 34.6 %collective-permute-start.46 = (bf16[128,2048]{1,0:T(8,128)(2,1)}, bf16[128,2048]{1,0:T(8,128)(2,1)}, u32[]{:S(2)}, u32[]{:S(2)}) collective-permute-start(bf16[128,2048]{1,0:T(8,128)(2,1)} %after.34), channel_id=1, source_target_pairs={{0,6},{1,7},{2,0},{3,1},{4,2},{5,3},{6,4},{7,5},{8,14},{9,15},{10,... | collective-permute-start | bytes 1572872 | tf_op jit(solution)/shard_map/ppermute | solution.py:140
  510.5 34.6 %collective-permute-start.49 = (bf16[128,2048]{1,0:T(8,128)(2,1)S(1)}, bf16[128,2048]{1,0:T(8,128)(2,1)S(1)}, u32[]{:S(2)}, u32[]{:S(2)}) collective-permute-start(bf16[128,2048]{1,0:T(8,128)(2,1)S(1)} %get-tuple-element.82), channel_id=1, source_target_pairs={{0,4},{1,5},{2,6},{3,7},{4,0},{5,1},{6,2},{7,3},{8,12},{9,13},{10,... | collective-permute-start | bytes 1572872 | tf_op jit(solution)/shard_map/ppermute | solution.py:140
  511.1 34.0 %collective-permute-start.50 = (bf16[128,2048]{1,0:T(8,128)(2,1)S(1)}, bf16[128,2048]{1,0:T(8,128)(2,1)S(1)}, u32[]{:S(2)}, u32[]{:S(2)}) collective-permute-start(bf16[128,2048]{1,0:T(8,128)(2,1)S(1)} %get-tuple-element.81), channel_id=1, source_target_pairs={{0,6},{1,7},{2,0},{3,1},{4,2},{5,3},{6,4},{7,5},{8,14},{9,15},{10,... | collective-permute-start | bytes 1572872 | tf_op jit(solution)/shard_map/ppermute | solution.py:140
  580.8 48.8 %collective-permute-start.56 = (bf16[2,80,1792]{2,1,0:T(8,128)(2,1)}, bf16[2,80,1792]{2,1,0:T(8,128)(2,1)}, u32[]{:S(2)}, u32[]{:S(2)}) collective-permute-start(bf16[2,80,1792]{2,1,0:T(8,128)(2,1)} %pad_maximum_fusion.2), channel_id=1, source_target_pairs={{0,4},{1,5},{2,6},{3,7},{4,0},{5,1},{6,2},{7,3},{8,12},{9,13},{10,... | collective-permute-start | bytes 1720328 | tf_op jit(solution)/shard_map/ppermute | solution.py:140
  581.7 47.9 %collective-permute-start.55 = (bf16[2,80,1792]{2,1,0:T(8,128)(2,1)}, bf16[2,80,1792]{2,1,0:T(8,128)(2,1)}, u32[]{:S(2)}, u32[]{:S(2)}) collective-permute-start(bf16[2,80,1792]{2,1,0:T(8,128)(2,1)} %pad_maximum_fusion.1), channel_id=1, source_target_pairs={{0,2},{1,3},{2,4},{3,5},{4,6},{5,7},{6,0},{7,1},{8,10},{9,11},{10,... | collective-permute-start | bytes 1720328 | tf_op jit(solution)/shard_map/ppermute | solution.py:140
  (105 other events, 1940.1 us)
Sparse Core Ops, SparseCore 0:
  9.7 70.7 all-gather.11
  87.7 45.3 all-gather.5
  164.2 53.4 all-gather.7
  219.4 52.6 all-gather.9
  323.7 62.7 reduce-scatter.6
  389.6 52.6 reduce-scatter.4
  445.3 27.6 reduce-scatter.8
  476.3 43.9 reduce-scatter.10

commit v3 on v2

--- a/solution.py
+++ b/solution.py
@@ -131,6 +131,58 @@
     )(qkv, grads, log_total, mixed, seg_col, seg_row, *earlier)
 
 
+def feed_kernel(normed_ref, grad_ref, up_ref, bias_ref, down_ref, hidden_ref, pre_ref, sum_ref):
+    block = 2 * QUERY_BLOCK
+    total = jnp.zeros(sum_ref.shape, F32)
+    down = jnp.transpose(down_ref[...])
+    for low in range(0, normed_ref.shape[0], block):
+        rows = slice(low, low + block)
+        u = dot(normed_ref[rows, :], up_ref[...]) + bias_ref[...]
+        grad_hidden = dot(grad_ref[rows, :], down)
+        square = u * u
+        bend = jnp.tanh(u * (0.7978845608028654 + (0.7978845608028654 * 0.044715) * square))
+        half = 0.5 + 0.5 * bend
+        hidden_ref[rows, :] = (u * half).astype(BF16)
+        slope = half + u * (half * (1.0 - bend)) * (
+            0.7978845608028654 + (3.0 * 0.7978845608028654 * 0.044715) * square
+        )
+        grad_pre = (grad_hidden * slope).astype(BF16)
+        pre_ref[rows, :] = grad_pre
+        total = total + jnp.sum(grad_pre.astype(F32), axis=0, keepdims=True)
+    sum_ref[...] = total
+
+
+def feed_forward(normed, grad, w_up, bias, w_down):
+    rows, width = normed.shape
+    units = w_up.shape[1]
+    tile = min(units, 256)
+    whole = pl.BlockSpec((rows, width), lambda i: (0, 0))
+    column = pl.BlockSpec((rows, tile), lambda i: (0, i))
+    line = pl.BlockSpec((1, tile), lambda i: (0, i))
+    return pl.pallas_call(
+        feed_kernel,
+        grid=(units // tile,),
+        out_shape=(
+            jax.ShapeDtypeStruct((rows, units), BF16),
+            jax.ShapeDtypeStruct((rows, units), BF16),
+            jax.ShapeDtypeStruct((1, units), F32),
+        ),
+        in_specs=[
+            whole,
+            whole,
+            pl.BlockSpec((width, tile), lambda i: (0, i)),
+            line,
+            pl.BlockSpec((tile, width), lambda i: (i, 0)),
+        ],
+        out_specs=(column, column, line),
+        compiler_params=pltpu.CompilerParams(vmem_limit_bytes=56 * 2**20),
+        cost_estimate=pl.CostEstimate(
+            flops=4 * rows * width * units, bytes_accessed=4 * rows * width, transcendentals=rows * units
+        ),
+        name="feed_forward",
+    )(normed, grad, w_up, bias, w_down)
+
+
 def chips():
     return lax.axis_size("ctx") // 2
 
@@ -234,7 +286,7 @@
 def pack_rows(arrays, more, height):
     count = chips()
     width = sum(item.shape[1] for item in arrays)
-    below = more.shape[1]
+    total = width + more.shape[2]
 
     def kernel(at_ref, *refs):
         ins, outs = refs[: len(arrays)], refs[-(count + 1) :]
@@ -246,13 +298,13 @@
                 end = start + ref.shape[1]
                 mine = pl.ds(pl.multiple_of((base + core) * height, height), height)
                 other = pl.ds(pl.multiple_of((base + 1 - core) * height, height), height)
-                outs[k][:height, start:end] = ref[mine, :]
-                outs[count][k, :height, start:end] = ref[other, :]
+                outs[k][:, start:end] = ref[mine, :]
+                outs[count][k, :, start:end] = ref[other, :]
                 start = end
-            outs[k][height:, :] = refs[len(arrays)][base + core]
-            outs[count][k, height:, :] = refs[len(arrays)][base + 1 - core]
-
-    block_shape = jax.ShapeDtypeStruct((height + below, width), BF16)
+            outs[k][:, width:] = refs[len(arrays)][base + core]
+            outs[count][k, :, width:] = refs[len(arrays)][base + 1 - core]
+
+    block_shape = jax.ShapeDtypeStruct((height, total), BF16)
     return pl.pallas_call(
         kernel,
         out_shape=[block_shape] * count + [jax.ShapeDtypeStruct((count,) + block_shape.shape, BF16)],
@@ -301,9 +353,9 @@
     )(where_am_i(), *got, *earlier)
 
 
-def unpack_to_columns(got, r, cuts):
-    count = chips()
-    height, total = got[0].shape[1:]
+def unpack_to_columns(got, cuts, lengths):
+    count = chips()
+    r, total = got[0].shape[1:]
 
     def kernel(at_ref, *refs):
         ins, outs, held = refs[:count], refs[count:-1], refs[-1]
@@ -311,24 +363,32 @@
             for side in range(2):
                 held[source_index(at_ref, k, side, count)] = ins[k][side]
         for j in range(2 * count):
-            block = held[j, :r, :].astype(F32)
+            block = held[j].astype(F32)
             start = 0
             for out, (lead, width) in zip(outs, cuts):
                 for a in range(lead):
                     column = (a * 2 * count + j) * width
                     out[:, column : column + width] = block[:, start : start + width]
                     start += width
-        below = held[0, r:, :].astype(F32)
+        added = held[0, :, total - 128 :].astype(F32)
         for j in range(1, 2 * count):
-            below = below + held[j, r:, :].astype(F32)
-        outs[-1][...] = jnp.sum(below, axis=0, keepdims=True)
+            added = added + held[j, :, total - 128 :].astype(F32)
+        lines = jnp.transpose(added)
+        columns = sum(lengths) // r
+        at = 0
+        for out, length in zip(outs[len(cuts) :], lengths):
+            parts = [
+                lines[i : i + 1, :] + lines[columns + i : columns + i + 1, :] for i in range(at, at + length // r)
+            ]
+            out[...] = parts[0] if len(parts) == 1 else jnp.concatenate(parts, axis=1)
+            at += length // r
 
     return pl.pallas_call(
         kernel,
         out_shape=[jax.ShapeDtypeStruct((r, 2 * count * lead * width), F32) for lead, width in cuts]
-        + [jax.ShapeDtypeStruct((1, total), F32)],
+        + [jax.ShapeDtypeStruct((1, length), F32) for length in lengths],
         in_specs=[pl.BlockSpec(memory_space=pltpu.SMEM)] + [pl.BlockSpec(memory_space=pltpu.VMEM)] * count,
-        scratch_shapes=[pltpu.VMEM((2 * count, height, total), BF16)],
+        scratch_shapes=[pltpu.VMEM((2 * count, r, total), BF16)],
         name="unpack_to_columns",
     )(where_am_i(), *got)
 
@@ -424,16 +484,6 @@
         - jnp.mean(scaled, axis=-1, keepdims=True)
         - standard * jnp.mean(scaled * standard, axis=-1, keepdims=True)
     ) * factor
-
-
-def smooth(pre_act):
-    return jax.nn.gelu(pre_act, approximate=True)
-
-
-def smooth_slope(u):
-    inner = 0.7978845608028654 * (u + 0.044715 * u * u * u)
-    bend = jnp.tanh(inner)
-    return 0.5 * (1.0 + bend) + 0.5 * u * (1.0 - bend * bend) * 0.7978845608028654 * (1.0 + 3.0 * 0.044715 * u * u)
 
 
 def local(
@@ -516,12 +566,8 @@
     standard_two, factor_two = standardize(middle)
     normed_two = (standard_two * gain_two + bias_two).astype(BF16)
     normed_two_all = gather_ctx(after(normed_two, cost=0))[0].reshape(S, D)
-    pre_act = dot(normed_two_all, w_up) + bias_up
-    hidden = smooth(pre_act).astype(BF16)
-
     grad_ffn = (active_row[:, None] * g_all).astype(BF16)
-    grad_hidden = dot(grad_ffn, w_down, NT)
-    grad_pre = (grad_hidden * smooth_slope(pre_act)).astype(BF16)
+    hidden, grad_pre, grad_up_sum = feed_forward(normed_two_all, grad_ffn, w_up, bias_up.reshape(1, N * f), w_down)
     sums_two = chip_sums(grad_pre, w_up, NT)
     grad_normed_two, begun_two = add_over_chips(sums_two)
     hidden = after(hidden, sums_two[0])
@@ -550,14 +596,15 @@
     grad_qkv_part = dot(normed_one, grad_qkv, TN).astype(BF16)
     feed, _ = add_over_chips([after(item, grad_branch_all) for item in feed_sums[:-1]] + feed_sums[-1:], (grad_qkv,))
     sums_one = chip_sums(grad_qkv, w_qkv, NT, (grad_qkv_part, feed, grad_out_w))
-    grad_normed_one, _ = add_over_chips(sums_one)
+    grad_normed_one, begun_one = add_over_chips(sums_one)
     grad_normed_one = after(grad_normed_one, cost=0)
     layer_out = (middle + active_own * (feed + bias_down)).astype(BF16)[None]
     standard_in, factor_in = standardize(inputs)
     grad_in = (grad_middle + norm_back(grad_normed_one, gain_one, standard_in, factor_in)).astype(BF16)[None]
 
-    grad_gain_one = jnp.sum(grad_normed_one * standard_in, axis=0)
-    grad_bias_one = jnp.sum(grad_normed_one, axis=0)
+    partial_one = dot(after(grad_qkv, begun_one), w_qkv, NT)
+    grad_gain_one = jnp.sum(partial_one * standard_one, axis=0)
+    grad_bias_one = jnp.sum(partial_one, axis=0)
     grad_gain_two = jnp.sum(grad_normed_two * standard_two, axis=0)
     grad_bias_two = jnp.sum(grad_normed_two, axis=0)
     ctx_index = lax.broadcasted_iota(jnp.int32, (1, T, 1), 1)
@@ -565,7 +612,6 @@
     grad_bias_qkv = jnp.sum(grad_qkv.astype(F32), axis=0)
     grad_out_sum = jnp.sum(grad_branch.astype(F32), axis=0)
     grad_down_sum = jnp.sum((active_own * grad_res), axis=0)
-    grad_up_sum = jnp.sum(grad_pre.astype(F32), axis=0)
     features = jnp.stack(
         [
             grad_gain_one,
@@ -585,15 +631,13 @@
     sums = jnp.concatenate([features, units], axis=2).reshape(N, T * (8 * r + f))
     sums = reduce_dp_small(sums).reshape(T, 8 * r + f)
     grad_qkv_mine = scatter_dp(grad_qkv_part)
+    sums = sums.reshape(T, 8 + f // r, r).transpose(0, 2, 1)
     coarse = sums.astype(BF16)
     fine = (sums - coarse.astype(F32)).astype(BF16)
-    more = jnp.stack([coarse, fine], axis=1)
-    more = jnp.pad(more, ((0, 0), (0, 14), (0, 3 * L + N * f - more.shape[2])))
+    more = jnp.pad(jnp.concatenate([coarse, fine], axis=2), ((0, 0), (0, 0), (0, 128 - 2 * sums.shape[2])))
     grad_got = exchange_ctx(pack_rows([after(grad_qkv_mine, grad_normed_one), grad_up_mine], more, r))
-    grad_q, grad_k, grad_v, grad_up, sums = unpack_to_columns(grad_got, r, [(A, B)] * 3 + [(N, f)])
-    sums = sums[0, : 8 * r + f]
-    begun_one = grad_got[0]
-    shard = lambda i: sums[i * r : (i + 1) * r]
+    grad_q, grad_k, grad_v, grad_up, *lines = unpack_to_columns(grad_got, [(A, B)] * 3 + [(N, f)], [r] * 8 + [f])
+    shard = lambda i: lines[i].reshape(-1)
     return (
         layer_out,
         grad_in,
@@ -609,8 +653,8 @@
         shard(5),
         shard(6),
         grad_up,
-        sums[8 * r :],
-        after(grad_down, begun_one).astype(F32),
+        shard(8),
+        after(grad_down, grad_got[0]).astype(F32),
         shard(7),
     )
 

time: 647 us -> 623 us (0.963)
  waiting for transfers between devices: 262 us -> 241 us
  matrix products: 83.9 us -> 66 us
  Pallas kernels: 33.2 us -> 49 us
  starting transfers between devices: 138 us -> 127 us
    ppermute x30, waiting for transfers between devices: 246 us -> 228 us  [turn(): lax.ppermute(value, 'ctx', [(2 * s + core, 2 * ((s + k) % count) + core)...]
    dot_general x16 -> x15, matrix products: 83.9 us -> 66 us  [dot(): return lax.dot_general(left, right, dims, preferred_element_type=F32)]
    pallas_call x0 -> x1, Pallas kernels: none -> 16.3 us  [feed_forward(): pl.pallas_call(feed_kernel, grid=(units // tile,), out_shape=(jax.ShapeDt...]
    ppermute x30, starting transfers between devices: 123 us -> 111 us  [turn(): lax.ppermute(value, 'ctx', [(2 * s + core, 2 * ((s + k) % count) + core)...]
    unnamed x146 -> x170, local copies, waits for them, and re-layouts: 20 us -> 20 us
  transfers between devices with their start and end apart: 66 -> 66, of which waited for: 24 -> 21; matrix products, arithmetic and copies ran while one was open for 23% -> 24% of each run, Pallas kernels for 3% -> 3%
where the time goes in v3:
time: 623 us; the launch traced here: 614 us
  waiting for transfers between devices  241 us (39%)
  starting transfers between devices  127 us (20%)
  matrix products  66 us (11%)
  local copies, waits for them, and re-layouts  57.4 us (9%)
  other arithmetic  57 us (9%)
  Pallas kernels  49 us (8%)
  between operations  16.8 us (3%)
    ppermute x30, waiting for transfers between devices, turn(): lax.ppermute(value, 'ctx', [(2 * s + core, 2 * ((s + k) % count) + core)...  228 us
    ppermute x30, starting transfers between devices, turn(): lax.ppermute(value, 'ctx', [(2 * s + core, 2 * ((s + k) % count) + core)...  111 us
    dot_general x15, matrix products, dot(): return lax.dot_general(left, right, dims, preferred_element_type=F32)  66 us
    unnamed x170, local copies, waits for them, and re-layouts  20 us
    pallas_call x1, Pallas kernels, feed_forward(): pl.pallas_call(feed_kernel, grid=(units // tile,), out_shape=(jax.ShapeDt...  16.3 us
  transfers between devices with their start and end apart: 66, of which 21 were waited for; matrix products, arithmetic and copies ran while one was open for 24% of the time, Pallas kernels for 3%

profile of v3, /device:TPU:0, one launch (start us, length us, event | category | flops | bytes accessed | tf_op | source)
XLA Modules:
  0.0 614.0 jit_solution(4670685096167702321)
XLA Ops:
  27.4 4.2 collective-permute-start.3
  33.6 12.8 %collective-permute-done.3.refs_3_ = bf16[2,80,768]{2,1,0:T(8,128)(2,1)S(1)} collective-permute-done((bf16[2,80,768]{2,1,0:T(8,128)(2,1)S(1)}, bf16[2,80,768]{2,1,0:T(8,128)(2,1)S(1)}, u32[]{:S(2)}, u32[]{:S(2)}) %collective-permute-start.3) | collective-permute-done | bytes 245792 | tf_op jit(solution)/shard_map/ppermute | solution.py:192
  46.4 30.2 %collective-permute-done.2.refs_2_ = bf16[2,80,768]{2,1,0:T(8,128)(2,1)S(1)} collective-permute-done((bf16[2,80,768]{2,1,0:T(8,128)(2,1)S(1)}, bf16[2,80,768]{2,1,0:T(8,128)(2,1)S(1)}, u32[]{:S(2)}, u32[]{:S(2)}) %collective-permute-start.2) | collective-permute-done | bytes 245792 | tf_op jit(solution)/shard_map/ppermute | solution.py:192
  107.8 4.7 fusion.5.refs_0_
  113.8 9.4 %collective-permute-done.13 = bf16[128,2048]{1,0:T(8,128)(2,1)S(1)} collective-permute-done((bf16[128,2048]{1,0:T(8,128)(2,1)S(1)}, bf16[128,2048]{1,0:T(8,128)(2,1)S(1)}, u32[]{:S(2)}, u32[]{:S(2)}) %collective-permute-start.13) | collective-permute-done | bytes 524320 | tf_op jit(solution)/shard_map/ppermute | solution.py:192
  128.2 10.2 %collective-permute-start.18 = (bf16[2,64,1024]{2,1,0:T(8,128)(2,1)}, bf16[2,64,1024]{2,1,0:T(8,128)(2,1)}, u32[]{:S(2)}, u32[]{:S(2)}) collective-permute-start(bf16[2,64,1024]{2,1,0:T(8,128)(2,1)} %pad_maximum_fusion.5), channel_id=1, source_target_pairs={{0,2},{1,3},{2,4},{3,5},{4,6},{5,7},{6,0},{7,1},{8,10},{9,11},{10,... | collective-permute-start | bytes 786440 | tf_op jit(solution)/shard_map/ppermute | solution.py:192
  149.0 6.6 %add_convert_fusion.refs_0_.refs_1_ = bf16[1024,768]{1,0:T(8,128)(2,1)S(1)} fusion(bf16[1024,2048]{1,0:T(8,128)(2,1)} %after.22, bf16[2048,768]{1,0:T(8,128)(2,1)} %all-gather.6.cloned.1.call-done, f32[768]{0:T(1024)S(1)} %pad_maximum_fusion.13), kind=kOutput, calls=%fused_computation.14 | convolution fusion | flops 3222798336 | bytes 8915968 | tf_op jit(solution)/shard_map/dot_general | solution.py:24
  155.6 5.2 attention_forward.1
  180.8 10.8 %collective-permute-done.22 = bf16[128,2048]{1,0:T(8,128)(2,1)S(1)} collective-permute-done((bf16[128,2048]{1,0:T(8,128)(2,1)}, bf16[128,2048]{1,0:T(8,128)(2,1)S(1)}, u32[]{:S(2)}, u32[]{:S(2)}) %collective-permute-start.22) | collective-permute-done | bytes 524320 | tf_op jit(solution)/shard_map/ppermute | solution.py:192
  191.6 21.7 %collective-permute-done.23 = bf16[128,2048]{1,0:T(8,128)(2,1)S(1)} collective-permute-done((bf16[128,2048]{1,0:T(8,128)(2,1)S(1)}, bf16[128,2048]{1,0:T(8,128)(2,1)S(1)}, u32[]{:S(2)}, u32[]{:S(2)}) %collective-permute-start.23) | collective-permute-done | bytes 524320 | tf_op jit(solution)/shard_map/ppermute | solution.py:192
  217.2 12.1 %collective-permute-start.26 = (bf16[128,2048]{1,0:T(8,128)(2,1)}, bf16[128,2048]{1,0:T(8,128)(2,1)S(1)}, u32[]{:S(2)}, u32[]{:S(2)}) collective-permute-start(bf16[128,2048]{1,0:T(8,128)(2,1)} %after.25), channel_id=1, source_target_pairs={{0,2},{1,3},{2,4},{3,5},{4,6},{5,7},{6,0},{7,1},{8,10},{9,11},{10,... | collective-permute-start | bytes 1572872 | tf_op jit(solution)/shard_map/ppermute | solution.py:192
  231.8 4.6 broadcast_multiply_fusion.grad_ref
  243.6 22.3 %collective-permute-done.28 = bf16[128,2048]{1,0:T(8,128)(2,1)S(1)} collective-permute-done((bf16[128,2048]{1,0:T(8,128)(2,1)}, bf16[128,2048]{1,0:T(8,128)(2,1)S(1)}, u32[]{:S(2)}, u32[]{:S(2)}) %collective-permute-start.28) | collective-permute-done | bytes 524320 | tf_op jit(solution)/shard_map/ppermute | solution.py:192
  272.3 16.3 %feed_forward.1 = (bf16[1024,1024]{1,0:T(8,128)(2,1)}, bf16[1024,1024]{1,0:T(8,128)(2,1)}, f32[1,1024]{1,0:T(1,128)}) custom-call(bf16[1024,2048]{1,0:T(8,128)(2,1)} %bitcast.60.normed_ref.refs_0_, bf16[1024,2048]{1,0:T(8,128)(2,1)} %broadcast_multiply_fusion.grad_ref, bf16[2048,1024]{1,0:T(8,128)(2,1)} %all-gather.8.cloned.1.call-done.up_ref, ...), custom_call_target="tpu_custom_call" | custom-call | flops 8589934592 | bytes 8388608 | tf_op jit(solution)/shard_map/feed_forward/pallas_call | solution.py:162
  301.7 8.4 %convolution_convert_fusion = bf16[2048,1024]{1,0:T(8,128)(2,1)} fusion(bf16[1024,2048]{1,0:T(8,128)(2,1)} %after.31, bf16[1024,1024]{1,0:T(8,128)(2,1)S(1)} %copy-done.37), kind=kOutput, calls=%fused_computation.10 | convolution fusion | flops 4297064448 | bytes 10485760 | tf_op jit(solution)/shard_map/dot_general | solution.py:24
  311.2 11.7 %collective-permute-start.33 = (bf16[128,2048]{1,0:T(8,128)(2,1)S(1)}, bf16[128,2048]{1,0:T(8,128)(2,1)S(1)}, u32[]{:S(2)}, u32[]{:S(2)}) collective-permute-start(bf16[128,2048]{1,0:T(8,128)(2,1)S(1)} %copy-done.25), channel_id=1, source_target_pairs={{0,2},{1,3},{2,4},{3,5},{4,6},{5,7},{6,0},{7,1},{8,10},{9,11},{10,... | collective-permute-start | bytes 1572872 | tf_op jit(solution)/shard_map/ppermute | solution.py:192
  325.4 10.1 %convolution_convert_fusion.1 = bf16[1024,2048]{1,0:T(8,128)(2,1)} fusion(bf16[1024,1024]{1,0:T(8,128)(2,1)} %after.27.refs_0_, bf16[1024,2048]{1,0:T(8,128)(2,1)} %broadcast_multiply_fusion.grad_ref), kind=kOutput, calls=%fused_computation.11 | convolution fusion | flops 4297064448 | bytes 10485760 | tf_op jit(solution)/shard_map/dot_general | solution.py:24
  336.4 22.4 %collective-permute-done.35 = bf16[128,2048]{1,0:T(8,128)(2,1)} collective-permute-done((bf16[128,2048]{1,0:T(8,128)(2,1)}, bf16[128,2048]{1,0:T(8,128)(2,1)}, u32[]{:S(2)}, u32[]{:S(2)}) %collective-permute-start.35) | collective-permute-done | bytes 524320 | tf_op jit(solution)/shard_map/ppermute | solution.py:192
  364.4 11.8 %collective-permute-start.38 = (bf16[128,2048]{1,0:T(8,128)(2,1)}, bf16[128,2048]{1,0:T(8,128)(2,1)S(1)}, u32[]{:S(2)}, u32[]{:S(2)}) collective-permute-start(bf16[128,2048]{1,0:T(8,128)(2,1)} %after.29), channel_id=1, source_target_pairs={{0,2},{1,3},{2,4},{3,5},{4,6},{5,7},{6,0},{7,1},{8,10},{9,11},{10,... | collective-permute-start | bytes 1572872 | tf_op jit(solution)/shard_map/ppermute | solution.py:192
  386.1 4.4 fusion.62
  390.5 21.7 %collective-permute-done.40 = bf16[128,2048]{1,0:T(8,128)(2,1)S(1)} collective-permute-done((bf16[128,2048]{1,0:T(8,128)(2,1)}, bf16[128,2048]{1,0:T(8,128)(2,1)S(1)}, u32[]{:S(2)}, u32[]{:S(2)}) %collective-permute-start.40) | collective-permute-done | bytes 524320 | tf_op jit(solution)/shard_map/ppermute | solution.py:192
  426.0 10.8 %collective-permute-start.44 = (bf16[128,2048]{1,0:T(8,128)(2,1)}, bf16[128,2048]{1,0:T(8,128)(2,1)}, u32[]{:S(2)}, u32[]{:S(2)}) collective-permute-start(bf16[128,2048]{1,0:T(8,128)(2,1)} %after.30), channel_id=1, source_target_pairs={{0,2},{1,3},{2,4},{3,5},{4,6},{5,7},{6,0},{7,1},{8,10},{9,11},{10,... | collective-permute-start | bytes 1572872 | tf_op jit(solution)/shard_map/ppermute | solution.py:192
  441.8 10.0 %attention_backward.1.refs_1_.refs_0_ = bf16[1024,768]{1,0:T(8,128)(2,1)S(1)} custom-call(bf16[1024,768]{1,0:T(8,128)(2,1)} %copy-done.6, bf16[1024,256]{1,0:T(8,128)(2,1)S(1)} %convolution_convert_fusion.8.refs_1_, f32[4,1024]{1,0:T(4,128)S(1)} %get-tuple-element.67.refs_2_, bf16[1024,256]{1,0:T(8,128)(2,1)S(1)} %copy-done.5, s32[1024,1]{1,0:T(8,128)S(1)} %copy-done.9, ...), custom_call_target="tpu_custom_call" | custom-call | flops 10485760000 | bytes 3670016 | tf_op jit(solution)/shard_map/attention_backward/pallas_call | solution.py:123
  451.8 5.3 convolution_convert_fusion.2.refs_1_
  457.2 16.7 %collective-permute-done.45.refs_0_ = bf16[128,2048]{1,0:T(8,128)(2,1)} collective-permute-done((bf16[128,2048]{1,0:T(8,128)(2,1)}, bf16[128,2048]{1,0:T(8,128)(2,1)}, u32[]{:S(2)}, u32[]{:S(2)}) %collective-permute-start.45) | collective-permute-done | bytes 524320 | tf_op jit(solution)/shard_map/ppermute | solution.py:192
  488.8 10.7 %collective-permute-start.48 = (bf16[128,2048]{1,0:T(8,128)(2,1)}, bf16[128,2048]{1,0:T(8,128)(2,1)S(1)}, u32[]{:S(2)}, u32[]{:S(2)}) collective-permute-start(bf16[128,2048]{1,0:T(8,128)(2,1)} %get-tuple-element.104), channel_id=1, source_target_pairs={{0,2},{1,3},{2,4},{3,5},{4,6},{5,7},{6,0},{7,1},{8,10},{9,11},{10,... | collective-permute-start | bytes 1572872 | tf_op jit(solution)/shard_map/ppermute | solution.py:192
  503.6 10.0 %collective-permute-done.48.refs_1_ = bf16[128,2048]{1,0:T(8,128)(2,1)S(1)} collective-permute-done((bf16[128,2048]{1,0:T(8,128)(2,1)}, bf16[128,2048]{1,0:T(8,128)(2,1)S(1)}, u32[]{:S(2)}, u32[]{:S(2)}) %collective-permute-start.48) | collective-permute-done | bytes 524320 | tf_op jit(solution)/shard_map/ppermute | solution.py:192
  514.3 7.2 %fusion.122 = (f32[2048]{0:T(1024)S(1)}, f32[2048]{0:T(1024)S(1)}) fusion(f32[1024]{0:T(1024)S(1)} %copy-done.73, f32[1024]{0:T(1024)S(1)} %copy-done.65, bf16[1,1024,2048]{2,1,0:T(8,128)(2,1)} %all-gather.12.cloned.1.call-done, bf16[1024,768]{1,0:T(8,128)(2,1)} %after.40, bf16[2048,768]{1,0:T(8,128)(2,1)} %all-gather.6.cloned.1.call-done), kind=kOutput, calls=%fused_computation.277 | convolution fusion | flops 3233804288 | bytes 8937472 | tf_op jit(solution)/shard_map/dot_general | solution.py:24
  526.7 9.1 %collective-permute-done.49 = bf16[128,2048]{1,0:T(8,128)(2,1)} collective-permute-done((bf16[128,2048]{1,0:T(8,128)(2,1)}, bf16[128,2048]{1,0:T(8,128)(2,1)}, u32[]{:S(2)}, u32[]{:S(2)}) %collective-permute-start.49) | collective-permute-done | bytes 524320 | tf_op jit(solution)/shard_map/ppermute | solution.py:192
  546.5 12.6 %collective-permute-start.57 = (bf16[2,64,1920]{2,1,0:T(8,128)(2,1)}, bf16[2,64,1920]{2,1,0:T(8,128)(2,1)S(1)}, u32[]{:S(2)}, u32[]{:S(2)}) collective-permute-start(bf16[2,64,1920]{2,1,0:T(8,128)(2,1)} %pad_maximum_fusion.3), channel_id=1, source_target_pairs={{0,6},{1,7},{2,0},{3,1},{4,2},{5,3},{6,4},{7,5},{8,14},{9,15},{10,... | collective-permute-start | bytes 1474568 | tf_op jit(solution)/shard_map/ppermute | solution.py:192
  566.2 4.8 collective-permute-done.57.refs_3_
  571.0 31.8 %collective-permute-done.56.refs_2_ = bf16[2,64,1920]{2,1,0:T(8,128)(2,1)} collective-permute-done((bf16[2,64,1920]{2,1,0:T(8,128)(2,1)}, bf16[2,64,1920]{2,1,0:T(8,128)(2,1)}, u32[]{:S(2)}, u32[]{:S(2)}) %collective-permute-start.56) | collective-permute-done | bytes 491552 | tf_op jit(solution)/shard_map/ppermute | solution.py:192
  (468 shorter events, 206.9 us)
Async XLA Ops:
  7.2 73.3 %all-gather.12.cloned.1.call-start = ((), (), s32[]{:S(2)}) async-start(), calls=%async_computation.11 | async-start | bytes 4718592 | tf_op jit(solution)/shard_map/all_gather | solution.py:524
  9.6 139.3 %all-gather.6.cloned.1.call-start = ((), (), s32[]{:S(2)}) async-start(), calls=%async_computation.4 | async-start | bytes 3932160 | tf_op jit(solution)/shard_map/all_gather | solution.py:441
  31.6 44.9 %collective-permute-start.2 = (bf16[2,80,768]{2,1,0:T(8,128)(2,1)S(1)}, bf16[2,80,768]{2,1,0:T(8,128)(2,1)S(1)}, u32[]{:S(2)}, u32[]{:S(2)}) collective-permute-start(bf16[2,80,768]{2,1,0:T(8,128)(2,1)S(1)} %pad_maximum_fusion.10), channel_id=1, source_target_pairs={{0,4},{1,5},{2,6},{3,7},{4,0},{5,1},{6,2},{7,3},{8,12},{9,13},{10,... | collective-permute-start | bytes 737288 | tf_op jit(solution)/shard_map/ppermute | solution.py:192
  31.7 44.8 %collective-permute-start.1 = (bf16[2,80,768]{2,1,0:T(8,128)(2,1)S(1)}, bf16[2,80,768]{2,1,0:T(8,128)(2,1)S(1)}, u32[]{:S(2)}, u32[]{:S(2)}) collective-permute-start(bf16[2,80,768]{2,1,0:T(8,128)(2,1)S(1)} %pad_maximum_fusion.9), channel_id=1, source_target_pairs={{0,2},{1,3},{2,4},{3,5},{4,6},{5,7},{6,0},{7,1},{8,10},{9,11},{10,... | collective-permute-start | bytes 737288 | tf_op jit(solution)/shard_map/ppermute | solution.py:192
  82.8 41.0 %collective-permute-start.10 = (bf16[128,2048]{1,0:T(8,128)(2,1)}, bf16[128,2048]{1,0:T(8,128)(2,1)S(1)}, u32[]{:S(2)}, u32[]{:S(2)}) collective-permute-start(bf16[128,2048]{1,0:T(8,128)(2,1)} %after.21), channel_id=1, source_target_pairs={{0,1},{1,0},{2,3},{3,2},{4,5},{5,4},{6,7},{7,6},{8,9},{9,8},{10,11... | collective-permute-start | bytes 1572872 | tf_op jit(solution)/shard_map/ppermute | solution.py:198
  83.1 29.5 %collective-permute-start.11 = (bf16[128,2048]{1,0:T(8,128)(2,1)}, bf16[128,2048]{1,0:T(8,128)(2,1)S(1)}, u32[]{:S(2)}, u32[]{:S(2)}) collective-permute-start(bf16[128,2048]{1,0:T(8,128)(2,1)} %after.21), channel_id=1, source_target_pairs={{0,2},{1,3},{2,4},{3,5},{4,6},{5,7},{6,0},{7,1},{8,10},{9,11},{10,... | collective-permute-start | bytes 1572872 | tf_op jit(solution)/shard_map/ppermute | solution.py:192
  87.6 184.7 %all-gather.8.cloned.1.call-start = ((), (), s32[]{:S(2)}) async-start(), calls=%async_computation.5 | async-start | bytes 5242880 | tf_op jit(solution)/shard_map/all_gather | solution.py:441
  113.3 29.4 %collective-permute-start.12 = (bf16[128,2048]{1,0:T(8,128)(2,1)}, bf16[128,2048]{1,0:T(8,128)(2,1)S(1)}, u32[]{:S(2)}, u32[]{:S(2)}) collective-permute-start(bf16[128,2048]{1,0:T(8,128)(2,1)} %copy-done.35), channel_id=1, source_target_pairs={{0,1},{1,0},{2,3},{3,2},{4,5},{5,4},{6,7},{7,6},{8,9},{9,8},{10,11... | collective-permute-start | bytes 1572872 | tf_op jit(solution)/shard_map/ppermute | solution.py:198
  128.2 33.4 %collective-permute-start.18 = (bf16[2,64,1024]{2,1,0:T(8,128)(2,1)}, bf16[2,64,1024]{2,1,0:T(8,128)(2,1)}, u32[]{:S(2)}, u32[]{:S(2)}) collective-permute-start(bf16[2,64,1024]{2,1,0:T(8,128)(2,1)} %pad_maximum_fusion.5), channel_id=1, source_target_pairs={{0,2},{1,3},{2,4},{3,5},{4,6},{5,7},{6,0},{7,1},{8,10},{9,11},{10,... | collective-permute-start | bytes 786440 | tf_op jit(solution)/shard_map/ppermute | solution.py:192
  164.0 108.3 %all-gather.10.cloned.1.call-start = ((), (), s32[]{:S(2)}) async-start(), calls=%async_computation.6 | async-start | bytes 5242880 | tf_op jit(solution)/shard_map/all_gather | solution.py:441
  167.5 271.9 %reduce-scatter.7.cloned.1.call-start = ((), (), s32[]{:S(2)}) async-start(), calls=%async_computation.8 | async-start | bytes 5242880 | tf_op jit(solution)/shard_map/reduce_scatter | solution.py:445
  177.6 35.7 %collective-permute-start.23 = (bf16[128,2048]{1,0:T(8,128)(2,1)S(1)}, bf16[128,2048]{1,0:T(8,128)(2,1)S(1)}, u32[]{:S(2)}, u32[]{:S(2)}) collective-permute-start(bf16[128,2048]{1,0:T(8,128)(2,1)S(1)} %get-tuple-element.115), channel_id=1, source_target_pairs={{0,4},{1,5},{2,6},{3,7},{4,0},{5,1},{6,2},{7,3},{8,12},{9,13},{10,... | collective-permute-start | bytes 1572872 | tf_op jit(solution)/shard_map/ppermute | solution.py:192
  178.5 34.8 %collective-permute-start.24 = (bf16[128,2048]{1,0:T(8,128)(2,1)S(1)}, bf16[128,2048]{1,0:T(8,128)(2,1)S(1)}, u32[]{:S(2)}, u32[]{:S(2)}) collective-permute-start(bf16[128,2048]{1,0:T(8,128)(2,1)S(1)} %get-tuple-element.114), channel_id=1, source_target_pairs={{0,6},{1,7},{2,0},{3,1},{4,2},{5,3},{6,4},{7,5},{8,14},{9,15},{10,... | collective-permute-start | bytes 1572872 | tf_op jit(solution)/shard_map/ppermute | solution.py:192
  217.2 49.2 %collective-permute-start.25 = (bf16[128,2048]{1,0:T(8,128)(2,1)}, bf16[128,2048]{1,0:T(8,128)(2,1)S(1)}, u32[]{:S(2)}, u32[]{:S(2)}) collective-permute-start(bf16[128,2048]{1,0:T(8,128)(2,1)} %after.25), channel_id=1, source_target_pairs={{0,1},{1,0},{2,3},{3,2},{4,5},{5,4},{6,7},{7,6},{8,9},{9,8},{10,11... | collective-permute-start | bytes 1572872 | tf_op jit(solution)/shard_map/ppermute | solution.py:198
  229.3 36.5 %collective-permute-start.28 = (bf16[128,2048]{1,0:T(8,128)(2,1)}, bf16[128,2048]{1,0:T(8,128)(2,1)S(1)}, u32[]{:S(2)}, u32[]{:S(2)}) collective-permute-start(bf16[128,2048]{1,0:T(8,128)(2,1)} %after.25), channel_id=1, source_target_pairs={{0,4},{1,5},{2,6},{3,7},{4,0},{5,1},{6,2},{7,3},{8,12},{9,13},{10,... | collective-permute-start | bytes 1572872 | tf_op jit(solution)/shard_map/ppermute | solution.py:192
  231.0 34.8 %collective-permute-start.30 = (bf16[128,2048]{1,0:T(8,128)(2,1)}, bf16[128,2048]{1,0:T(8,128)(2,1)S(1)}, u32[]{:S(2)}, u32[]{:S(2)}) collective-permute-start(bf16[128,2048]{1,0:T(8,128)(2,1)} %after.25), channel_id=1, source_target_pairs={{0,6},{1,7},{2,0},{3,1},{4,2},{5,3},{6,4},{7,5},{8,14},{9,15},{10,... | collective-permute-start | bytes 1572872 | tf_op jit(solution)/shard_map/ppermute | solution.py:192
  310.1 129.2 %reduce-scatter.5.cloned.1.call-start = ((), (), s32[]{:S(2)}) async-start(), calls=%async_computation.7 | async-start | bytes 5242880 | tf_op jit(solution)/shard_map/reduce_scatter | solution.py:445
  322.9 35.9 %collective-permute-start.35 = (bf16[128,2048]{1,0:T(8,128)(2,1)}, bf16[128,2048]{1,0:T(8,128)(2,1)}, u32[]{:S(2)}, u32[]{:S(2)}) collective-permute-start(bf16[128,2048]{1,0:T(8,128)(2,1)} %get-tuple-element.110), channel_id=1, source_target_pairs={{0,4},{1,5},{2,6},{3,7},{4,0},{5,1},{6,2},{7,3},{8,12},{9,13},{10,... | collective-permute-start | bytes 1572872 | tf_op jit(solution)/shard_map/ppermute | solution.py:192
  324.0 34.7 %collective-permute-start.36 = (bf16[128,2048]{1,0:T(8,128)(2,1)S(1)}, bf16[128,2048]{1,0:T(8,128)(2,1)}, u32[]{:S(2)}, u32[]{:S(2)}) collective-permute-start(bf16[128,2048]{1,0:T(8,128)(2,1)S(1)} %copy-done.42), channel_id=1, source_target_pairs={{0,6},{1,7},{2,0},{3,1},{4,2},{5,3},{6,4},{7,5},{8,14},{9,15},{10,... | collective-permute-start | bytes 1572872 | tf_op jit(solution)/shard_map/ppermute | solution.py:192
  335.5 146.2 %reduce-scatter.9.cloned.1.call-start = ((), (), s32[]{:S(2)}) async-start(), calls=%async_computation.9 | async-start | bytes 1310720 | tf_op jit(solution)/shard_map/reduce_scatter | solution.py:445
  364.4 48.3 %collective-permute-start.37 = (bf16[128,2048]{1,0:T(8,128)(2,1)}, bf16[128,2048]{1,0:T(8,128)(2,1)S(1)}, u32[]{:S(2)}, u32[]{:S(2)}) collective-permute-start(bf16[128,2048]{1,0:T(8,128)(2,1)} %after.29), channel_id=1, source_target_pairs={{0,1},{1,0},{2,3},{3,2},{4,5},{5,4},{6,7},{7,6},{8,9},{9,8},{10,11... | collective-permute-start | bytes 1572872 | tf_op jit(solution)/shard_map/ppermute | solution.py:198
  376.2 36.0 %collective-permute-start.40 = (bf16[128,2048]{1,0:T(8,128)(2,1)}, bf16[128,2048]{1,0:T(8,128)(2,1)S(1)}, u32[]{:S(2)}, u32[]{:S(2)}) collective-permute-start(bf16[128,2048]{1,0:T(8,128)(2,1)} %after.29), channel_id=1, source_target_pairs={{0,4},{1,5},{2,6},{3,7},{4,0},{5,1},{6,2},{7,3},{8,12},{9,13},{10,... | collective-permute-start | bytes 1572872 | tf_op jit(solution)/shard_map/ppermute | solution.py:192
  377.3 34.8 %collective-permute-start.42 = (bf16[128,2048]{1,0:T(8,128)(2,1)}, bf16[128,2048]{1,0:T(8,128)(2,1)S(1)}, u32[]{:S(2)}, u32[]{:S(2)}) collective-permute-start(bf16[128,2048]{1,0:T(8,128)(2,1)} %after.29), channel_id=1, source_target_pairs={{0,6},{1,7},{2,0},{3,1},{4,2},{5,3},{6,4},{7,5},{8,14},{9,15},{10,... | collective-permute-start | bytes 1572872 | tf_op jit(solution)/shard_map/ppermute | solution.py:192
  385.0 38.2 %collective-permute-start.34 = (bf16[512,2048]{1,0:T(8,128)(2,1)}, bf16[512,2048]{1,0:T(8,128)(2,1)}, u32[]{:S(2)}, u32[]{:S(2)}) collective-permute-start(bf16[512,2048]{1,0:T(8,128)(2,1)} %convolution_convert_fusion.3), channel_id=1, source_target_pairs={{0,1},{1,0},{2,3},{3,2},{4,5},{5,4},{6,7},{7,6},{8,9},{9,8},{10,11... | collective-permute-start | bytes 6291464 | tf_op jit(solution)/shard_map/ppermute | solution.py:198
  419.2 120.5 %reduce-scatter.11.cloned.1.call-start = ((), (), s32[]{:S(2)}) async-start(), calls=%async_computation.10 | async-start | bytes 3932160 | tf_op jit(solution)/shard_map/reduce_scatter | solution.py:445
  426.0 31.1 %collective-permute-start.44 = (bf16[128,2048]{1,0:T(8,128)(2,1)}, bf16[128,2048]{1,0:T(8,128)(2,1)}, u32[]{:S(2)}, u32[]{:S(2)}) collective-permute-start(bf16[128,2048]{1,0:T(8,128)(2,1)} %after.30), channel_id=1, source_target_pairs={{0,2},{1,3},{2,4},{3,5},{4,6},{5,7},{6,0},{7,1},{8,10},{9,11},{10,... | collective-permute-start | bytes 1572872 | tf_op jit(solution)/shard_map/ppermute | solution.py:192
  436.9 37.0 %collective-permute-start.45 = (bf16[128,2048]{1,0:T(8,128)(2,1)}, bf16[128,2048]{1,0:T(8,128)(2,1)}, u32[]{:S(2)}, u32[]{:S(2)}) collective-permute-start(bf16[128,2048]{1,0:T(8,128)(2,1)} %after.33), channel_id=1, source_target_pairs={{0,4},{1,5},{2,6},{3,7},{4,0},{5,1},{6,2},{7,3},{8,12},{9,13},{10,... | collective-permute-start | bytes 1572872 | tf_op jit(solution)/shard_map/ppermute | solution.py:192
  439.3 35.5 %collective-permute-start.46 = (bf16[128,2048]{1,0:T(8,128)(2,1)}, bf16[128,2048]{1,0:T(8,128)(2,1)}, u32[]{:S(2)}, u32[]{:S(2)}) collective-permute-start(bf16[128,2048]{1,0:T(8,128)(2,1)} %after.35), channel_id=1, source_target_pairs={{0,6},{1,7},{2,0},{3,1},{4,2},{5,3},{6,4},{7,5},{8,14},{9,15},{10,... | collective-permute-start | bytes 1572872 | tf_op jit(solution)/shard_map/ppermute | solution.py:192
  500.1 35.8 %collective-permute-start.49 = (bf16[128,2048]{1,0:T(8,128)(2,1)}, bf16[128,2048]{1,0:T(8,128)(2,1)}, u32[]{:S(2)}, u32[]{:S(2)}) collective-permute-start(bf16[128,2048]{1,0:T(8,128)(2,1)} %get-tuple-element.106), channel_id=1, source_target_pairs={{0,4},{1,5},{2,6},{3,7},{4,0},{5,1},{6,2},{7,3},{8,12},{9,13},{10,... | collective-permute-start | bytes 1572872 | tf_op jit(solution)/shard_map/ppermute | solution.py:192
  501.6 34.2 %collective-permute-start.50 = (bf16[128,2048]{1,0:T(8,128)(2,1)S(1)}, bf16[128,2048]{1,0:T(8,128)(2,1)}, u32[]{:S(2)}, u32[]{:S(2)}) collective-permute-start(bf16[128,2048]{1,0:T(8,128)(2,1)S(1)} %get-tuple-element.105), channel_id=1, source_target_pairs={{0,6},{1,7},{2,0},{3,1},{4,2},{5,3},{6,4},{7,5},{8,14},{9,15},{10,... | collective-permute-start | bytes 1572872 | tf_op jit(solution)/shard_map/ppermute | solution.py:192
  559.9 42.9 %collective-permute-start.56 = (bf16[2,64,1920]{2,1,0:T(8,128)(2,1)}, bf16[2,64,1920]{2,1,0:T(8,128)(2,1)}, u32[]{:S(2)}, u32[]{:S(2)}) collective-permute-start(bf16[2,64,1920]{2,1,0:T(8,128)(2,1)} %pad_maximum_fusion.2), channel_id=1, source_target_pairs={{0,4},{1,5},{2,6},{3,7},{4,0},{5,1},{6,2},{7,3},{8,12},{9,13},{10,... | collective-permute-start | bytes 1474568 | tf_op jit(solution)/shard_map/ppermute | solution.py:192
  561.3 41.5 %collective-permute-start.55 = (bf16[2,64,1920]{2,1,0:T(8,128)(2,1)}, bf16[2,64,1920]{2,1,0:T(8,128)(2,1)}, u32[]{:S(2)}, u32[]{:S(2)}) collective-permute-start(bf16[2,64,1920]{2,1,0:T(8,128)(2,1)} %pad_maximum_fusion.1), channel_id=1, source_target_pairs={{0,2},{1,3},{2,4},{3,5},{4,6},{5,7},{6,0},{7,1},{8,10},{9,11},{10,... | collective-permute-start | bytes 1474568 | tf_op jit(solution)/shard_map/ppermute | solution.py:192
  (117 other events, 1904.3 us)
Sparse Core Ops, SparseCore 0:
  9.7 70.6 all-gather.11
  87.7 45.4 all-gather.5
  164.1 53.5 all-gather.7
  219.4 52.6 all-gather.9
  310.3 62.9 reduce-scatter.6
  376.4 52.6 reduce-scatter.4
  432.0 27.7 reduce-scatter.8
  463.0 43.9 reduce-scatter.10

commit v4 on v3

--- a/solution.py
+++ b/solution.py
@@ -194,6 +194,17 @@
     )
 
 
+FAR = ((0, 2), (1, 3), (2, 0), (3, 1))
+NEAR = ((0, 1), (1, 0), (2, 3), (3, 2))
+MIDDLE = ((1, 2), (2, 1))
+OUT = ((2, 3), (1, 0))
+BACK = ((3, 2), (0, 1))
+
+
+def chip_permute(value, pairs):
+    return lax.ppermute(value, "ctx", [(2 * s + core, 2 * t + core) for s, t in pairs for core in range(2)])
+
+
 def swap(value):
     return lax.ppermute(value, "ctx", [(i, i ^ 1) for i in range(2 * chips())])
 
@@ -221,8 +232,13 @@
 def gather_ctx(block):
     count = chips()
     chip, core = place()
-    same = [block] + [turn(block, k) for k in range(1, count)]
-    chip_of = [(chip + count - k) % count for k in range(count)]
+    if count == 4:
+        far, near, middle = (chip_permute(block, pairs) for pairs in (FAR, NEAR, MIDDLE))
+        last = jnp.where((chip == 0) | (chip == 3), chip_permute(far, OUT), middle)
+        same, chip_of = [block, near, far, last], [chip, chip ^ 1, chip ^ 2, chip ^ 3]
+    else:
+        same = [block] + [turn(block, k) for k in range(1, count)]
+        chip_of = [(chip + count - k) % count for k in range(count)]
     other = [swap(item) for item in same]
     out = jnp.zeros((2 * count,) + block.shape, block.dtype)
     for k in range(count):
@@ -397,7 +413,7 @@
     count = chips()
     chip, core = place()
     pairs = rows.reshape((count, 2, rows.shape[0] // (2 * count), rows.shape[1]))
-    order = [(chip + k) % count for k in range(1, count + 1)]
+    order = [chip ^ (3 - k) for k in range(4)] if count == 4 else [(chip + k) % count for k in range(1, count + 1)]
     turned = [lax.dynamic_index_in_dim(pairs, index, 0, keepdims=False) for index in order]
     pick = lambda which: jnp.concatenate(
         [lax.dynamic_index_in_dim(item, which, 0, keepdims=False) for item in turned], axis=0
@@ -419,6 +435,13 @@
 def add_over_chips(sums, earlier=()):
     count = chips()
     total = sums[-1]
+    if count == 4:
+        ends, middle, near = (chip_permute(*pair) for pair in ((sums[0], BACK), (sums[0], MIDDLE), (sums[2], NEAR)))
+        far = chip_permute((sums[1].astype(F32) + ends.astype(F32)).astype(BF16), FAR)
+        for arrived in (middle, near, far):
+            arrived = after(arrived, *earlier) if earlier else arrived
+            total = total + arrived.astype(F32)
+        return total, near
     for k in range(1, count):
         arrived = turn(sums[k - 1], k)
         arrived = after(arrived, *earlier) if earlier else arrived

time: 623 us -> 627 us (level)
  starting transfers between devices: 127 us -> 74 us
  waiting for transfers between devices: 241 us -> 280 us
  local copies, waits for them, and re-layouts: 57.4 us -> 66.9 us
  Pallas kernels: 49 us -> 57.2 us
    ppermute x0 -> x28, waiting for transfers between devices: none -> 187 us  [chip_permute(): lax.ppermute(value, 'ctx', [(2 * s + core, 2 * t + core) for s, t in pair...]
    ppermute x30 -> x9, waiting for transfers between devices: 228 us -> 80.4 us  [turn(): lax.ppermute(value, 'ctx', [(2 * s + core, 2 * ((s + k) % count) + core)...]
    ppermute x30 -> x9, starting transfers between devices: 111 us -> 11.9 us  [turn(): lax.ppermute(value, 'ctx', [(2 * s + core, 2 * ((s + k) % count) + core)...]
    ppermute x0 -> x28, starting transfers between devices: none -> 46.9 us  [chip_permute(): lax.ppermute(value, 'ctx', [(2 * s + core, 2 * t + core) for s, t in pair...]
    pallas_call x1, Pallas kernels: 16.3 us -> 24.8 us  [feed_forward(): pl.pallas_call(feed_kernel, grid=(units // tile,), out_shape=(jax.ShapeDt...]
    unnamed x170 -> x180, local copies, waits for them, and re-layouts: 20 us -> 28.3 us
  transfers between devices with their start and end apart: 66 -> 73, of which waited for: 21 -> 27; matrix products, arithmetic and copies ran while one was open for 24% -> 24% of each run, Pallas kernels for 3% -> 3%
where the time goes in v4:
time: 627 us; the launch traced here: 619 us
  waiting for transfers between devices  280 us (45%)
  starting transfers between devices  74 us (12%)
  local copies, waits for them, and re-layouts  66.9 us (11%)
  matrix products  66.2 us (11%)
  other arithmetic  58.2 us (9%)
  Pallas kernels  57.2 us (9%)
  between operations  16.6 us (3%)
    ppermute x28, waiting for transfers between devices, chip_permute(): lax.ppermute(value, 'ctx', [(2 * s + core, 2 * t + core) for s, t in pair...  187 us
    ppermute x9, waiting for transfers between devices, turn(): lax.ppermute(value, 'ctx', [(2 * s + core, 2 * ((s + k) % count) + core)...  80.4 us
    dot_general x15, matrix products, dot(): return lax.dot_general(left, right, dims, preferred_element_type=F32)  66.2 us
    ppermute x28, starting transfers between devices, chip_permute(): lax.ppermute(value, 'ctx', [(2 * s + core, 2 * t + core) for s, t in pair...  46.9 us
    unnamed x180, local copies, waits for them, and re-layouts  28.3 us
    pallas_call x1, Pallas kernels, feed_forward(): pl.pallas_call(feed_kernel, grid=(units // tile,), out_shape=(jax.ShapeDt...  24.8 us
  transfers between devices with their start and end apart: 73, of which 27 were waited for; matrix products, arithmetic and copies ran while one was open for 24% of the time, Pallas kernels for 3%

profile of v4, /device:TPU:0, one launch (start us, length us, event | category | flops | bytes accessed | tf_op | source)
XLA Modules:
  0.0 619.2 jit_solution(13460018009647877740)
XLA Ops:
  27.4 4.2 collective-permute-start.3
  33.5 12.8 %collective-permute-done.3.refs_3_ = bf16[2,80,768]{2,1,0:T(8,128)(2,1)S(1)} collective-permute-done((bf16[2,80,768]{2,1,0:T(8,128)(2,1)S(1)}, bf16[2,80,768]{2,1,0:T(8,128)(2,1)S(1)}, u32[]{:S(2)}, u32[]{:S(2)}) %collective-permute-start.3) | collective-permute-done | bytes 245792 | tf_op jit(solution)/shard_map/ppermute | solution.py:192
  46.3 30.2 %collective-permute-done.2.refs_2_ = bf16[2,80,768]{2,1,0:T(8,128)(2,1)S(1)} collective-permute-done((bf16[2,80,768]{2,1,0:T(8,128)(2,1)S(1)}, bf16[2,80,768]{2,1,0:T(8,128)(2,1)S(1)}, u32[]{:S(2)}, u32[]{:S(2)}) %collective-permute-start.2) | collective-permute-done | bytes 245792 | tf_op jit(solution)/shard_map/ppermute | solution.py:192
  106.1 4.7 fusion.5.refs_0_
  112.1 11.3 %collective-permute-done.13 = bf16[128,2048]{1,0:T(8,128)(2,1)S(1)} collective-permute-done((bf16[128,2048]{1,0:T(8,128)(2,1)S(1)}, bf16[128,2048]{1,0:T(8,128)(2,1)S(1)}, u32[]{:S(2)}, u32[]{:S(2)}) %collective-permute-start.13) | collective-permute-done | bytes 524320 | tf_op jit(solution)/shard_map/ppermute | solution.py:205
  130.0 9.6 %collective-permute-done.15 = bf16[128,2048]{1,0:T(8,128)(2,1)S(1)} collective-permute-done((bf16[128,2048]{1,0:T(8,128)(2,1)S(1)}, bf16[128,2048]{1,0:T(8,128)(2,1)S(1)}, u32[]{:S(2)}, u32[]{:S(2)}) %collective-permute-start.15) | collective-permute-done | bytes 524320 | tf_op jit(solution)/shard_map/ppermute | solution.py:205
  146.6 6.6 %add_convert_fusion.refs_0_.refs_1_ = bf16[1024,768]{1,0:T(8,128)(2,1)S(1)} fusion(bf16[1024,2048]{1,0:T(8,128)(2,1)} %after.22, bf16[2048,768]{1,0:T(8,128)(2,1)} %all-gather.6.cloned.1.call-done, f32[768]{0:T(1024)S(1)} %pad_maximum_fusion.13), kind=kOutput, calls=%fused_computation.14 | convolution fusion | flops 3222798336 | bytes 8915968 | tf_op jit(solution)/shard_map/dot_general | solution.py:24
  153.2 5.2 attention_forward.1
  173.8 7.6 %collective-permute-start.25 = (bf16[128,2048]{1,0:T(8,128)(2,1)}, bf16[128,2048]{1,0:T(8,128)(2,1)S(1)}, u32[]{:S(2)}, u32[]{:S(2)}) collective-permute-start(bf16[128,2048]{1,0:T(8,128)(2,1)} %fusion.41), channel_id=1, source_target_pairs={{6,4},{7,5},{0,2},{1,3},{14,12},{15,13},{8,10},{9,11},{22,20},{23,... | collective-permute-start | bytes 1572872 | tf_op jit(solution)/shard_map/ppermute | solution.py:205
  182.4 10.9 %collective-permute-done.25 = bf16[128,2048]{1,0:T(8,128)(2,1)S(1)} collective-permute-done((bf16[128,2048]{1,0:T(8,128)(2,1)}, bf16[128,2048]{1,0:T(8,128)(2,1)S(1)}, u32[]{:S(2)}, u32[]{:S(2)}) %collective-permute-start.25) | collective-permute-done | bytes 524320 | tf_op jit(solution)/shard_map/ppermute | solution.py:205
  197.1 20.6 %collective-permute-done.24 = bf16[128,2048]{1,0:T(8,128)(2,1)S(1)} collective-permute-done((bf16[128,2048]{1,0:T(8,128)(2,1)}, bf16[128,2048]{1,0:T(8,128)(2,1)S(1)}, u32[]{:S(2)}, u32[]{:S(2)}) %collective-permute-start.24) | collective-permute-done | bytes 524320 | tf_op jit(solution)/shard_map/ppermute | solution.py:205
  217.7 4.1 collective-permute-done.26
  231.8 22.1 %collective-permute-done.30 = bf16[128,2048]{1,0:T(8,128)(2,1)S(1)} collective-permute-done((bf16[128,2048]{1,0:T(8,128)(2,1)}, bf16[128,2048]{1,0:T(8,128)(2,1)S(1)}, u32[]{:S(2)}, u32[]{:S(2)}) %collective-permute-start.30) | collective-permute-done | bytes 524320 | tf_op jit(solution)/shard_map/ppermute | solution.py:205
  260.0 10.1 %collective-permute-done.32 = bf16[128,2048]{1,0:T(8,128)(2,1)S(1)} collective-permute-done((bf16[128,2048]{1,0:T(8,128)(2,1)S(1)}, bf16[128,2048]{1,0:T(8,128)(2,1)S(1)}, u32[]{:S(2)}, u32[]{:S(2)}) %collective-permute-start.32) | collective-permute-done | bytes 524320 | tf_op jit(solution)/shard_map/ppermute | solution.py:205
  275.8 24.8 %feed_forward.1 = (bf16[1024,1024]{1,0:T(8,128)(2,1)}, bf16[1024,1024]{1,0:T(8,128)(2,1)}, f32[1,1024]{1,0:T(1,128)}) custom-call(bf16[1024,2048]{1,0:T(8,128)(2,1)} %bitcast.60.normed_ref.refs_0_, bf16[1024,2048]{1,0:T(8,128)(2,1)} %broadcast_multiply_fusion.grad_ref, bf16[2048,1024]{1,0:T(8,128)(2,1)} %all-gather.8.cloned.1.call-done.up_ref, ...), custom_call_target="tpu_custom_call" | custom-call | flops 8589934592 | bytes 8388608 | tf_op jit(solution)/shard_map/feed_forward/pallas_call | solution.py:162
  312.4 9.5 %convolution_convert_fusion = bf16[2048,1024]{1,0:T(8,128)(2,1)} fusion(bf16[1024,2048]{1,0:T(8,128)(2,1)} %after.31, bf16[1024,1024]{1,0:T(8,128)(2,1)} %get-tuple-element.66), kind=kOutput, calls=%fused_computation.10 | convolution fusion | flops 4297064448 | bytes 10485760 | tf_op jit(solution)/shard_map/dot_general | solution.py:24
  328.5 9.6 %collective-permute-done.39 = bf16[128,2048]{1,0:T(8,128)(2,1)S(1)} collective-permute-done((bf16[128,2048]{1,0:T(8,128)(2,1)S(1)}, bf16[128,2048]{1,0:T(8,128)(2,1)S(1)}, u32[]{:S(2)}, u32[]{:S(2)}) %collective-permute-start.39) | collective-permute-done | bytes 524320 | tf_op jit(solution)/shard_map/ppermute | solution.py:205
  344.8 8.7 %convolution_convert_fusion.1 = bf16[1024,2048]{1,0:T(8,128)(2,1)} fusion(bf16[1024,1024]{1,0:T(8,128)(2,1)S(1)} %copy-done.14, bf16[1024,2048]{1,0:T(8,128)(2,1)} %broadcast_multiply_fusion.grad_ref), kind=kOutput, calls=%fused_computation.11 | convolution fusion | flops 4297064448 | bytes 10485760 | tf_op jit(solution)/shard_map/dot_general | solution.py:24
  353.5 13.6 %collective-permute-done.36.refs_1_ = bf16[128,2048]{1,0:T(8,128)(2,1)S(1)} collective-permute-done((bf16[128,2048]{1,0:T(8,128)(2,1)}, bf16[128,2048]{1,0:T(8,128)(2,1)S(1)}, u32[]{:S(2)}, u32[]{:S(2)}) %collective-permute-start.36) | collective-permute-done | bytes 524320 | tf_op jit(solution)/shard_map/ppermute | solution.py:205
  386.2 16.9 %collective-permute-done.44 = bf16[128,2048]{1,0:T(8,128)(2,1)} collective-permute-done((bf16[128,2048]{1,0:T(8,128)(2,1)}, bf16[128,2048]{1,0:T(8,128)(2,1)}, u32[]{:S(2)}, u32[]{:S(2)}) %collective-permute-start.44) | collective-permute-done | bytes 524320 | tf_op jit(solution)/shard_map/ppermute | solution.py:205
  408.4 11.1 %collective-permute-done.46 = bf16[128,2048]{1,0:T(8,128)(2,1)S(1)} collective-permute-done((bf16[128,2048]{1,0:T(8,128)(2,1)}, bf16[128,2048]{1,0:T(8,128)(2,1)S(1)}, u32[]{:S(2)}, u32[]{:S(2)}) %collective-permute-start.46) | collective-permute-done | bytes 524320 | tf_op jit(solution)/shard_map/ppermute | solution.py:205
  431.0 4.5 convolution_convert_fusion.7
  450.4 9.8 %attention_backward.1.refs_1_.refs_0_ = bf16[1024,768]{1,0:T(8,128)(2,1)S(1)} custom-call(bf16[1024,768]{1,0:T(8,128)(2,1)} %copy-done.5, bf16[1024,256]{1,0:T(8,128)(2,1)S(1)} %convolution_convert_fusion.8.refs_1_, f32[4,1024]{1,0:T(4,128)S(1)} %get-tuple-element.67.refs_2_, bf16[1024,256]{1,0:T(8,128)(2,1)S(1)} %copy-done.4, ...), custom_call_target="tpu_custom_call" | custom-call | flops 10485760000 | bytes 3670016 | tf_op jit(solution)/shard_map/attention_backward/pallas_call | solution.py:123
  463.0 13.2 %collective-permute-done.52.refs_0_ = bf16[128,2048]{1,0:T(8,128)(2,1)} collective-permute-done((bf16[128,2048]{1,0:T(8,128)(2,1)}, bf16[128,2048]{1,0:T(8,128)(2,1)}, u32[]{:S(2)}, u32[]{:S(2)}) %collective-permute-start.52) | collective-permute-done | bytes 524320 | tf_op jit(solution)/shard_map/ppermute | solution.py:205
  477.1 5.2 convolution_convert_fusion.6.refs_0_
  485.6 5.1 convolution_convert_fusion.2.refs_1_
  501.9 9.6 %collective-permute-done.56 = bf16[128,2048]{1,0:T(8,128)(2,1)S(1)} collective-permute-done((bf16[128,2048]{1,0:T(8,128)(2,1)S(1)}, bf16[128,2048]{1,0:T(8,128)(2,1)S(1)}, u32[]{:S(2)}, u32[]{:S(2)}) %collective-permute-start.56) | collective-permute-done | bytes 524320 | tf_op jit(solution)/shard_map/ppermute | solution.py:205
  520.2 8.4 %collective-permute-done.55.refs_1_ = bf16[128,2048]{1,0:T(8,128)(2,1)S(1)} collective-permute-done((bf16[128,2048]{1,0:T(8,128)(2,1)S(1)}, bf16[128,2048]{1,0:T(8,128)(2,1)S(1)}, u32[]{:S(2)}, u32[]{:S(2)}) %collective-permute-start.55) | collective-permute-done | bytes 524320 | tf_op jit(solution)/shard_map/ppermute | solution.py:205
  529.4 7.3 %fusion.122 = (f32[2048]{0:T(1024)S(1)}, f32[2048]{0:T(1024)S(1)}) fusion(f32[1024]{0:T(1024)S(1)} %copy-done.79, f32[1024]{0:T(1024)S(1)} %copy-done.71, bf16[1,1024,2048]{2,1,0:T(8,128)(2,1)} %all-gather.12.cloned.1.call-done, bf16[1024,768]{1,0:T(8,128)(2,1)} %after.40, bf16[2048,768]{1,0:T(8,128)(2,1)} %all-gather.6.cloned.1.call-done), kind=kOutput, calls=%fused_computation.284 | convolution fusion | flops 3233804288 | bytes 8937472 | tf_op jit(solution)/shard_map/dot_general | solution.py:24
  541.8 12.2 %collective-permute-done.57 = bf16[128,2048]{1,0:T(8,128)(2,1)} collective-permute-done((bf16[128,2048]{1,0:T(8,128)(2,1)S(1)}, bf16[128,2048]{1,0:T(8,128)(2,1)}, u32[]{:S(2)}, u32[]{:S(2)}) %collective-permute-start.57) | collective-permute-done | bytes 524320 | tf_op jit(solution)/shard_map/ppermute | solution.py:205
  573.7 6.3 %collective-permute-done.64.refs_3_ = bf16[2,64,1920]{2,1,0:T(8,128)(2,1)S(1)} collective-permute-done((bf16[2,64,1920]{2,1,0:T(8,128)(2,1)}, bf16[2,64,1920]{2,1,0:T(8,128)(2,1)S(1)}, u32[]{:S(2)}, u32[]{:S(2)}) %collective-permute-start.64) | collective-permute-done | bytes 491552 | tf_op jit(solution)/shard_map/ppermute | solution.py:192
  580.0 28.2 %collective-permute-done.63.refs_2_ = bf16[2,64,1920]{2,1,0:T(8,128)(2,1)} collective-permute-done((bf16[2,64,1920]{2,1,0:T(8,128)(2,1)}, bf16[2,64,1920]{2,1,0:T(8,128)(2,1)}, u32[]{:S(2)}, u32[]{:S(2)}) %collective-permute-start.63) | collective-permute-done | bytes 491552 | tf_op jit(solution)/shard_map/ppermute | solution.py:192
  (496 shorter events, 238.9 us)
Async XLA Ops:
  7.2 73.3 %all-gather.12.cloned.1.call-start = ((), (), s32[]{:S(2)}) async-start(), calls=%async_computation.11 | async-start | bytes 4718592 | tf_op jit(solution)/shard_map/all_gather | solution.py:547
  9.6 137.0 %all-gather.6.cloned.1.call-start = ((), (), s32[]{:S(2)}) async-start(), calls=%async_computation.4 | async-start | bytes 3932160 | tf_op jit(solution)/shard_map/all_gather | solution.py:464
  31.5 44.9 %collective-permute-start.2 = (bf16[2,80,768]{2,1,0:T(8,128)(2,1)S(1)}, bf16[2,80,768]{2,1,0:T(8,128)(2,1)S(1)}, u32[]{:S(2)}, u32[]{:S(2)}) collective-permute-start(bf16[2,80,768]{2,1,0:T(8,128)(2,1)S(1)} %pad_maximum_fusion.10), channel_id=1, source_target_pairs={{0,4},{1,5},{2,6},{3,7},{4,0},{5,1},{6,2},{7,3},{8,12},{9,13},{10,... | collective-permute-start | bytes 737288 | tf_op jit(solution)/shard_map/ppermute | solution.py:192
  31.7 44.8 %collective-permute-start.1 = (bf16[2,80,768]{2,1,0:T(8,128)(2,1)S(1)}, bf16[2,80,768]{2,1,0:T(8,128)(2,1)S(1)}, u32[]{:S(2)}, u32[]{:S(2)}) collective-permute-start(bf16[2,80,768]{2,1,0:T(8,128)(2,1)S(1)} %pad_maximum_fusion.9), channel_id=1, source_target_pairs={{0,2},{1,3},{2,4},{3,5},{4,6},{5,7},{6,0},{7,1},{8,10},{9,11},{10,... | collective-permute-start | bytes 737288 | tf_op jit(solution)/shard_map/ppermute | solution.py:192
  82.8 40.6 %collective-permute-start.10 = (bf16[128,2048]{1,0:T(8,128)(2,1)}, bf16[128,2048]{1,0:T(8,128)(2,1)S(1)}, u32[]{:S(2)}, u32[]{:S(2)}) collective-permute-start(bf16[128,2048]{1,0:T(8,128)(2,1)} %after.21), channel_id=1, source_target_pairs={{0,1},{1,0},{2,3},{3,2},{4,5},{5,4},{6,7},{7,6},{8,9},{9,8},{10,11... | collective-permute-start | bytes 1572872 | tf_op jit(solution)/shard_map/ppermute | solution.py:209
  83.1 27.7 %collective-permute-start.11 = (bf16[128,2048]{1,0:T(8,128)(2,1)}, bf16[128,2048]{1,0:T(8,128)(2,1)S(1)}, u32[]{:S(2)}, u32[]{:S(2)}) collective-permute-start(bf16[128,2048]{1,0:T(8,128)(2,1)} %after.21), channel_id=1, source_target_pairs={{0,2},{1,3},{2,0},{3,1},{4,6},{5,7},{6,4},{7,5},{8,10},{9,11},{10,... | collective-permute-start | bytes 1572872 | tf_op jit(solution)/shard_map/ppermute | solution.py:205
  87.6 187.2 %all-gather.8.cloned.1.call-start = ((), (), s32[]{:S(2)}) async-start(), calls=%async_computation.5 | async-start | bytes 5242880 | tf_op jit(solution)/shard_map/all_gather | solution.py:464
  96.6 26.8 %collective-permute-start.13 = (bf16[128,2048]{1,0:T(8,128)(2,1)S(1)}, bf16[128,2048]{1,0:T(8,128)(2,1)S(1)}, u32[]{:S(2)}, u32[]{:S(2)}) collective-permute-start(bf16[128,2048]{1,0:T(8,128)(2,1)S(1)} %copy-done.22), channel_id=1, source_target_pairs={{0,4},{1,5},{2,6},{3,7},{4,0},{5,1},{6,2},{7,3},{8,12},{9,13},{10,... | collective-permute-start | bytes 1572872 | tf_op jit(solution)/shard_map/ppermute | solution.py:205
  98.3 31.7 %collective-permute-start.16 = (bf16[128,2048]{1,0:T(8,128)(2,1)S(1)}, bf16[128,2048]{1,0:T(8,128)(2,1)S(1)}, u32[]{:S(2)}, u32[]{:S(2)}) collective-permute-start(bf16[128,2048]{1,0:T(8,128)(2,1)S(1)} %copy-done.22), channel_id=1, source_target_pairs={{2,4},{3,5},{4,2},{5,3},{10,12},{11,13},{12,10},{13,11},{18,20},{1... | collective-permute-start | bytes 1572872 | tf_op jit(solution)/shard_map/ppermute | solution.py:205
  111.6 29.0 %collective-permute-start.18 = (bf16[4,64,1024]{2,1,0:T(8,128)(2,1)}, bf16[4,64,1024]{2,1,0:T(8,128)(2,1)S(1)}, u32[]{:S(2)}, u32[]{:S(2)}) collective-permute-start(bf16[4,64,1024]{2,1,0:T(8,128)(2,1)} %after.23), channel_id=1, source_target_pairs={{0,1},{1,0},{2,3},{3,2},{4,5},{5,4},{6,7},{7,6},{8,9},{9,8},{10,11... | collective-permute-start | bytes 1572872 | tf_op jit(solution)/shard_map/ppermute | solution.py:209
  165.2 110.6 %all-gather.10.cloned.1.call-start = ((), (), s32[]{:S(2)}) async-start(), calls=%async_computation.6 | async-start | bytes 5242880 | tf_op jit(solution)/shard_map/all_gather | solution.py:464
  196.8 251.1 %reduce-scatter.7.cloned.1.call-start = ((), (), s32[]{:S(2)}) async-start(), calls=%async_computation.8 | async-start | bytes 5242880 | tf_op jit(solution)/shard_map/reduce_scatter | solution.py:468
  226.7 29.1 %collective-permute-start.27 = (bf16[128,2048]{1,0:T(8,128)(2,1)}, bf16[128,2048]{1,0:T(8,128)(2,1)S(1)}, u32[]{:S(2)}, u32[]{:S(2)}) collective-permute-start(bf16[128,2048]{1,0:T(8,128)(2,1)} %after.25), channel_id=1, source_target_pairs={{0,1},{1,0},{2,3},{3,2},{4,5},{5,4},{6,7},{7,6},{8,9},{9,8},{10,11... | collective-permute-start | bytes 1572872 | tf_op jit(solution)/shard_map/ppermute | solution.py:209
  226.7 28.5 %collective-permute-start.28 = (bf16[128,2048]{1,0:T(8,128)(2,1)}, bf16[128,2048]{1,0:T(8,128)(2,1)S(1)}, u32[]{:S(2)}, u32[]{:S(2)}) collective-permute-start(bf16[128,2048]{1,0:T(8,128)(2,1)} %after.25), channel_id=1, source_target_pairs={{0,2},{1,3},{2,0},{3,1},{4,6},{5,7},{6,4},{7,5},{8,10},{9,11},{10,... | collective-permute-start | bytes 1572872 | tf_op jit(solution)/shard_map/ppermute | solution.py:205
  226.7 27.2 %collective-permute-start.30 = (bf16[128,2048]{1,0:T(8,128)(2,1)}, bf16[128,2048]{1,0:T(8,128)(2,1)S(1)}, u32[]{:S(2)}, u32[]{:S(2)}) collective-permute-start(bf16[128,2048]{1,0:T(8,128)(2,1)} %after.25), channel_id=1, source_target_pairs={{0,4},{1,5},{2,6},{3,7},{4,0},{5,1},{6,2},{7,3},{8,12},{9,13},{10,... | collective-permute-start | bytes 1572872 | tf_op jit(solution)/shard_map/ppermute | solution.py:205
  227.8 32.2 %collective-permute-start.33 = (bf16[128,2048]{1,0:T(8,128)(2,1)}, bf16[128,2048]{1,0:T(8,128)(2,1)S(1)}, u32[]{:S(2)}, u32[]{:S(2)}) collective-permute-start(bf16[128,2048]{1,0:T(8,128)(2,1)} %after.25), channel_id=1, source_target_pairs={{2,4},{3,5},{4,2},{5,3},{10,12},{11,13},{12,10},{13,11},{18,20},{1... | collective-permute-start | bytes 1572872 | tf_op jit(solution)/shard_map/ppermute | solution.py:205
  322.0 126.0 %reduce-scatter.5.cloned.1.call-start = ((), (), s32[]{:S(2)}) async-start(), calls=%async_computation.7 | async-start | bytes 5242880 | tf_op jit(solution)/shard_map/reduce_scatter | solution.py:468
  327.1 26.5 %collective-permute-start.38 = (bf16[128,2048]{1,0:T(8,128)(2,1)S(1)}, bf16[128,2048]{1,0:T(8,128)(2,1)}, u32[]{:S(2)}, u32[]{:S(2)}) collective-permute-start(bf16[128,2048]{1,0:T(8,128)(2,1)S(1)} %copy-done.23), channel_id=1, source_target_pairs={{2,4},{3,5},{4,2},{5,3},{10,12},{11,13},{12,10},{13,11},{18,20},{1... | collective-permute-start | bytes 1572872 | tf_op jit(solution)/shard_map/ppermute | solution.py:205
  341.4 25.7 %collective-permute-start.36 = (bf16[128,2048]{1,0:T(8,128)(2,1)}, bf16[128,2048]{1,0:T(8,128)(2,1)S(1)}, u32[]{:S(2)}, u32[]{:S(2)}) collective-permute-start(bf16[128,2048]{1,0:T(8,128)(2,1)} %get-tuple-element.116), channel_id=1, source_target_pairs={{0,2},{1,3},{2,0},{3,1},{4,6},{5,7},{6,4},{7,5},{8,10},{9,11},{10,... | collective-permute-start | bytes 1572872 | tf_op jit(solution)/shard_map/ppermute | solution.py:205
  343.9 25.9 %collective-permute-start.40 = (bf16[128,2048]{1,0:T(8,128)(2,1)}, bf16[128,2048]{1,0:T(8,128)(2,1)}, u32[]{:S(2)}, u32[]{:S(2)}) collective-permute-start(bf16[128,2048]{1,0:T(8,128)(2,1)} %get-tuple-element.115), channel_id=1, source_target_pairs={{0,4},{1,5},{2,6},{3,7},{4,0},{5,1},{6,2},{7,3},{8,12},{9,13},{10,... | collective-permute-start | bytes 1572872 | tf_op jit(solution)/shard_map/ppermute | solution.py:205
  353.5 137.3 %reduce-scatter.9.cloned.1.call-start = ((), (), s32[]{:S(2)}) async-start(), calls=%async_computation.9 | async-start | bytes 1310720 | tf_op jit(solution)/shard_map/reduce_scatter | solution.py:468
  375.4 27.7 %collective-permute-start.41 = (bf16[128,2048]{1,0:T(8,128)(2,1)}, bf16[128,2048]{1,0:T(8,128)(2,1)}, u32[]{:S(2)}, u32[]{:S(2)}) collective-permute-start(bf16[128,2048]{1,0:T(8,128)(2,1)} %after.29), channel_id=1, source_target_pairs={{0,1},{1,0},{2,3},{3,2},{4,5},{5,4},{6,7},{7,6},{8,9},{9,8},{10,11... | collective-permute-start | bytes 1572872 | tf_op jit(solution)/shard_map/ppermute | solution.py:209
  375.4 29.0 %collective-permute-start.42 = (bf16[128,2048]{1,0:T(8,128)(2,1)}, bf16[128,2048]{1,0:T(8,128)(2,1)}, u32[]{:S(2)}, u32[]{:S(2)}) collective-permute-start(bf16[128,2048]{1,0:T(8,128)(2,1)} %after.29), channel_id=1, source_target_pairs={{0,2},{1,3},{2,0},{3,1},{4,6},{5,7},{6,4},{7,5},{8,10},{9,11},{10,... | collective-permute-start | bytes 1572872 | tf_op jit(solution)/shard_map/ppermute | solution.py:205
  375.9 27.3 %collective-permute-start.44 = (bf16[128,2048]{1,0:T(8,128)(2,1)}, bf16[128,2048]{1,0:T(8,128)(2,1)}, u32[]{:S(2)}, u32[]{:S(2)}) collective-permute-start(bf16[128,2048]{1,0:T(8,128)(2,1)} %after.29), channel_id=1, source_target_pairs={{0,4},{1,5},{2,6},{3,7},{4,0},{5,1},{6,2},{7,3},{8,12},{9,13},{10,... | collective-permute-start | bytes 1572872 | tf_op jit(solution)/shard_map/ppermute | solution.py:205
  378.4 30.0 %collective-permute-start.47 = (bf16[128,2048]{1,0:T(8,128)(2,1)}, bf16[128,2048]{1,0:T(8,128)(2,1)}, u32[]{:S(2)}, u32[]{:S(2)}) collective-permute-start(bf16[128,2048]{1,0:T(8,128)(2,1)} %after.29), channel_id=1, source_target_pairs={{2,4},{3,5},{4,2},{5,3},{10,12},{11,13},{12,10},{13,11},{18,20},{1... | collective-permute-start | bytes 1572872 | tf_op jit(solution)/shard_map/ppermute | solution.py:205
  385.1 37.1 %collective-permute-start.37 = (bf16[512,2048]{1,0:T(8,128)(2,1)S(1)}, bf16[512,2048]{1,0:T(8,128)(2,1)S(1)}, u32[]{:S(2)}, u32[]{:S(2)}) collective-permute-start(bf16[512,2048]{1,0:T(8,128)(2,1)S(1)} %convolution_convert_fusion.3), channel_id=1, source_target_pairs={{0,1},{1,0},{2,3},{3,2},{4,5},{5,4},{6,7},{7,6},{8,9},{9,8},{10,11... | collective-permute-start | bytes 6291464 | tf_op jit(solution)/shard_map/ppermute | solution.py:209
  435.5 122.4 %reduce-scatter.11.cloned.1.call-start = ((), (), s32[]{:S(2)}) async-start(), calls=%async_computation.10 | async-start | bytes 3932160 | tf_op jit(solution)/shard_map/reduce_scatter | solution.py:468
  444.9 31.3 %collective-permute-start.52 = (bf16[128,2048]{1,0:T(8,128)(2,1)}, bf16[128,2048]{1,0:T(8,128)(2,1)}, u32[]{:S(2)}, u32[]{:S(2)}) collective-permute-start(bf16[128,2048]{1,0:T(8,128)(2,1)} %add_convert_fusion.3), channel_id=1, source_target_pairs={{0,4},{1,5},{2,6},{3,7},{4,0},{5,1},{6,2},{7,3},{8,12},{9,13},{10,... | collective-permute-start | bytes 1572872 | tf_op jit(solution)/shard_map/ppermute | solution.py:205
  516.8 25.1 %collective-permute-start.54 = (bf16[128,2048]{1,0:T(8,128)(2,1)}, bf16[128,2048]{1,0:T(8,128)(2,1)S(1)}, u32[]{:S(2)}, u32[]{:S(2)}) collective-permute-start(bf16[128,2048]{1,0:T(8,128)(2,1)} %copy-done.44), channel_id=1, source_target_pairs={{2,4},{3,5},{4,2},{5,3},{10,12},{11,13},{12,10},{13,11},{18,20},{1... | collective-permute-start | bytes 1572872 | tf_op jit(solution)/shard_map/ppermute | solution.py:205
  517.5 36.6 %collective-permute-start.57 = (bf16[128,2048]{1,0:T(8,128)(2,1)S(1)}, bf16[128,2048]{1,0:T(8,128)(2,1)}, u32[]{:S(2)}, u32[]{:S(2)}) collective-permute-start(bf16[128,2048]{1,0:T(8,128)(2,1)S(1)} %get-tuple-element.111), channel_id=1, source_target_pairs={{0,4},{1,5},{2,6},{3,7},{4,0},{5,1},{6,2},{7,3},{8,12},{9,13},{10,... | collective-permute-start | bytes 1572872 | tf_op jit(solution)/shard_map/ppermute | solution.py:205
  567.4 40.9 %collective-permute-start.63 = (bf16[2,64,1920]{2,1,0:T(8,128)(2,1)}, bf16[2,64,1920]{2,1,0:T(8,128)(2,1)}, u32[]{:S(2)}, u32[]{:S(2)}) collective-permute-start(bf16[2,64,1920]{2,1,0:T(8,128)(2,1)} %pad_maximum_fusion.2), channel_id=1, source_target_pairs={{0,4},{1,5},{2,6},{3,7},{4,0},{5,1},{6,2},{7,3},{8,12},{9,13},{10,... | collective-permute-start | bytes 1474568 | tf_op jit(solution)/shard_map/ppermute | solution.py:192
  568.2 40.0 %collective-permute-start.62 = (bf16[2,64,1920]{2,1,0:T(8,128)(2,1)}, bf16[2,64,1920]{2,1,0:T(8,128)(2,1)}, u32[]{:S(2)}, u32[]{:S(2)}) collective-permute-start(bf16[2,64,1920]{2,1,0:T(8,128)(2,1)} %pad_maximum_fusion.1), channel_id=1, source_target_pairs={{0,2},{1,3},{2,4},{3,5},{4,6},{5,7},{6,0},{7,1},{8,10},{9,11},{10,... | collective-permute-start | bytes 1474568 | tf_op jit(solution)/shard_map/ppermute | solution.py:192
  (129 other events, 1817.1 us)
Sparse Core Ops, SparseCore 0:
  9.7 70.7 all-gather.11
  87.7 43.5 all-gather.5
  165.3 55.9 all-gather.7
  223.0 52.6 all-gather.9
  322.1 52.8 reduce-scatter.6
  378.1 52.6 reduce-scatter.4
  435.6 26.5 reduce-scatter.8
  491.0 42.8 reduce-scatter.10

commit v5 on v4

--- a/solution.py
+++ b/solution.py
@@ -229,10 +229,10 @@
     )(value, *earlier)
 
 
-def gather_ctx(block):
+def gather_ctx(block, relay=False):
     count = chips()
     chip, core = place()
-    if count == 4:
+    if relay and count == 4:
         far, near, middle = (chip_permute(block, pairs) for pairs in (FAR, NEAR, MIDDLE))
         last = jnp.where((chip == 0) | (chip == 3), chip_permute(far, OUT), middle)
         same, chip_of = [block, near, far, last], [chip, chip ^ 1, chip ^ 2, chip ^ 3]
@@ -409,11 +409,11 @@
     )(where_am_i(), *got)
 
 
-def split_rows(rows):
+def split_rows(rows, relay):
     count = chips()
     chip, core = place()
     pairs = rows.reshape((count, 2, rows.shape[0] // (2 * count), rows.shape[1]))
-    order = [chip ^ (3 - k) for k in range(4)] if count == 4 else [(chip + k) % count for k in range(1, count + 1)]
+    order = [chip ^ (3 - k) for k in range(4)] if relay and count == 4 else [(chip + k) % count for k in range(1, count + 1)]
     turned = [lax.dynamic_index_in_dim(pairs, index, 0, keepdims=False) for index in order]
     pick = lambda which: jnp.concatenate(
         [lax.dynamic_index_in_dim(item, which, 0, keepdims=False) for item in turned], axis=0
@@ -421,9 +421,9 @@
     return pick(core), pick(1 - core)
 
 
-def chip_sums(left, right, dims, earlier=()):
-    count = chips()
-    mine, other = split_rows(left)
+def chip_sums(left, right, dims, earlier=(), relay=False):
+    count = chips()
+    mine, other = split_rows(left, relay)
     leaving = dot(other, right, dims).astype(BF16)
     arrived = swap(after(leaving, *earlier) if earlier else leaving)
     own = dot(mine, right, dims)
@@ -432,10 +432,10 @@
     return [item.astype(BF16) for item in sums[:-1]] + sums[-1:]
 
 
-def add_over_chips(sums, earlier=()):
+def add_over_chips(sums, earlier=(), relay=False):
     count = chips()
     total = sums[-1]
-    if count == 4:
+    if relay and count == 4:
         ends, middle, near = (chip_permute(*pair) for pair in ((sums[0], BACK), (sums[0], MIDDLE), (sums[2], NEAR)))
         far = chip_permute((sums[1].astype(F32) + ends.astype(F32)).astype(BF16), FAR)
         for arrived in (middle, near, far):
@@ -581,14 +581,14 @@
     mixed, log_total = attention_forward(qkv, seg_col, seg_row, ())
     (up_rows,) = unpack_to_rows(up_got, r, (N * f,), (mixed,))
     w_up = gather_dp(up_rows)
-    branch = add_over_chips(chip_sums(mixed, w_out, NN, (up_rows,)))[0] + bias_out
+    branch = add_over_chips(chip_sums(mixed, w_out, NN, (up_rows,), True), relay=True)[0] + bias_out
     inputs = x.astype(F32)
     active_own = active[:, None]
     middle = inputs + active_own * branch
 
     standard_two, factor_two = standardize(middle)
     normed_two = (standard_two * gain_two + bias_two).astype(BF16)
-    normed_two_all = gather_ctx(after(normed_two, cost=0))[0].reshape(S, D)
+    normed_two_all = gather_ctx(after(normed_two, cost=0), True)[0].reshape(S, D)
     grad_ffn = (active_row[:, None] * g_all).astype(BF16)
     hidden, grad_pre, grad_up_sum = feed_forward(normed_two_all, grad_ffn, w_up, bias_up.reshape(1, N * f), w_down)
     sums_two = chip_sums(grad_pre, w_up, NT)

time: 627 us -> 614 us (0.979)
  starting transfers between devices: 74 us -> 110 us
  waiting for transfers between devices: 280 us -> 250 us
  local copies, waits for them, and re-layouts: 66.9 us -> 57.1 us
  Pallas kernels: 57.2 us -> 49 us
    ppermute x28 -> x8, waiting for transfers between devices: 187 us -> 67.2 us  [chip_permute(): lax.ppermute(value, 'ctx', [(2 * s + core, 2 * t + core) for s, t in pair...]
    ppermute x9 -> x24, waiting for transfers between devices: 80.4 us -> 170 us  [turn(): lax.ppermute(value, 'ctx', [(2 * s + core, 2 * ((s + k) % count) + core)...]
    ppermute x9 -> x24, starting transfers between devices: 11.9 us -> 82.7 us  [turn(): lax.ppermute(value, 'ctx', [(2 * s + core, 2 * ((s + k) % count) + core)...]
    ppermute x28 -> x8, starting transfers between devices: 46.9 us -> 10.6 us  [chip_permute(): lax.ppermute(value, 'ctx', [(2 * s + core, 2 * t + core) for s, t in pair...]
    pallas_call x1, Pallas kernels: 24.8 us -> 16.3 us  [feed_forward(): pl.pallas_call(feed_kernel, grid=(units // tile,), out_shape=(jax.ShapeDt...]
    unnamed x180 -> x174, local copies, waits for them, and re-layouts: 28.3 us -> 20.7 us
  transfers between devices with their start and end apart: 73 -> 68, of which waited for: 27 -> 22; matrix products, arithmetic and copies ran while one was open for 24% -> 24% of each run, Pallas kernels for 3% -> 4%
where the time goes in v5:
time: 614 us; the launch traced here: 605 us
  waiting for transfers between devices  250 us (41%)
  starting transfers between devices  110 us (18%)
  matrix products  65.4 us (11%)
  other arithmetic  57.3 us (9%)
  local copies, waits for them, and re-layouts  57.1 us (9%)
  Pallas kernels  49 us (8%)
  between operations  16.9 us (3%)
    ppermute x24, waiting for transfers between devices, turn(): lax.ppermute(value, 'ctx', [(2 * s + core, 2 * ((s + k) % count) + core)...  170 us
    ppermute x24, starting transfers between devices, turn(): lax.ppermute(value, 'ctx', [(2 * s + core, 2 * ((s + k) % count) + core)...  82.7 us
    ppermute x8, waiting for transfers between devices, chip_permute(): lax.ppermute(value, 'ctx', [(2 * s + core, 2 * t + core) for s, t in pair...  67.2 us
    dot_general x15, matrix products, dot(): return lax.dot_general(left, right, dims, preferred_element_type=F32)  65.4 us
    unnamed x174, local copies, waits for them, and re-layouts  20.7 us
    pallas_call x1, Pallas kernels, feed_forward(): pl.pallas_call(feed_kernel, grid=(units // tile,), out_shape=(jax.ShapeDt...  16.3 us
  transfers between devices with their start and end apart: 68, of which 22 were waited for; matrix products, arithmetic and copies ran while one was open for 24% of the time, Pallas kernels for 4%

profile of v5, /device:TPU:0, one launch (start us, length us, event | category | flops | bytes accessed | tf_op | source)
XLA Modules:
  0.0 605.2 jit_solution(12224025217946072200)
XLA Ops:
  27.4 4.2 collective-permute-start.3
  33.6 12.8 %collective-permute-done.3.refs_3_ = bf16[2,80,768]{2,1,0:T(8,128)(2,1)S(1)} collective-permute-done((bf16[2,80,768]{2,1,0:T(8,128)(2,1)S(1)}, bf16[2,80,768]{2,1,0:T(8,128)(2,1)S(1)}, u32[]{:S(2)}, u32[]{:S(2)}) %collective-permute-start.3) | collective-permute-done | bytes 245792 | tf_op jit(solution)/shard_map/ppermute | solution.py:192
  46.4 30.1 %collective-permute-done.2.refs_2_ = bf16[2,80,768]{2,1,0:T(8,128)(2,1)S(1)} collective-permute-done((bf16[2,80,768]{2,1,0:T(8,128)(2,1)S(1)}, bf16[2,80,768]{2,1,0:T(8,128)(2,1)S(1)}, u32[]{:S(2)}, u32[]{:S(2)}) %collective-permute-start.2) | collective-permute-done | bytes 245792 | tf_op jit(solution)/shard_map/ppermute | solution.py:192
  107.7 4.6 fusion.5.refs_0_
  113.7 9.5 %collective-permute-done.13 = bf16[128,2048]{1,0:T(8,128)(2,1)S(1)} collective-permute-done((bf16[128,2048]{1,0:T(8,128)(2,1)S(1)}, bf16[128,2048]{1,0:T(8,128)(2,1)S(1)}, u32[]{:S(2)}, u32[]{:S(2)}) %collective-permute-start.13) | collective-permute-done | bytes 524320 | tf_op jit(solution)/shard_map/ppermute | solution.py:192
  128.1 10.2 %collective-permute-start.18 = (bf16[2,64,1024]{2,1,0:T(8,128)(2,1)}, bf16[2,64,1024]{2,1,0:T(8,128)(2,1)}, u32[]{:S(2)}, u32[]{:S(2)}) collective-permute-start(bf16[2,64,1024]{2,1,0:T(8,128)(2,1)} %pad_maximum_fusion.5), channel_id=1, source_target_pairs={{0,2},{1,3},{2,4},{3,5},{4,6},{5,7},{6,0},{7,1},{8,10},{9,11},{10,... | collective-permute-start | bytes 786440 | tf_op jit(solution)/shard_map/ppermute | solution.py:192
  148.8 6.6 %add_convert_fusion.refs_0_.refs_1_ = bf16[1024,768]{1,0:T(8,128)(2,1)S(1)} fusion(bf16[1024,2048]{1,0:T(8,128)(2,1)} %after.22, bf16[2048,768]{1,0:T(8,128)(2,1)} %all-gather.6.cloned.1.call-done, f32[768]{0:T(1024)S(1)} %pad_maximum_fusion.13), kind=kOutput, calls=%fused_computation.14 | convolution fusion | flops 3222798336 | bytes 8915968 | tf_op jit(solution)/shard_map/dot_general | solution.py:24
  155.4 5.2 attention_forward.1
  173.0 5.0 collective-permute-start.24
  179.0 10.8 %collective-permute-done.24 = bf16[128,2048]{1,0:T(8,128)(2,1)S(1)} collective-permute-done((bf16[128,2048]{1,0:T(8,128)(2,1)}, bf16[128,2048]{1,0:T(8,128)(2,1)S(1)}, u32[]{:S(2)}, u32[]{:S(2)}) %collective-permute-start.24) | collective-permute-done | bytes 524320 | tf_op jit(solution)/shard_map/ppermute | solution.py:205
  195.9 20.1 %collective-permute-done.23 = bf16[128,2048]{1,0:T(8,128)(2,1)S(1)} collective-permute-done((bf16[128,2048]{1,0:T(8,128)(2,1)}, bf16[128,2048]{1,0:T(8,128)(2,1)S(1)}, u32[]{:S(2)}, u32[]{:S(2)}) %collective-permute-start.23) | collective-permute-done | bytes 524320 | tf_op jit(solution)/shard_map/ppermute | solution.py:205
  216.0 4.2 collective-permute-done.25
  229.2 22.0 %collective-permute-done.29 = bf16[128,2048]{1,0:T(8,128)(2,1)S(1)} collective-permute-done((bf16[128,2048]{1,0:T(8,128)(2,1)}, bf16[128,2048]{1,0:T(8,128)(2,1)S(1)}, u32[]{:S(2)}, u32[]{:S(2)}) %collective-permute-start.29) | collective-permute-done | bytes 524320 | tf_op jit(solution)/shard_map/ppermute | solution.py:205
  257.4 10.1 %collective-permute-done.31 = bf16[128,2048]{1,0:T(8,128)(2,1)S(1)} collective-permute-done((bf16[128,2048]{1,0:T(8,128)(2,1)S(1)}, bf16[128,2048]{1,0:T(8,128)(2,1)S(1)}, u32[]{:S(2)}, u32[]{:S(2)}) %collective-permute-start.31) | collective-permute-done | bytes 524320 | tf_op jit(solution)/shard_map/ppermute | solution.py:205
  272.1 16.3 %feed_forward.1 = (bf16[1024,1024]{1,0:T(8,128)(2,1)}, bf16[1024,1024]{1,0:T(8,128)(2,1)}, f32[1,1024]{1,0:T(1,128)}) custom-call(bf16[1024,2048]{1,0:T(8,128)(2,1)} %bitcast.60.normed_ref.refs_0_, bf16[1024,2048]{1,0:T(8,128)(2,1)} %broadcast_multiply_fusion.grad_ref, bf16[2048,1024]{1,0:T(8,128)(2,1)} %all-gather.8.cloned.1.call-done.up_ref, ...), custom_call_target="tpu_custom_call" | custom-call | flops 8589934592 | bytes 8388608 | tf_op jit(solution)/shard_map/feed_forward/pallas_call | solution.py:162
  302.0 8.3 %convolution_convert_fusion = bf16[2048,1024]{1,0:T(8,128)(2,1)} fusion(bf16[1024,2048]{1,0:T(8,128)(2,1)} %after.31, bf16[1024,1024]{1,0:T(8,128)(2,1)S(1)} %copy-done.38), kind=kOutput, calls=%fused_computation.10 | convolution fusion | flops 4297064448 | bytes 10485760 | tf_op jit(solution)/shard_map/dot_general | solution.py:24
  316.3 9.7 %convolution_convert_fusion.1 = bf16[1024,2048]{1,0:T(8,128)(2,1)} fusion(bf16[1024,1024]{1,0:T(8,128)(2,1)} %after.27.refs_0_, bf16[1024,2048]{1,0:T(8,128)(2,1)} %broadcast_multiply_fusion.grad_ref), kind=kOutput, calls=%fused_computation.11 | convolution fusion | flops 4297064448 | bytes 10485760 | tf_op jit(solution)/shard_map/dot_general | solution.py:24
  328.1 21.6 %collective-permute-done.37 = bf16[128,2048]{1,0:T(8,128)(2,1)} collective-permute-done((bf16[128,2048]{1,0:T(8,128)(2,1)}, bf16[128,2048]{1,0:T(8,128)(2,1)}, u32[]{:S(2)}, u32[]{:S(2)}) %collective-permute-start.37) | collective-permute-done | bytes 524320 | tf_op jit(solution)/shard_map/ppermute | solution.py:192
  355.3 11.8 %collective-permute-start.40 = (bf16[128,2048]{1,0:T(8,128)(2,1)}, bf16[128,2048]{1,0:T(8,128)(2,1)S(1)}, u32[]{:S(2)}, u32[]{:S(2)}) collective-permute-start(bf16[128,2048]{1,0:T(8,128)(2,1)} %after.29), channel_id=1, source_target_pairs={{0,2},{1,3},{2,4},{3,5},{4,6},{5,7},{6,0},{7,1},{8,10},{9,11},{10,... | collective-permute-start | bytes 1572872 | tf_op jit(solution)/shard_map/ppermute | solution.py:192
  377.1 4.4 fusion.62
  381.5 21.8 %collective-permute-done.42 = bf16[128,2048]{1,0:T(8,128)(2,1)S(1)} collective-permute-done((bf16[128,2048]{1,0:T(8,128)(2,1)}, bf16[128,2048]{1,0:T(8,128)(2,1)S(1)}, u32[]{:S(2)}, u32[]{:S(2)}) %collective-permute-start.42) | collective-permute-done | bytes 524320 | tf_op jit(solution)/shard_map/ppermute | solution.py:192
  417.0 11.0 %collective-permute-start.46 = (bf16[128,2048]{1,0:T(8,128)(2,1)}, bf16[128,2048]{1,0:T(8,128)(2,1)}, u32[]{:S(2)}, u32[]{:S(2)}) collective-permute-start(bf16[128,2048]{1,0:T(8,128)(2,1)} %after.30), channel_id=1, source_target_pairs={{0,2},{1,3},{2,4},{3,5},{4,6},{5,7},{6,0},{7,1},{8,10},{9,11},{10,... | collective-permute-start | bytes 1572872 | tf_op jit(solution)/shard_map/ppermute | solution.py:192
  432.9 10.0 %attention_backward.1.refs_1_.refs_0_ = bf16[1024,768]{1,0:T(8,128)(2,1)S(1)} custom-call(bf16[1024,768]{1,0:T(8,128)(2,1)} %copy-done.6, bf16[1024,256]{1,0:T(8,128)(2,1)S(1)} %convolution_convert_fusion.8.refs_1_, f32[4,1024]{1,0:T(4,128)S(1)} %get-tuple-element.67.refs_2_, bf16[1024,256]{1,0:T(8,128)(2,1)S(1)} %copy-done.5, s32[1024,1]{1,0:T(8,128)S(1)} %copy-done.9, ...), custom_call_target="tpu_custom_call" | custom-call | flops 10485760000 | bytes 3670016 | tf_op jit(solution)/shard_map/attention_backward/pallas_call | solution.py:123
  443.0 5.3 convolution_convert_fusion.2.refs_1_
  448.3 16.5 %collective-permute-done.47.refs_0_ = bf16[128,2048]{1,0:T(8,128)(2,1)} collective-permute-done((bf16[128,2048]{1,0:T(8,128)(2,1)}, bf16[128,2048]{1,0:T(8,128)(2,1)}, u32[]{:S(2)}, u32[]{:S(2)}) %collective-permute-start.47) | collective-permute-done | bytes 524320 | tf_op jit(solution)/shard_map/ppermute | solution.py:192
  479.9 11.0 %collective-permute-start.50 = (bf16[128,2048]{1,0:T(8,128)(2,1)}, bf16[128,2048]{1,0:T(8,128)(2,1)S(1)}, u32[]{:S(2)}, u32[]{:S(2)}) collective-permute-start(bf16[128,2048]{1,0:T(8,128)(2,1)} %get-tuple-element.106), channel_id=1, source_target_pairs={{0,2},{1,3},{2,4},{3,5},{4,6},{5,7},{6,0},{7,1},{8,10},{9,11},{10,... | collective-permute-start | bytes 1572872 | tf_op jit(solution)/shard_map/ppermute | solution.py:192
  495.0 9.7 %collective-permute-done.50.refs_1_ = bf16[128,2048]{1,0:T(8,128)(2,1)S(1)} collective-permute-done((bf16[128,2048]{1,0:T(8,128)(2,1)}, bf16[128,2048]{1,0:T(8,128)(2,1)S(1)}, u32[]{:S(2)}, u32[]{:S(2)}) %collective-permute-start.50) | collective-permute-done | bytes 524320 | tf_op jit(solution)/shard_map/ppermute | solution.py:192
  505.5 7.2 %fusion.122 = (f32[2048]{0:T(1024)S(1)}, f32[2048]{0:T(1024)S(1)}) fusion(f32[1024]{0:T(1024)S(1)} %copy-done.75, f32[1024]{0:T(1024)S(1)} %copy-done.67, bf16[1,1024,2048]{2,1,0:T(8,128)(2,1)} %all-gather.12.cloned.1.call-done, bf16[1024,768]{1,0:T(8,128)(2,1)} %after.40, bf16[2048,768]{1,0:T(8,128)(2,1)} %all-gather.6.cloned.1.call-done), kind=kOutput, calls=%fused_computation.279 | convolution fusion | flops 3233804288 | bytes 8937472 | tf_op jit(solution)/shard_map/dot_general | solution.py:24
  517.8 9.3 %collective-permute-done.51 = bf16[128,2048]{1,0:T(8,128)(2,1)} collective-permute-done((bf16[128,2048]{1,0:T(8,128)(2,1)}, bf16[128,2048]{1,0:T(8,128)(2,1)}, u32[]{:S(2)}, u32[]{:S(2)}) %collective-permute-start.51) | collective-permute-done | bytes 524320 | tf_op jit(solution)/shard_map/ppermute | solution.py:192
  537.7 12.8 %collective-permute-start.59 = (bf16[2,64,1920]{2,1,0:T(8,128)(2,1)}, bf16[2,64,1920]{2,1,0:T(8,128)(2,1)S(1)}, u32[]{:S(2)}, u32[]{:S(2)}) collective-permute-start(bf16[2,64,1920]{2,1,0:T(8,128)(2,1)} %pad_maximum_fusion.3), channel_id=1, source_target_pairs={{0,6},{1,7},{2,0},{3,1},{4,2},{5,3},{6,4},{7,5},{8,14},{9,15},{10,... | collective-permute-start | bytes 1474568 | tf_op jit(solution)/shard_map/ppermute | solution.py:192
  557.6 4.9 collective-permute-done.59.refs_3_
  562.5 31.6 %collective-permute-done.58.refs_2_ = bf16[2,64,1920]{2,1,0:T(8,128)(2,1)} collective-permute-done((bf16[2,64,1920]{2,1,0:T(8,128)(2,1)}, bf16[2,64,1920]{2,1,0:T(8,128)(2,1)}, u32[]{:S(2)}, u32[]{:S(2)}) %collective-permute-start.58) | collective-permute-done | bytes 491552 | tf_op jit(solution)/shard_map/ppermute | solution.py:192
  (477 shorter events, 209.8 us)
Async XLA Ops:
  7.2 73.2 %all-gather.12.cloned.1.call-start = ((), (), s32[]{:S(2)}) async-start(), calls=%async_computation.11 | async-start | bytes 4718592 | tf_op jit(solution)/shard_map/all_gather | solution.py:547
  9.6 139.2 %all-gather.6.cloned.1.call-start = ((), (), s32[]{:S(2)}) async-start(), calls=%async_computation.4 | async-start | bytes 3932160 | tf_op jit(solution)/shard_map/all_gather | solution.py:464
  31.6 44.9 %collective-permute-start.2 = (bf16[2,80,768]{2,1,0:T(8,128)(2,1)S(1)}, bf16[2,80,768]{2,1,0:T(8,128)(2,1)S(1)}, u32[]{:S(2)}, u32[]{:S(2)}) collective-permute-start(bf16[2,80,768]{2,1,0:T(8,128)(2,1)S(1)} %pad_maximum_fusion.10), channel_id=1, source_target_pairs={{0,4},{1,5},{2,6},{3,7},{4,0},{5,1},{6,2},{7,3},{8,12},{9,13},{10,... | collective-permute-start | bytes 737288 | tf_op jit(solution)/shard_map/ppermute | solution.py:192
  31.7 44.8 %collective-permute-start.1 = (bf16[2,80,768]{2,1,0:T(8,128)(2,1)S(1)}, bf16[2,80,768]{2,1,0:T(8,128)(2,1)S(1)}, u32[]{:S(2)}, u32[]{:S(2)}) collective-permute-start(bf16[2,80,768]{2,1,0:T(8,128)(2,1)S(1)} %pad_maximum_fusion.9), channel_id=1, source_target_pairs={{0,2},{1,3},{2,4},{3,5},{4,6},{5,7},{6,0},{7,1},{8,10},{9,11},{10,... | collective-permute-start | bytes 737288 | tf_op jit(solution)/shard_map/ppermute | solution.py:192
  82.8 40.9 %collective-permute-start.10 = (bf16[128,2048]{1,0:T(8,128)(2,1)}, bf16[128,2048]{1,0:T(8,128)(2,1)S(1)}, u32[]{:S(2)}, u32[]{:S(2)}) collective-permute-start(bf16[128,2048]{1,0:T(8,128)(2,1)} %after.21), channel_id=1, source_target_pairs={{0,1},{1,0},{2,3},{3,2},{4,5},{5,4},{6,7},{7,6},{8,9},{9,8},{10,11... | collective-permute-start | bytes 1572872 | tf_op jit(solution)/shard_map/ppermute | solution.py:209
  83.0 29.3 %collective-permute-start.11 = (bf16[128,2048]{1,0:T(8,128)(2,1)}, bf16[128,2048]{1,0:T(8,128)(2,1)S(1)}, u32[]{:S(2)}, u32[]{:S(2)}) collective-permute-start(bf16[128,2048]{1,0:T(8,128)(2,1)} %after.21), channel_id=1, source_target_pairs={{0,2},{1,3},{2,4},{3,5},{4,6},{5,7},{6,0},{7,1},{8,10},{9,11},{10,... | collective-permute-start | bytes 1572872 | tf_op jit(solution)/shard_map/ppermute | solution.py:192
  87.5 184.6 %all-gather.8.cloned.1.call-start = ((), (), s32[]{:S(2)}) async-start(), calls=%async_computation.5 | async-start | bytes 5242880 | tf_op jit(solution)/shard_map/all_gather | solution.py:464
  96.6 26.6 %collective-permute-start.13 = (bf16[128,2048]{1,0:T(8,128)(2,1)S(1)}, bf16[128,2048]{1,0:T(8,128)(2,1)S(1)}, u32[]{:S(2)}, u32[]{:S(2)}) collective-permute-start(bf16[128,2048]{1,0:T(8,128)(2,1)S(1)} %copy-done.27), channel_id=1, source_target_pairs={{0,4},{1,5},{2,6},{3,7},{4,0},{5,1},{6,2},{7,3},{8,12},{9,13},{10,... | collective-permute-start | bytes 1572872 | tf_op jit(solution)/shard_map/ppermute | solution.py:192
  113.2 29.5 %collective-permute-start.12 = (bf16[128,2048]{1,0:T(8,128)(2,1)}, bf16[128,2048]{1,0:T(8,128)(2,1)S(1)}, u32[]{:S(2)}, u32[]{:S(2)}) collective-permute-start(bf16[128,2048]{1,0:T(8,128)(2,1)} %copy-done.36), channel_id=1, source_target_pairs={{0,1},{1,0},{2,3},{3,2},{4,5},{5,4},{6,7},{7,6},{8,9},{9,8},{10,11... | collective-permute-start | bytes 1572872 | tf_op jit(solution)/shard_map/ppermute | solution.py:209
  128.1 33.4 %collective-permute-start.18 = (bf16[2,64,1024]{2,1,0:T(8,128)(2,1)}, bf16[2,64,1024]{2,1,0:T(8,128)(2,1)}, u32[]{:S(2)}, u32[]{:S(2)}) collective-permute-start(bf16[2,64,1024]{2,1,0:T(8,128)(2,1)} %pad_maximum_fusion.5), channel_id=1, source_target_pairs={{0,2},{1,3},{2,4},{3,5},{4,6},{5,7},{6,0},{7,1},{8,10},{9,11},{10,... | collective-permute-start | bytes 786440 | tf_op jit(solution)/shard_map/ppermute | solution.py:192
  163.8 108.3 %all-gather.10.cloned.1.call-start = ((), (), s32[]{:S(2)}) async-start(), calls=%async_computation.6 | async-start | bytes 5242880 | tf_op jit(solution)/shard_map/all_gather | solution.py:464
  195.2 235.2 %reduce-scatter.7.cloned.1.call-start = ((), (), s32[]{:S(2)}) async-start(), calls=%async_computation.8 | async-start | bytes 5242880 | tf_op jit(solution)/shard_map/reduce_scatter | solution.py:468
  224.1 29.1 %collective-permute-start.26 = (bf16[128,2048]{1,0:T(8,128)(2,1)}, bf16[128,2048]{1,0:T(8,128)(2,1)S(1)}, u32[]{:S(2)}, u32[]{:S(2)}) collective-permute-start(bf16[128,2048]{1,0:T(8,128)(2,1)} %after.25), channel_id=1, source_target_pairs={{0,1},{1,0},{2,3},{3,2},{4,5},{5,4},{6,7},{7,6},{8,9},{9,8},{10,11... | collective-permute-start | bytes 1572872 | tf_op jit(solution)/shard_map/ppermute | solution.py:209
  224.1 28.5 %collective-permute-start.27 = (bf16[128,2048]{1,0:T(8,128)(2,1)}, bf16[128,2048]{1,0:T(8,128)(2,1)S(1)}, u32[]{:S(2)}, u32[]{:S(2)}) collective-permute-start(bf16[128,2048]{1,0:T(8,128)(2,1)} %after.25), channel_id=1, source_target_pairs={{0,2},{1,3},{2,0},{3,1},{4,6},{5,7},{6,4},{7,5},{8,10},{9,11},{10,... | collective-permute-start | bytes 1572872 | tf_op jit(solution)/shard_map/ppermute | solution.py:205
  224.1 27.2 %collective-permute-start.29 = (bf16[128,2048]{1,0:T(8,128)(2,1)}, bf16[128,2048]{1,0:T(8,128)(2,1)S(1)}, u32[]{:S(2)}, u32[]{:S(2)}) collective-permute-start(bf16[128,2048]{1,0:T(8,128)(2,1)} %after.25), channel_id=1, source_target_pairs={{0,4},{1,5},{2,6},{3,7},{4,0},{5,1},{6,2},{7,3},{8,12},{9,13},{10,... | collective-permute-start | bytes 1572872 | tf_op jit(solution)/shard_map/ppermute | solution.py:205
  225.2 32.2 %collective-permute-start.32 = (bf16[128,2048]{1,0:T(8,128)(2,1)}, bf16[128,2048]{1,0:T(8,128)(2,1)S(1)}, u32[]{:S(2)}, u32[]{:S(2)}) collective-permute-start(bf16[128,2048]{1,0:T(8,128)(2,1)} %after.25), channel_id=1, source_target_pairs={{2,4},{3,5},{4,2},{5,3},{10,12},{11,13},{12,10},{13,11},{18,20},{1... | collective-permute-start | bytes 1572872 | tf_op jit(solution)/shard_map/ppermute | solution.py:205
  310.4 120.0 %reduce-scatter.5.cloned.1.call-start = ((), (), s32[]{:S(2)}) async-start(), calls=%async_computation.7 | async-start | bytes 5242880 | tf_op jit(solution)/shard_map/reduce_scatter | solution.py:468
  312.3 37.5 %collective-permute-start.37 = (bf16[128,2048]{1,0:T(8,128)(2,1)}, bf16[128,2048]{1,0:T(8,128)(2,1)}, u32[]{:S(2)}, u32[]{:S(2)}) collective-permute-start(bf16[128,2048]{1,0:T(8,128)(2,1)} %get-tuple-element.112), channel_id=1, source_target_pairs={{0,4},{1,5},{2,6},{3,7},{4,0},{5,1},{6,2},{7,3},{8,12},{9,13},{10,... | collective-permute-start | bytes 1572872 | tf_op jit(solution)/shard_map/ppermute | solution.py:192
  314.7 35.1 %collective-permute-start.38 = (bf16[128,2048]{1,0:T(8,128)(2,1)S(1)}, bf16[128,2048]{1,0:T(8,128)(2,1)}, u32[]{:S(2)}, u32[]{:S(2)}) collective-permute-start(bf16[128,2048]{1,0:T(8,128)(2,1)S(1)} %copy-done.44), channel_id=1, source_target_pairs={{0,6},{1,7},{2,0},{3,1},{4,2},{5,3},{6,4},{7,5},{8,14},{9,15},{10,... | collective-permute-start | bytes 1572872 | tf_op jit(solution)/shard_map/ppermute | solution.py:192
  326.0 146.8 %reduce-scatter.9.cloned.1.call-start = ((), (), s32[]{:S(2)}) async-start(), calls=%async_computation.9 | async-start | bytes 1310720 | tf_op jit(solution)/shard_map/reduce_scatter | solution.py:468
  355.3 48.5 %collective-permute-start.39 = (bf16[128,2048]{1,0:T(8,128)(2,1)}, bf16[128,2048]{1,0:T(8,128)(2,1)S(1)}, u32[]{:S(2)}, u32[]{:S(2)}) collective-permute-start(bf16[128,2048]{1,0:T(8,128)(2,1)} %after.29), channel_id=1, source_target_pairs={{0,1},{1,0},{2,3},{3,2},{4,5},{5,4},{6,7},{7,6},{8,9},{9,8},{10,11... | collective-permute-start | bytes 1572872 | tf_op jit(solution)/shard_map/ppermute | solution.py:209
  367.1 36.2 %collective-permute-start.42 = (bf16[128,2048]{1,0:T(8,128)(2,1)}, bf16[128,2048]{1,0:T(8,128)(2,1)S(1)}, u32[]{:S(2)}, u32[]{:S(2)}) collective-permute-start(bf16[128,2048]{1,0:T(8,128)(2,1)} %after.29), channel_id=1, source_target_pairs={{0,4},{1,5},{2,6},{3,7},{4,0},{5,1},{6,2},{7,3},{8,12},{9,13},{10,... | collective-permute-start | bytes 1572872 | tf_op jit(solution)/shard_map/ppermute | solution.py:192
  368.5 34.8 %collective-permute-start.44 = (bf16[128,2048]{1,0:T(8,128)(2,1)}, bf16[128,2048]{1,0:T(8,128)(2,1)S(1)}, u32[]{:S(2)}, u32[]{:S(2)}) collective-permute-start(bf16[128,2048]{1,0:T(8,128)(2,1)} %after.29), channel_id=1, source_target_pairs={{0,6},{1,7},{2,0},{3,1},{4,2},{5,3},{6,4},{7,5},{8,14},{9,15},{10,... | collective-permute-start | bytes 1572872 | tf_op jit(solution)/shard_map/ppermute | solution.py:192
  376.0 38.2 %collective-permute-start.36 = (bf16[512,2048]{1,0:T(8,128)(2,1)}, bf16[512,2048]{1,0:T(8,128)(2,1)}, u32[]{:S(2)}, u32[]{:S(2)}) collective-permute-start(bf16[512,2048]{1,0:T(8,128)(2,1)} %convolution_convert_fusion.3), channel_id=1, source_target_pairs={{0,1},{1,0},{2,3},{3,2},{4,5},{5,4},{6,7},{7,6},{8,9},{9,8},{10,11... | collective-permute-start | bytes 6291464 | tf_op jit(solution)/shard_map/ppermute | solution.py:209
  410.3 120.7 %reduce-scatter.11.cloned.1.call-start = ((), (), s32[]{:S(2)}) async-start(), calls=%async_computation.10 | async-start | bytes 3932160 | tf_op jit(solution)/shard_map/reduce_scatter | solution.py:468
  417.0 31.3 %collective-permute-start.46 = (bf16[128,2048]{1,0:T(8,128)(2,1)}, bf16[128,2048]{1,0:T(8,128)(2,1)}, u32[]{:S(2)}, u32[]{:S(2)}) collective-permute-start(bf16[128,2048]{1,0:T(8,128)(2,1)} %after.30), channel_id=1, source_target_pairs={{0,2},{1,3},{2,4},{3,5},{4,6},{5,7},{6,0},{7,1},{8,10},{9,11},{10,... | collective-permute-start | bytes 1572872 | tf_op jit(solution)/shard_map/ppermute | solution.py:192
  428.0 36.8 %collective-permute-start.47 = (bf16[128,2048]{1,0:T(8,128)(2,1)}, bf16[128,2048]{1,0:T(8,128)(2,1)}, u32[]{:S(2)}, u32[]{:S(2)}) collective-permute-start(bf16[128,2048]{1,0:T(8,128)(2,1)} %after.33), channel_id=1, source_target_pairs={{0,4},{1,5},{2,6},{3,7},{4,0},{5,1},{6,2},{7,3},{8,12},{9,13},{10,... | collective-permute-start | bytes 1572872 | tf_op jit(solution)/shard_map/ppermute | solution.py:192
  430.2 35.5 %collective-permute-start.48 = (bf16[128,2048]{1,0:T(8,128)(2,1)}, bf16[128,2048]{1,0:T(8,128)(2,1)}, u32[]{:S(2)}, u32[]{:S(2)}) collective-permute-start(bf16[128,2048]{1,0:T(8,128)(2,1)} %after.35), channel_id=1, source_target_pairs={{0,6},{1,7},{2,0},{3,1},{4,2},{5,3},{6,4},{7,5},{8,14},{9,15},{10,... | collective-permute-start | bytes 1572872 | tf_op jit(solution)/shard_map/ppermute | solution.py:192
  491.5 35.6 %collective-permute-start.51 = (bf16[128,2048]{1,0:T(8,128)(2,1)}, bf16[128,2048]{1,0:T(8,128)(2,1)}, u32[]{:S(2)}, u32[]{:S(2)}) collective-permute-start(bf16[128,2048]{1,0:T(8,128)(2,1)} %get-tuple-element.108), channel_id=1, source_target_pairs={{0,4},{1,5},{2,6},{3,7},{4,0},{5,1},{6,2},{7,3},{8,12},{9,13},{10,... | collective-permute-start | bytes 1572872 | tf_op jit(solution)/shard_map/ppermute | solution.py:192
  492.7 34.3 %collective-permute-start.52 = (bf16[128,2048]{1,0:T(8,128)(2,1)S(1)}, bf16[128,2048]{1,0:T(8,128)(2,1)}, u32[]{:S(2)}, u32[]{:S(2)}) collective-permute-start(bf16[128,2048]{1,0:T(8,128)(2,1)S(1)} %get-tuple-element.107), channel_id=1, source_target_pairs={{0,6},{1,7},{2,0},{3,1},{4,2},{5,3},{6,4},{7,5},{8,14},{9,15},{10,... | collective-permute-start | bytes 1572872 | tf_op jit(solution)/shard_map/ppermute | solution.py:192
  551.3 42.7 %collective-permute-start.58 = (bf16[2,64,1920]{2,1,0:T(8,128)(2,1)}, bf16[2,64,1920]{2,1,0:T(8,128)(2,1)}, u32[]{:S(2)}, u32[]{:S(2)}) collective-permute-start(bf16[2,64,1920]{2,1,0:T(8,128)(2,1)} %pad_maximum_fusion.2), channel_id=1, source_target_pairs={{0,4},{1,5},{2,6},{3,7},{4,0},{5,1},{6,2},{7,3},{8,12},{9,13},{10,... | collective-permute-start | bytes 1474568 | tf_op jit(solution)/shard_map/ppermute | solution.py:192
  552.6 41.5 %collective-permute-start.57 = (bf16[2,64,1920]{2,1,0:T(8,128)(2,1)}, bf16[2,64,1920]{2,1,0:T(8,128)(2,1)}, u32[]{:S(2)}, u32[]{:S(2)}) collective-permute-start(bf16[2,64,1920]{2,1,0:T(8,128)(2,1)} %pad_maximum_fusion.1), channel_id=1, source_target_pairs={{0,2},{1,3},{2,4},{3,5},{4,6},{5,7},{6,0},{7,1},{8,10},{9,11},{10,... | collective-permute-start | bytes 1474568 | tf_op jit(solution)/shard_map/ppermute | solution.py:192
  (121 other events, 1916.7 us)
Sparse Core Ops, SparseCore 0:
  9.7 70.6 all-gather.11
  87.6 45.4 all-gather.5
  164.0 53.5 all-gather.7
  219.3 52.6 all-gather.9
  310.5 52.2 reduce-scatter.6
  365.9 52.6 reduce-scatter.4
  421.5 27.6 reduce-scatter.8
  452.5 43.9 reduce-scatter.10

commit v6 on v5

--- a/solution.py
+++ b/solution.py
@@ -598,7 +598,7 @@
     grad_down = scatter_dp(grad_down_part)
     grad_up_part = dot(after(normed_two_all, sums_two[0]), grad_pre, TN).astype(BF16)
     grad_up_mine = scatter_dp(grad_up_part)
-    feed_sums = chip_sums(after(hidden, begun_two), w_down, NN)
+    feed_sums = chip_sums(after(hidden, begun_two), w_down, NN, relay=True)
     grad_res = g_out.astype(F32)
     grad_middle = grad_res + norm_back(grad_normed_two, gain_two, standard_two, factor_two)
     grad_branch = after((active_own * grad_middle).astype(BF16), cost=250)
@@ -617,7 +617,7 @@
     )
 
     grad_qkv_part = dot(normed_one, grad_qkv, TN).astype(BF16)
-    feed, _ = add_over_chips([after(item, grad_branch_all) for item in feed_sums[:-1]] + feed_sums[-1:], (grad_qkv,))
+    feed, _ = add_over_chips([after(item, grad_branch_all) for item in feed_sums[:-1]] + feed_sums[-1:], (grad_qkv,), True)
     sums_one = chip_sums(grad_qkv, w_qkv, NT, (grad_qkv_part, feed, grad_out_w))
     grad_normed_one, begun_one = add_over_chips(sums_one)
     grad_normed_one = after(grad_normed_one, cost=0)

time: 614 us -> 609 us (level)
  starting transfers between devices: 110 us -> 101 us
    ppermute x24 -> x21, starting transfers between devices: 82.7 us -> 57.4 us  [turn(): lax.ppermute(value, 'ctx', [(2 * s + core, 2 * ((s + k) % count) + core)...]
    ppermute x8 -> x12, starting transfers between devices: 10.6 us -> 27.2 us  [chip_permute(): lax.ppermute(value, 'ctx', [(2 * s + core, 2 * t + core) for s, t in pair...]
    ppermute x8 -> x12, waiting for transfers between devices: 67.2 us -> 79.4 us  [chip_permute(): lax.ppermute(value, 'ctx', [(2 * s + core, 2 * t + core) for s, t in pair...]
    ppermute x24 -> x21, waiting for transfers between devices: 170 us -> 159 us  [turn(): lax.ppermute(value, 'ctx', [(2 * s + core, 2 * ((s + k) % count) + core)...]
    unnamed x174 -> x176, local copies, waits for them, and re-layouts: 20.7 us -> 23.3 us
  transfers between devices with their start and end apart: 68 -> 69, of which waited for: 22 -> 24; matrix products, arithmetic and copies ran while one was open for 24% -> 24% of each run, Pallas kernels for 4% -> 4%
where the time goes in v6:
time: 609 us; the launch traced here: 600 us
  waiting for transfers between devices  251 us (41%)
  starting transfers between devices  101 us (17%)
  matrix products  64.1 us (11%)
  local copies, waits for them, and re-layouts  59.7 us (10%)
  other arithmetic  57.9 us (10%)
  Pallas kernels  48.9 us (8%)
  between operations  16.9 us (3%)
    ppermute x21, waiting for transfers between devices, turn(): lax.ppermute(value, 'ctx', [(2 * s + core, 2 * ((s + k) % count) + core)...  159 us
    ppermute x12, waiting for transfers between devices, chip_permute(): lax.ppermute(value, 'ctx', [(2 * s + core, 2 * t + core) for s, t in pair...  79.4 us
    dot_general x15, matrix products, dot(): return lax.dot_general(left, right, dims, preferred_element_type=F32)  64.1 us
    ppermute x21, starting transfers between devices, turn(): lax.ppermute(value, 'ctx', [(2 * s + core, 2 * ((s + k) % count) + core)...  57.4 us
    ppermute x12, starting transfers between devices, chip_permute(): lax.ppermute(value, 'ctx', [(2 * s + core, 2 * t + core) for s, t in pair...  27.2 us
    unnamed x176, local copies, waits for them, and re-layouts  23.3 us
    pallas_call x1, Pallas kernels, feed_forward(): pl.pallas_call(feed_kernel, grid=(units // tile,), out_shape=(jax.ShapeDt...  16.3 us
  transfers between devices with their start and end apart: 69, of which 24 were waited for; matrix products, arithmetic and copies ran while one was open for 24% of the time, Pallas kernels for 4%

profile of v6, /device:TPU:0, one launch (start us, length us, event | category | flops | bytes accessed | tf_op | source)
XLA Modules:
  0.0 599.8 jit_solution(2872030563948166927)
XLA Ops:
  27.3 4.2 collective-permute-start.3
  33.5 12.8 %collective-permute-done.3.refs_3_ = bf16[2,80,768]{2,1,0:T(8,128)(2,1)S(1)} collective-permute-done((bf16[2,80,768]{2,1,0:T(8,128)(2,1)S(1)}, bf16[2,80,768]{2,1,0:T(8,128)(2,1)S(1)}, u32[]{:S(2)}, u32[]{:S(2)}) %collective-permute-start.3) | collective-permute-done | bytes 245792 | tf_op jit(solution)/shard_map/ppermute | solution.py:192
  46.3 30.2 %collective-permute-done.2.refs_2_ = bf16[2,80,768]{2,1,0:T(8,128)(2,1)S(1)} collective-permute-done((bf16[2,80,768]{2,1,0:T(8,128)(2,1)S(1)}, bf16[2,80,768]{2,1,0:T(8,128)(2,1)S(1)}, u32[]{:S(2)}, u32[]{:S(2)}) %collective-permute-start.2) | collective-permute-done | bytes 245792 | tf_op jit(solution)/shard_map/ppermute | solution.py:192
  76.5 4.0 all-gather.12.cloned.1.call-done
  107.8 4.7 fusion.5.refs_0_
  113.8 9.5 %collective-permute-done.13 = bf16[128,2048]{1,0:T(8,128)(2,1)S(1)} collective-permute-done((bf16[128,2048]{1,0:T(8,128)(2,1)S(1)}, bf16[128,2048]{1,0:T(8,128)(2,1)S(1)}, u32[]{:S(2)}, u32[]{:S(2)}) %collective-permute-start.13) | collective-permute-done | bytes 524320 | tf_op jit(solution)/shard_map/ppermute | solution.py:192
  128.2 10.2 %collective-permute-start.18 = (bf16[2,64,1024]{2,1,0:T(8,128)(2,1)}, bf16[2,64,1024]{2,1,0:T(8,128)(2,1)}, u32[]{:S(2)}, u32[]{:S(2)}) collective-permute-start(bf16[2,64,1024]{2,1,0:T(8,128)(2,1)} %pad_maximum_fusion.5), channel_id=1, source_target_pairs={{0,2},{1,3},{2,4},{3,5},{4,6},{5,7},{6,0},{7,1},{8,10},{9,11},{10,... | collective-permute-start | bytes 786440 | tf_op jit(solution)/shard_map/ppermute | solution.py:192
  148.9 6.6 %add_convert_fusion.refs_0_.refs_1_ = bf16[1024,768]{1,0:T(8,128)(2,1)S(1)} fusion(bf16[1024,2048]{1,0:T(8,128)(2,1)} %after.22, bf16[2048,768]{1,0:T(8,128)(2,1)} %all-gather.6.cloned.1.call-done, f32[768]{0:T(1024)S(1)} %pad_maximum_fusion.13), kind=kOutput, calls=%fused_computation.14 | convolution fusion | flops 3222798336 | bytes 8915968 | tf_op jit(solution)/shard_map/dot_general | solution.py:24
  155.5 5.2 attention_forward.1
  173.1 5.1 collective-permute-start.24
  179.1 10.8 %collective-permute-done.24 = bf16[128,2048]{1,0:T(8,128)(2,1)S(1)} collective-permute-done((bf16[128,2048]{1,0:T(8,128)(2,1)}, bf16[128,2048]{1,0:T(8,128)(2,1)S(1)}, u32[]{:S(2)}, u32[]{:S(2)}) %collective-permute-start.24) | collective-permute-done | bytes 524320 | tf_op jit(solution)/shard_map/ppermute | solution.py:205
  196.0 20.1 %collective-permute-done.23 = bf16[128,2048]{1,0:T(8,128)(2,1)S(1)} collective-permute-done((bf16[128,2048]{1,0:T(8,128)(2,1)}, bf16[128,2048]{1,0:T(8,128)(2,1)S(1)}, u32[]{:S(2)}, u32[]{:S(2)}) %collective-permute-start.23) | collective-permute-done | bytes 524320 | tf_op jit(solution)/shard_map/ppermute | solution.py:205
  216.1 4.2 collective-permute-done.25
  229.3 22.1 %collective-permute-done.29 = bf16[128,2048]{1,0:T(8,128)(2,1)S(1)} collective-permute-done((bf16[128,2048]{1,0:T(8,128)(2,1)}, bf16[128,2048]{1,0:T(8,128)(2,1)S(1)}, u32[]{:S(2)}, u32[]{:S(2)}) %collective-permute-start.29) | collective-permute-done | bytes 524320 | tf_op jit(solution)/shard_map/ppermute | solution.py:205
  257.5 10.1 %collective-permute-done.31 = bf16[128,2048]{1,0:T(8,128)(2,1)S(1)} collective-permute-done((bf16[128,2048]{1,0:T(8,128)(2,1)S(1)}, bf16[128,2048]{1,0:T(8,128)(2,1)S(1)}, u32[]{:S(2)}, u32[]{:S(2)}) %collective-permute-start.31) | collective-permute-done | bytes 524320 | tf_op jit(solution)/shard_map/ppermute | solution.py:205
  272.2 16.3 %feed_forward.1 = (bf16[1024,1024]{1,0:T(8,128)(2,1)}, bf16[1024,1024]{1,0:T(8,128)(2,1)}, f32[1,1024]{1,0:T(1,128)}) custom-call(bf16[1024,2048]{1,0:T(8,128)(2,1)} %bitcast.60.normed_ref.refs_0_, bf16[1024,2048]{1,0:T(8,128)(2,1)} %broadcast_multiply_fusion.grad_ref, bf16[2048,1024]{1,0:T(8,128)(2,1)} %all-gather.8.cloned.1.call-done.up_ref, ...), custom_call_target="tpu_custom_call" | custom-call | flops 8589934592 | bytes 8388608 | tf_op jit(solution)/shard_map/feed_forward/pallas_call | solution.py:162
  302.2 8.3 %convolution_convert_fusion = bf16[2048,1024]{1,0:T(8,128)(2,1)} fusion(bf16[1024,2048]{1,0:T(8,128)(2,1)} %after.31, bf16[1024,1024]{1,0:T(8,128)(2,1)S(1)} %copy-done.39), kind=kOutput, calls=%fused_computation.10 | convolution fusion | flops 4297064448 | bytes 10485760 | tf_op jit(solution)/shard_map/dot_general | solution.py:24
  316.3 9.7 %convolution_convert_fusion.1 = bf16[1024,2048]{1,0:T(8,128)(2,1)} fusion(bf16[1024,1024]{1,0:T(8,128)(2,1)} %after.27.refs_0_, bf16[1024,2048]{1,0:T(8,128)(2,1)} %broadcast_multiply_fusion.grad_ref), kind=kOutput, calls=%fused_computation.11 | convolution fusion | flops 4297064448 | bytes 10485760 | tf_op jit(solution)/shard_map/dot_general | solution.py:24
  328.3 21.6 %collective-permute-done.37 = bf16[128,2048]{1,0:T(8,128)(2,1)} collective-permute-done((bf16[128,2048]{1,0:T(8,128)(2,1)}, bf16[128,2048]{1,0:T(8,128)(2,1)}, u32[]{:S(2)}, u32[]{:S(2)}) %collective-permute-start.37) | collective-permute-done | bytes 524320 | tf_op jit(solution)/shard_map/ppermute | solution.py:192
  355.4 11.8 %collective-permute-start.40 = (bf16[128,2048]{1,0:T(8,128)(2,1)}, bf16[128,2048]{1,0:T(8,128)(2,1)S(1)}, u32[]{:S(2)}, u32[]{:S(2)}) collective-permute-start(bf16[128,2048]{1,0:T(8,128)(2,1)} %after.29), channel_id=1, source_target_pairs={{0,2},{1,3},{2,4},{3,5},{4,6},{5,7},{6,0},{7,1},{8,10},{9,11},{10,... | collective-permute-start | bytes 1572872 | tf_op jit(solution)/shard_map/ppermute | solution.py:192
  381.0 22.3 %collective-permute-done.42 = bf16[128,2048]{1,0:T(8,128)(2,1)S(1)} collective-permute-done((bf16[128,2048]{1,0:T(8,128)(2,1)}, bf16[128,2048]{1,0:T(8,128)(2,1)S(1)}, u32[]{:S(2)}, u32[]{:S(2)}) %collective-permute-start.42) | collective-permute-done | bytes 524320 | tf_op jit(solution)/shard_map/ppermute | solution.py:192
  409.8 13.2 %collective-permute-start.48 = (bf16[128,2048]{1,0:T(8,128)(2,1)}, bf16[128,2048]{1,0:T(8,128)(2,1)S(1)}, u32[]{:S(2)}, u32[]{:S(2)}) collective-permute-start(bf16[128,2048]{1,0:T(8,128)(2,1)} %after.30), channel_id=1, source_target_pairs={{6,4},{7,5},{0,2},{1,3},{14,12},{15,13},{8,10},{9,11},{22,20},{23,... | collective-permute-start | bytes 1572872 | tf_op jit(solution)/shard_map/ppermute | solution.py:205
  423.1 4.5 convolution_convert_fusion.7
  441.7 9.9 %attention_backward.1.refs_1_.refs_0_ = bf16[1024,768]{1,0:T(8,128)(2,1)S(1)} custom-call(bf16[1024,768]{1,0:T(8,128)(2,1)} %copy-done.6, bf16[1024,256]{1,0:T(8,128)(2,1)S(1)} %convolution_convert_fusion.8.refs_1_, f32[4,1024]{1,0:T(4,128)S(1)} %get-tuple-element.67.refs_2_, bf16[1024,256]{1,0:T(8,128)(2,1)S(1)} %copy-done.5, s32[1024,1]{1,0:T(8,128)S(1)} %copy-done.9, ...), custom_call_target="tpu_custom_call" | custom-call | flops 10485760000 | bytes 3670016 | tf_op jit(solution)/shard_map/attention_backward/pallas_call | solution.py:123
  451.7 5.3 convolution_convert_fusion.2.refs_1_
  459.3 9.3 %collective-permute-done.49.refs_0_ = bf16[128,2048]{1,0:T(8,128)(2,1)} collective-permute-done((bf16[128,2048]{1,0:T(8,128)(2,1)}, bf16[128,2048]{1,0:T(8,128)(2,1)}, u32[]{:S(2)}, u32[]{:S(2)}) %collective-permute-start.49) | collective-permute-done | bytes 524320 | tf_op jit(solution)/shard_map/ppermute | solution.py:205
  487.1 12.4 %collective-permute-done.51.refs_1_ = bf16[128,2048]{1,0:T(8,128)(2,1)S(1)} collective-permute-done((bf16[128,2048]{1,0:T(8,128)(2,1)}, bf16[128,2048]{1,0:T(8,128)(2,1)S(1)}, u32[]{:S(2)}, u32[]{:S(2)}) %collective-permute-start.51) | collective-permute-done | bytes 524320 | tf_op jit(solution)/shard_map/ppermute | solution.py:192
  500.3 7.3 %fusion.122 = (f32[2048]{0:T(1024)S(1)}, f32[2048]{0:T(1024)S(1)}) fusion(f32[1024]{0:T(1024)S(1)} %copy-done.76, f32[1024]{0:T(1024)S(1)} %copy-done.68, bf16[1,1024,2048]{2,1,0:T(8,128)(2,1)} %all-gather.12.cloned.1.call-done, bf16[1024,768]{1,0:T(8,128)(2,1)} %after.40, bf16[2048,768]{1,0:T(8,128)(2,1)} %all-gather.6.cloned.1.call-done), kind=kOutput, calls=%fused_computation.280 | convolution fusion | flops 3233804288 | bytes 8937472 | tf_op jit(solution)/shard_map/dot_general | solution.py:24
  512.6 9.0 %collective-permute-done.52 = bf16[128,2048]{1,0:T(8,128)(2,1)} collective-permute-done((bf16[128,2048]{1,0:T(8,128)(2,1)}, bf16[128,2048]{1,0:T(8,128)(2,1)}, u32[]{:S(2)}, u32[]{:S(2)}) %collective-permute-start.52) | collective-permute-done | bytes 524320 | tf_op jit(solution)/shard_map/ppermute | solution.py:192
  532.2 9.7 %collective-permute-start.60 = (bf16[2,64,1920]{2,1,0:T(8,128)(2,1)}, bf16[2,64,1920]{2,1,0:T(8,128)(2,1)S(1)}, u32[]{:S(2)}, u32[]{:S(2)}) collective-permute-start(bf16[2,64,1920]{2,1,0:T(8,128)(2,1)} %pad_maximum_fusion.3), channel_id=1, source_target_pairs={{0,6},{1,7},{2,0},{3,1},{4,2},{5,3},{6,4},{7,5},{8,14},{9,15},{10,... | collective-permute-start | bytes 1474568 | tf_op jit(solution)/shard_map/ppermute | solution.py:192
  555.7 32.9 %collective-permute-done.59.refs_2_ = bf16[2,64,1920]{2,1,0:T(8,128)(2,1)} collective-permute-done((bf16[2,64,1920]{2,1,0:T(8,128)(2,1)}, bf16[2,64,1920]{2,1,0:T(8,128)(2,1)}, u32[]{:S(2)}, u32[]{:S(2)}) %collective-permute-start.59) | collective-permute-done | bytes 491552 | tf_op jit(solution)/shard_map/ppermute | solution.py:192
  588.6 3.9 unpack_to_columns.1
  (482 shorter events, 216.0 us)
Async XLA Ops:
  7.2 73.3 %all-gather.12.cloned.1.call-start = ((), (), s32[]{:S(2)}) async-start(), calls=%async_computation.11 | async-start | bytes 4718592 | tf_op jit(solution)/shard_map/all_gather | solution.py:547
  9.6 139.3 %all-gather.6.cloned.1.call-start = ((), (), s32[]{:S(2)}) async-start(), calls=%async_computation.4 | async-start | bytes 3932160 | tf_op jit(solution)/shard_map/all_gather | solution.py:464
  31.5 44.9 %collective-permute-start.2 = (bf16[2,80,768]{2,1,0:T(8,128)(2,1)S(1)}, bf16[2,80,768]{2,1,0:T(8,128)(2,1)S(1)}, u32[]{:S(2)}, u32[]{:S(2)}) collective-permute-start(bf16[2,80,768]{2,1,0:T(8,128)(2,1)S(1)} %pad_maximum_fusion.10), channel_id=1, source_target_pairs={{0,4},{1,5},{2,6},{3,7},{4,0},{5,1},{6,2},{7,3},{8,12},{9,13},{10,... | collective-permute-start | bytes 737288 | tf_op jit(solution)/shard_map/ppermute | solution.py:192
  31.6 44.8 %collective-permute-start.1 = (bf16[2,80,768]{2,1,0:T(8,128)(2,1)S(1)}, bf16[2,80,768]{2,1,0:T(8,128)(2,1)S(1)}, u32[]{:S(2)}, u32[]{:S(2)}) collective-permute-start(bf16[2,80,768]{2,1,0:T(8,128)(2,1)S(1)} %pad_maximum_fusion.9), channel_id=1, source_target_pairs={{0,2},{1,3},{2,4},{3,5},{4,6},{5,7},{6,0},{7,1},{8,10},{9,11},{10,... | collective-permute-start | bytes 737288 | tf_op jit(solution)/shard_map/ppermute | solution.py:192
  82.8 41.0 %collective-permute-start.10 = (bf16[128,2048]{1,0:T(8,128)(2,1)}, bf16[128,2048]{1,0:T(8,128)(2,1)S(1)}, u32[]{:S(2)}, u32[]{:S(2)}) collective-permute-start(bf16[128,2048]{1,0:T(8,128)(2,1)} %after.21), channel_id=1, source_target_pairs={{0,1},{1,0},{2,3},{3,2},{4,5},{5,4},{6,7},{7,6},{8,9},{9,8},{10,11... | collective-permute-start | bytes 1572872 | tf_op jit(solution)/shard_map/ppermute | solution.py:209
  83.1 29.4 %collective-permute-start.11 = (bf16[128,2048]{1,0:T(8,128)(2,1)}, bf16[128,2048]{1,0:T(8,128)(2,1)S(1)}, u32[]{:S(2)}, u32[]{:S(2)}) collective-permute-start(bf16[128,2048]{1,0:T(8,128)(2,1)} %after.21), channel_id=1, source_target_pairs={{0,2},{1,3},{2,4},{3,5},{4,6},{5,7},{6,0},{7,1},{8,10},{9,11},{10,... | collective-permute-start | bytes 1572872 | tf_op jit(solution)/shard_map/ppermute | solution.py:192
  87.6 184.7 %all-gather.8.cloned.1.call-start = ((), (), s32[]{:S(2)}) async-start(), calls=%async_computation.5 | async-start | bytes 5242880 | tf_op jit(solution)/shard_map/all_gather | solution.py:464
  96.7 26.6 %collective-permute-start.13 = (bf16[128,2048]{1,0:T(8,128)(2,1)S(1)}, bf16[128,2048]{1,0:T(8,128)(2,1)S(1)}, u32[]{:S(2)}, u32[]{:S(2)}) collective-permute-start(bf16[128,2048]{1,0:T(8,128)(2,1)S(1)} %copy-done.27), channel_id=1, source_target_pairs={{0,4},{1,5},{2,6},{3,7},{4,0},{5,1},{6,2},{7,3},{8,12},{9,13},{10,... | collective-permute-start | bytes 1572872 | tf_op jit(solution)/shard_map/ppermute | solution.py:192
  113.3 29.5 %collective-permute-start.12 = (bf16[128,2048]{1,0:T(8,128)(2,1)}, bf16[128,2048]{1,0:T(8,128)(2,1)S(1)}, u32[]{:S(2)}, u32[]{:S(2)}) collective-permute-start(bf16[128,2048]{1,0:T(8,128)(2,1)} %copy-done.36), channel_id=1, source_target_pairs={{0,1},{1,0},{2,3},{3,2},{4,5},{5,4},{6,7},{7,6},{8,9},{9,8},{10,11... | collective-permute-start | bytes 1572872 | tf_op jit(solution)/shard_map/ppermute | solution.py:209
  128.2 33.3 %collective-permute-start.18 = (bf16[2,64,1024]{2,1,0:T(8,128)(2,1)}, bf16[2,64,1024]{2,1,0:T(8,128)(2,1)}, u32[]{:S(2)}, u32[]{:S(2)}) collective-permute-start(bf16[2,64,1024]{2,1,0:T(8,128)(2,1)} %pad_maximum_fusion.5), channel_id=1, source_target_pairs={{0,2},{1,3},{2,4},{3,5},{4,6},{5,7},{6,0},{7,1},{8,10},{9,11},{10,... | collective-permute-start | bytes 786440 | tf_op jit(solution)/shard_map/ppermute | solution.py:192
  163.9 108.3 %all-gather.10.cloned.1.call-start = ((), (), s32[]{:S(2)}) async-start(), calls=%async_computation.6 | async-start | bytes 5242880 | tf_op jit(solution)/shard_map/all_gather | solution.py:464
  195.3 244.0 %reduce-scatter.7.cloned.1.call-start = ((), (), s32[]{:S(2)}) async-start(), calls=%async_computation.8 | async-start | bytes 5242880 | tf_op jit(solution)/shard_map/reduce_scatter | solution.py:468
  224.2 29.1 %collective-permute-start.26 = (bf16[128,2048]{1,0:T(8,128)(2,1)}, bf16[128,2048]{1,0:T(8,128)(2,1)S(1)}, u32[]{:S(2)}, u32[]{:S(2)}) collective-permute-start(bf16[128,2048]{1,0:T(8,128)(2,1)} %after.25), channel_id=1, source_target_pairs={{0,1},{1,0},{2,3},{3,2},{4,5},{5,4},{6,7},{7,6},{8,9},{9,8},{10,11... | collective-permute-start | bytes 1572872 | tf_op jit(solution)/shard_map/ppermute | solution.py:209
  224.2 28.5 %collective-permute-start.27 = (bf16[128,2048]{1,0:T(8,128)(2,1)}, bf16[128,2048]{1,0:T(8,128)(2,1)S(1)}, u32[]{:S(2)}, u32[]{:S(2)}) collective-permute-start(bf16[128,2048]{1,0:T(8,128)(2,1)} %after.25), channel_id=1, source_target_pairs={{0,2},{1,3},{2,0},{3,1},{4,6},{5,7},{6,4},{7,5},{8,10},{9,11},{10,... | collective-permute-start | bytes 1572872 | tf_op jit(solution)/shard_map/ppermute | solution.py:205
  224.2 27.2 %collective-permute-start.29 = (bf16[128,2048]{1,0:T(8,128)(2,1)}, bf16[128,2048]{1,0:T(8,128)(2,1)S(1)}, u32[]{:S(2)}, u32[]{:S(2)}) collective-permute-start(bf16[128,2048]{1,0:T(8,128)(2,1)} %after.25), channel_id=1, source_target_pairs={{0,4},{1,5},{2,6},{3,7},{4,0},{5,1},{6,2},{7,3},{8,12},{9,13},{10,... | collective-permute-start | bytes 1572872 | tf_op jit(solution)/shard_map/ppermute | solution.py:205
  225.3 32.2 %collective-permute-start.32 = (bf16[128,2048]{1,0:T(8,128)(2,1)}, bf16[128,2048]{1,0:T(8,128)(2,1)S(1)}, u32[]{:S(2)}, u32[]{:S(2)}) collective-permute-start(bf16[128,2048]{1,0:T(8,128)(2,1)} %after.25), channel_id=1, source_target_pairs={{2,4},{3,5},{4,2},{5,3},{10,12},{11,13},{12,10},{13,11},{18,20},{1... | collective-permute-start | bytes 1572872 | tf_op jit(solution)/shard_map/ppermute | solution.py:205
  310.5 128.8 %reduce-scatter.5.cloned.1.call-start = ((), (), s32[]{:S(2)}) async-start(), calls=%async_computation.7 | async-start | bytes 5242880 | tf_op jit(solution)/shard_map/reduce_scatter | solution.py:468
  312.3 37.6 %collective-permute-start.37 = (bf16[128,2048]{1,0:T(8,128)(2,1)}, bf16[128,2048]{1,0:T(8,128)(2,1)}, u32[]{:S(2)}, u32[]{:S(2)}) collective-permute-start(bf16[128,2048]{1,0:T(8,128)(2,1)} %get-tuple-element.112), channel_id=1, source_target_pairs={{0,4},{1,5},{2,6},{3,7},{4,0},{5,1},{6,2},{7,3},{8,12},{9,13},{10,... | collective-permute-start | bytes 1572872 | tf_op jit(solution)/shard_map/ppermute | solution.py:192
  314.7 35.2 %collective-permute-start.38 = (bf16[128,2048]{1,0:T(8,128)(2,1)S(1)}, bf16[128,2048]{1,0:T(8,128)(2,1)}, u32[]{:S(2)}, u32[]{:S(2)}) collective-permute-start(bf16[128,2048]{1,0:T(8,128)(2,1)S(1)} %copy-done.45), channel_id=1, source_target_pairs={{0,6},{1,7},{2,0},{3,1},{4,2},{5,3},{6,4},{7,5},{8,14},{9,15},{10,... | collective-permute-start | bytes 1572872 | tf_op jit(solution)/shard_map/ppermute | solution.py:192
  326.0 149.5 %reduce-scatter.9.cloned.1.call-start = ((), (), s32[]{:S(2)}) async-start(), calls=%async_computation.9 | async-start | bytes 1310720 | tf_op jit(solution)/shard_map/reduce_scatter | solution.py:468
  355.4 48.4 %collective-permute-start.39 = (bf16[128,2048]{1,0:T(8,128)(2,1)}, bf16[128,2048]{1,0:T(8,128)(2,1)S(1)}, u32[]{:S(2)}, u32[]{:S(2)}) collective-permute-start(bf16[128,2048]{1,0:T(8,128)(2,1)} %after.29), channel_id=1, source_target_pairs={{0,1},{1,0},{2,3},{3,2},{4,5},{5,4},{6,7},{7,6},{8,9},{9,8},{10,11... | collective-permute-start | bytes 1572872 | tf_op jit(solution)/shard_map/ppermute | solution.py:209
  367.2 36.1 %collective-permute-start.42 = (bf16[128,2048]{1,0:T(8,128)(2,1)}, bf16[128,2048]{1,0:T(8,128)(2,1)S(1)}, u32[]{:S(2)}, u32[]{:S(2)}) collective-permute-start(bf16[128,2048]{1,0:T(8,128)(2,1)} %after.29), channel_id=1, source_target_pairs={{0,4},{1,5},{2,6},{3,7},{4,0},{5,1},{6,2},{7,3},{8,12},{9,13},{10,... | collective-permute-start | bytes 1572872 | tf_op jit(solution)/shard_map/ppermute | solution.py:192
  368.5 34.8 %collective-permute-start.44 = (bf16[128,2048]{1,0:T(8,128)(2,1)}, bf16[128,2048]{1,0:T(8,128)(2,1)S(1)}, u32[]{:S(2)}, u32[]{:S(2)}) collective-permute-start(bf16[128,2048]{1,0:T(8,128)(2,1)} %after.29), channel_id=1, source_target_pairs={{0,6},{1,7},{2,0},{3,1},{4,2},{5,3},{6,4},{7,5},{8,14},{9,15},{10,... | collective-permute-start | bytes 1572872 | tf_op jit(solution)/shard_map/ppermute | solution.py:192
  374.8 31.2 %collective-permute-start.36 = (bf16[512,2048]{1,0:T(8,128)(2,1)S(1)}, bf16[512,2048]{1,0:T(8,128)(2,1)S(1)}, u32[]{:S(2)}, u32[]{:S(2)}) collective-permute-start(bf16[512,2048]{1,0:T(8,128)(2,1)S(1)} %convolution_convert_fusion.3), channel_id=1, source_target_pairs={{0,1},{1,0},{2,3},{3,2},{4,5},{5,4},{6,7},{7,6},{8,9},{9,8},{10,11... | collective-permute-start | bytes 6291464 | tf_op jit(solution)/shard_map/ppermute | solution.py:209
  409.8 25.6 %collective-permute-start.48 = (bf16[128,2048]{1,0:T(8,128)(2,1)}, bf16[128,2048]{1,0:T(8,128)(2,1)S(1)}, u32[]{:S(2)}, u32[]{:S(2)}) collective-permute-start(bf16[128,2048]{1,0:T(8,128)(2,1)} %after.30), channel_id=1, source_target_pairs={{6,4},{7,5},{0,2},{1,3},{14,12},{15,13},{8,10},{9,11},{22,20},{23,... | collective-permute-start | bytes 1572872 | tf_op jit(solution)/shard_map/ppermute | solution.py:205
  427.6 97.8 %reduce-scatter.11.cloned.1.call-start = ((), (), s32[]{:S(2)}) async-start(), calls=%async_computation.10 | async-start | bytes 3932160 | tf_op jit(solution)/shard_map/reduce_scatter | solution.py:468
  431.2 25.8 %collective-permute-start.46 = (bf16[128,2048]{1,0:T(8,128)(2,1)}, bf16[128,2048]{1,0:T(8,128)(2,1)}, u32[]{:S(2)}, u32[]{:S(2)}) collective-permute-start(bf16[128,2048]{1,0:T(8,128)(2,1)} %after.30), channel_id=1, source_target_pairs={{2,4},{3,5},{4,2},{5,3},{10,12},{11,13},{12,10},{13,11},{18,20},{1... | collective-permute-start | bytes 1572872 | tf_op jit(solution)/shard_map/ppermute | solution.py:205
  437.4 31.2 %collective-permute-start.49 = (bf16[128,2048]{1,0:T(8,128)(2,1)}, bf16[128,2048]{1,0:T(8,128)(2,1)}, u32[]{:S(2)}, u32[]{:S(2)}) collective-permute-start(bf16[128,2048]{1,0:T(8,128)(2,1)} %add_convert_fusion.2), channel_id=1, source_target_pairs={{0,4},{1,5},{2,6},{3,7},{4,0},{5,1},{6,2},{7,3},{8,12},{9,13},{10,... | collective-permute-start | bytes 1572872 | tf_op jit(solution)/shard_map/ppermute | solution.py:205
  484.3 37.3 %collective-permute-start.52 = (bf16[128,2048]{1,0:T(8,128)(2,1)}, bf16[128,2048]{1,0:T(8,128)(2,1)}, u32[]{:S(2)}, u32[]{:S(2)}) collective-permute-start(bf16[128,2048]{1,0:T(8,128)(2,1)} %get-tuple-element.108), channel_id=1, source_target_pairs={{0,4},{1,5},{2,6},{3,7},{4,0},{5,1},{6,2},{7,3},{8,12},{9,13},{10,... | collective-permute-start | bytes 1572872 | tf_op jit(solution)/shard_map/ppermute | solution.py:192
  485.0 36.6 %collective-permute-start.53 = (bf16[128,2048]{1,0:T(8,128)(2,1)S(1)}, bf16[128,2048]{1,0:T(8,128)(2,1)}, u32[]{:S(2)}, u32[]{:S(2)}) collective-permute-start(bf16[128,2048]{1,0:T(8,128)(2,1)S(1)} %get-tuple-element.107), channel_id=1, source_target_pairs={{0,6},{1,7},{2,0},{3,1},{4,2},{5,3},{6,4},{7,5},{8,14},{9,15},{10,... | collective-permute-start | bytes 1572872 | tf_op jit(solution)/shard_map/ppermute | solution.py:192
  542.8 45.8 %collective-permute-start.59 = (bf16[2,64,1920]{2,1,0:T(8,128)(2,1)}, bf16[2,64,1920]{2,1,0:T(8,128)(2,1)}, u32[]{:S(2)}, u32[]{:S(2)}) collective-permute-start(bf16[2,64,1920]{2,1,0:T(8,128)(2,1)} %pad_maximum_fusion.2), channel_id=1, source_target_pairs={{0,4},{1,5},{2,6},{3,7},{4,0},{5,1},{6,2},{7,3},{8,12},{9,13},{10,... | collective-permute-start | bytes 1474568 | tf_op jit(solution)/shard_map/ppermute | solution.py:192
  547.1 41.5 %collective-permute-start.58 = (bf16[2,64,1920]{2,1,0:T(8,128)(2,1)}, bf16[2,64,1920]{2,1,0:T(8,128)(2,1)}, u32[]{:S(2)}, u32[]{:S(2)}) collective-permute-start(bf16[2,64,1920]{2,1,0:T(8,128)(2,1)} %pad_maximum_fusion.1), channel_id=1, source_target_pairs={{0,2},{1,3},{2,4},{3,5},{4,6},{5,7},{6,0},{7,1},{8,10},{9,11},{10,... | collective-permute-start | bytes 1474568 | tf_op jit(solution)/shard_map/ppermute | solution.py:192
  (123 other events, 1935.5 us)
Sparse Core Ops, SparseCore 0:
  9.7 70.7 all-gather.11
  87.7 45.3 all-gather.5
  164.0 53.5 all-gather.7
  219.3 52.6 all-gather.9
  310.6 52.1 reduce-scatter.6
  365.9 52.6 reduce-scatter.4
  427.7 25.8 reduce-scatter.8
  457.1 43.7 reduce-scatter.10
